TPU v7x, 32 devices: a whole 2x2x4 slice. The times are simulated.
32 devices in a mesh: fsdp: 4 (over y, core), tp: 8 (over z, x).
Axes of the slice: x: 2, y: 2, z: 4, core: 2. Of those that a mesh axis runs over, the one named last changes fastest.
Arguments:
- tokens: bfloat16 [16384, 1024], P(('fsdp', 'tp')), may hold values from -6 to 6
- segment_ids: int32 [16, 1024], P('fsdp'), may hold values from 0 to 3, never falling along the last dimension, each value on 1 to 768 neighbouring positions
- w_qkv: bfloat16 [1024, 3, 1024], P('fsdp', None, 'tp'), may hold values from -0.1875 to 0.1875
- b_qv: float32 [2, 1024], replicated, may hold values from -3 to 3
- w_out: bfloat16 [1024, 1024], P('fsdp', 'tp'), may hold values from -1.5 to 1.5
- b_out: float32 [1024], replicated, may hold values from -3 to 3
- w_up: bfloat16 [1024, 4096], P('fsdp', 'tp'), may hold values from -0.1875 to 0.1875
- b_up: float32 [4096], replicated, may hold values from -3 to 3
- w_down: bfloat16 [1024, 4096], P('fsdp', 'tp'), may hold values from -0.09375 to 0.09375
- b_down: float32 [1024], replicated, may hold values from -3 to 3
- ln1_gain: float32 [1024], replicated, may hold values from 0.1 to 1.9
- ln1_shift: float32 [1024], replicated, may hold values from -2 to 2
- ln2_gain: float32 [1024], replicated, may hold values from 0.1 to 1.9
- ln2_shift: float32 [1024], replicated, may hold values from -2 to 2
- grad_out: bfloat16 [16384, 1024], P(('fsdp', 'tp')), may hold values from -6 to 6
Outputs:
- result: bfloat16 [16384, 1024], P(('fsdp', 'tp'))
- token_grad: bfloat16 [16384, 1024], P(('fsdp', 'tp'))
- grad_w_qkv: float32 [1024, 3, 1024], P('fsdp', None, 'tp')
- grad_b_qv: float32 [2, 1024], replicated
- grad_w_out: float32 [1024, 1024], P('fsdp', 'tp')
- grad_b_out: float32 [1024], replicated
- grad_w_up: float32 [1024, 4096], P('fsdp', 'tp')
- grad_b_up: float32 [4096], replicated
- grad_w_down: float32 [1024, 4096], P('fsdp', 'tp')
- grad_b_down: float32 [1024], replicated
- grad_ln1_gain: float32 [1024], replicated
- grad_ln1_shift: float32 [1024], replicated
- grad_ln2_gain: float32 [1024], replicated
- grad_ln2_shift: float32 [1024], replicated
Inputs may be any that keep to these rules, and one draw needn't show every extreme that they name: `segment_ids`: along a sequence the ids never fall; each of the 4 documents of a sequence is a run of 1 to 768 tokens, and some run has exactly 768.
All inputs are finite; a program needn't handle non-finite values.
Results may differ from a plain program's by a relative error of at most 0.017.
Values may be sent and summed in bfloat16 or wider, within the bound.
No kernel may reach another device: no remote copies, remote signals or barrier semaphores. Data moves between devices by JAX's collectives and lax.ppermute only.
A program may use at most 192 MiB of HBM per device.

v0:
```python
import jax
import jax.numpy as jnp
from jax import lax
from jax.sharding import PartitionSpec as P

HEAD_DIM = 64


EPS = 1e-05


def norm_forward(values, gain, shift):
    centred = values - jnp.mean(values, axis=-1, keepdims=True)
    inverse = lax.rsqrt(jnp.mean(centred * centred, axis=-1, keepdims=True) + EPS)
    unit = centred * inverse
    return (unit * gain + shift, unit, inverse)


def norm_backward(grad, unit, inverse, gain):
    scaled = grad * gain
    return inverse * (
        scaled
        - jnp.mean(scaled, axis=-1, keepdims=True)
        - unit * jnp.mean(scaled * unit, axis=-1, keepdims=True)
    )


def score_block(query, key, segment):
    length = segment.shape[0]
    place = jnp.arange(length, dtype=jnp.int32)
    allowed = (segment[:, None] == segment[None, :]) & (place[None, :] <= place[:, None])
    scores = jnp.einsum(
        "qhd,khd->hqk", query, key, preferred_element_type=jnp.float32
    ) * query.shape[-1] ** (-0.5)
    return jnp.where(allowed[None], scores, -1e30)


def attend_forward(item):
    query, key, value, segment = item
    scores = score_block(query, key, segment)
    top = jnp.max(scores, axis=-1, keepdims=True)
    expo = jnp.exp(scores - top)
    total = jnp.sum(expo, axis=-1, keepdims=True)
    probs = (expo / total).astype(jnp.bfloat16)
    mixed = jnp.einsum("hqk,khd->qhd", probs, value, preferred_element_type=jnp.float32)
    return (mixed.astype(jnp.bfloat16), top + jnp.log(total))


def attend_backward(item):
    query, key, value, segment, log_total, mixed_grad = item
    scale = query.shape[-1] ** (-0.5)
    probs = jnp.exp(score_block(query, key, segment) - log_total)
    value_grad = jnp.einsum(
        "hqk,qhd->khd", probs.astype(jnp.bfloat16), mixed_grad, preferred_element_type=jnp.float32
    )
    prob_grad = jnp.einsum("qhd,khd->hqk", mixed_grad, value, preferred_element_type=jnp.float32)
    inner = jnp.sum(probs * prob_grad, axis=-1, keepdims=True)
    score_grad = (probs * (prob_grad - inner)).astype(jnp.bfloat16)
    query_grad = (
        jnp.einsum("hqk,khd->qhd", score_grad, key, preferred_element_type=jnp.float32) * scale
    )
    key_grad = (
        jnp.einsum("hqk,qhd->khd", score_grad, query, preferred_element_type=jnp.float32) * scale
    )
    return (
        query_grad.astype(jnp.bfloat16),
        key_grad.astype(jnp.bfloat16),
        value_grad.astype(jnp.bfloat16),
    )


def per_device(
    tokens,
    segment_ids,
    w_qkv,
    b_qv,
    w_out,
    b_out,
    w_up,
    b_up,
    w_down,
    b_down,
    ln1_gain,
    ln1_shift,
    ln2_gain,
    ln2_shift,
    grad_out,
):
    whole_qkv, whole_out, whole_up, whole_down = (
        lax.all_gather(w_qkv, "fsdp", axis=0, tiled=True),
        lax.all_gather(w_out, "fsdp", axis=0, tiled=True),
        lax.all_gather(w_up, "fsdp", axis=0, tiled=True),
        lax.all_gather(w_down, "fsdp", axis=0, tiled=True),
    )
    local_width = whole_qkv.shape[2]
    hidden_width = whole_up.shape[1]
    tp_index = lax.axis_index("tp")
    bias_query = lax.dynamic_slice_in_dim(b_qv[0], tp_index * local_width, local_width, 0)
    bias_value = lax.dynamic_slice_in_dim(b_qv[1], tp_index * local_width, local_width, 0)
    bias_hidden = lax.dynamic_slice_in_dim(b_up, tp_index * hidden_width, hidden_width, 0)
    token_vals = tokens.astype(jnp.float32)
    first_norm, first_unit, first_inverse = norm_forward(token_vals, ln1_gain, ln1_shift)
    first_low = first_norm.astype(jnp.bfloat16)
    first_all = lax.all_gather(first_low, "tp", axis=0, tiled=True)
    proj = jnp.einsum("rd,dcf->rcf", first_all, whole_qkv, preferred_element_type=jnp.float32)
    group_rows = proj.shape[0]
    seq_count, length = segment_ids.shape
    heads_local = local_width // HEAD_DIM

    def heads_view(block):
        return block.reshape(seq_count, length, heads_local, HEAD_DIM)

    query = heads_view((proj[:, 0] + bias_query).astype(jnp.bfloat16))
    key = heads_view(proj[:, 1].astype(jnp.bfloat16))
    value = heads_view((proj[:, 2] + bias_value).astype(jnp.bfloat16))
    mixed, log_total = lax.map(attend_forward, (query, key, value, segment_ids))
    mixed_rows = mixed.reshape(group_rows, local_width)
    branch_part = jnp.einsum("rf,df->rd", mixed_rows, whole_out, preferred_element_type=jnp.float32)
    branch = lax.psum_scatter(branch_part, "tp", scatter_dimension=0, tiled=True)
    middle = token_vals + branch + b_out
    second_norm, second_unit, second_inverse = norm_forward(middle, ln2_gain, ln2_shift)
    second_all = lax.all_gather(second_norm.astype(jnp.bfloat16), "tp", axis=0, tiled=True)
    pre_gelu = jnp.dot(second_all, whole_up, preferred_element_type=jnp.float32) + bias_hidden
    gelu_low = jax.nn.gelu(pre_gelu, approximate=True).astype(jnp.bfloat16)
    down_part = jnp.einsum("rf,df->rd", gelu_low, whole_down, preferred_element_type=jnp.float32)
    down = lax.psum_scatter(
        down_part.astype(jnp.bfloat16), "tp", scatter_dimension=0, tiled=True
    ).astype(jnp.float32)
    result = (middle + down + b_down).astype(jnp.bfloat16)
    grad_vals = grad_out.astype(jnp.float32)
    grad_all = lax.all_gather(grad_out, "tp", axis=0, tiled=True)
    grad_down_w = jnp.einsum("rd,rf->df", grad_all, gelu_low, preferred_element_type=jnp.float32)
    gelu_grad = jnp.einsum("rd,df->rf", grad_all, whole_down, preferred_element_type=jnp.float32)
    gelu_pull = jax.vjp(lambda inside: jax.nn.gelu(inside, approximate=True), pre_gelu)[1]
    pre_grad = gelu_pull(gelu_grad)[0].astype(jnp.bfloat16)
    grad_up_w = jnp.einsum("rd,rf->df", second_all, pre_grad, preferred_element_type=jnp.float32)
    second_part = jnp.einsum("rf,df->rd", pre_grad, whole_up, preferred_element_type=jnp.float32)
    second_grad = lax.psum_scatter(second_part, "tp", scatter_dimension=0, tiled=True)
    middle_grad = grad_vals + norm_backward(second_grad, second_unit, second_inverse, ln2_gain)
    branch_grad_all = lax.all_gather(middle_grad.astype(jnp.bfloat16), "tp", axis=0, tiled=True)
    ln2_gain_grad = jnp.sum(second_grad * second_unit, axis=0)
    ln2_shift_grad = jnp.sum(second_grad, axis=0)
    grad_out_w = jnp.einsum(
        "rd,rf->df", branch_grad_all, mixed_rows, preferred_element_type=jnp.float32
    )
    mixed_grad = jnp.einsum(
        "rd,df->rf", branch_grad_all, whole_out, preferred_element_type=jnp.float32
    ).astype(jnp.bfloat16)
    query_grad, key_grad, value_grad = lax.map(
        attend_backward, (query, key, value, segment_ids, log_total, heads_view(mixed_grad))
    )
    stacked = jnp.stack(
        [
            query_grad.reshape(group_rows, local_width),
            key_grad.reshape(group_rows, local_width),
            value_grad.reshape(group_rows, local_width),
        ],
        axis=1,
    )
    grad_qkv_w = jnp.einsum("rd,rcf->dcf", first_all, stacked, preferred_element_type=jnp.float32)
    first_part = jnp.einsum("rcf,dcf->rd", stacked, whole_qkv, preferred_element_type=jnp.float32)
    first_grad = lax.psum_scatter(
        first_part.astype(jnp.bfloat16), "tp", scatter_dimension=0, tiled=True
    ).astype(jnp.float32)
    token_grad = (
        middle_grad + norm_backward(first_grad, first_unit, first_inverse, ln1_gain)
    ).astype(jnp.bfloat16)
    grad_w_qkv, grad_w_out, grad_w_up, grad_w_down = (
        lax.psum_scatter(
            grad_qkv_w.astype(jnp.bfloat16), "fsdp", scatter_dimension=0, tiled=True
        ).astype(jnp.float32),
        lax.psum_scatter(
            grad_out_w.astype(jnp.bfloat16), "fsdp", scatter_dimension=0, tiled=True
        ).astype(jnp.float32),
        lax.psum_scatter(
            grad_up_w.astype(jnp.bfloat16), "fsdp", scatter_dimension=0, tiled=True
        ).astype(jnp.float32),
        lax.psum_scatter(
            grad_down_w.astype(jnp.bfloat16), "fsdp", scatter_dimension=0, tiled=True
        ).astype(jnp.float32),
    )
    column_sums = jnp.sum(stacked.astype(jnp.float32), axis=0)
    qv_local = jnp.stack([column_sums[0], column_sums[2]], axis=0)
    qv_padded = lax.dynamic_update_slice_in_dim(
        jnp.zeros(b_qv.shape, jnp.float32), qv_local, tp_index * local_width, 1
    )
    hidden_local = jnp.sum(pre_grad.astype(jnp.float32), axis=0)
    hidden_padded = lax.dynamic_update_slice_in_dim(
        jnp.zeros(b_up.shape, jnp.float32), hidden_local, tp_index * hidden_width, 0
    )
    small = lax.psum(
        (
            qv_padded,
            jnp.sum(middle_grad, axis=0),
            hidden_padded,
            jnp.sum(grad_vals, axis=0),
            jnp.sum(first_grad * first_unit, axis=0),
            jnp.sum(first_grad, axis=0),
            ln2_gain_grad,
            ln2_shift_grad,
        ),
        ("fsdp", "tp"),
    )
    return (
        result,
        token_grad,
        grad_w_qkv,
        small[0],
        grad_w_out,
        small[1],
        grad_w_up,
        small[2],
        grad_w_down,
        small[3],
        small[4],
        small[5],
        small[6],
        small[7],
    )


def solution(mesh):
    placed = (
        P(("fsdp", "tp"), None),
        P("fsdp", None),
        P("fsdp", None, "tp"),
        P(),
        P("fsdp", "tp"),
        P(),
        P("fsdp", "tp"),
        P(),
        P("fsdp", "tp"),
        P(),
        P(),
        P(),
        P(),
        P(),
        P(("fsdp", "tp"), None),
    )
    return jax.shard_map(
        per_device,
        mesh=mesh,
        in_specs=placed,
        out_specs=(
            P(("fsdp", "tp"), None),
            P(("fsdp", "tp"), None),
            P("fsdp", None, "tp"),
            P(),
            P("fsdp", "tp"),
            P(),
            P("fsdp", "tp"),
            P(),
            P("fsdp", "tp"),
            P(),
            P(),
            P(),
            P(),
            P(),
        ),
        check_vma=False,
    )
```

profile of v0, /device:TPU:0, one launch (start us, length us, event | category | flops | bytes accessed | tf_op | source)
XLA Modules:
  0.0 1703.4 jit_solution(11786888579731748366)
XLA Ops:
  14.2 7.2 all_gather.26
  21.5 8.7 all_gather.25
  30.2 111.6 %all-gather.7.cloned.1.call-done = bf16[4096,1024]{1,0:T(8,128)(2,1)} async-done(((bf16[512,1024]{1,0:T(8,128)(2,1)}), bf16[4096,1024]{1,0:T(8,128)(2,1)}) %all-gather.7.cloned.1.call-update) | async-done | bytes 8388624 | tf_op jit(solution)/shard_map/all_gather | solution.py:104
  141.7 6.9 fusion.70
  157.5 4.6 copy.52
  172.2 32.5 %while.26 = (s32[]{:T(128)}, bf16[4,1024,2,64]{1,3,2,0:T(8,128)(2,1)}, f32[4,2,1024,1]{2,1,3,0:T(2,128)S(1)}, bf16[4,1024,2,64]{1,3,2,0:T(8,128)(2,1)S(1)}, s32[...) while((s32[]{:T(128)}, ...), condition=%wide.region_5.6_spmd, body=%wide.region_2.5_spmd.sunk | while | flops 565311488 | bytes 30488676 | solution.py:116
  208.9 8.1 fusion.102
  217.7 279.9 %reduce-scatter.9.cloned.1.call-done = f32[512,1024]{1,0:T(8,128)} async-done(((f32[4096,1024]{1,0:T(8,128)}), f32[512,1024]{1,0:T(8,128)}) %reduce-scatter.9.cloned.1.call-update) | async-done | bytes 2097168 | tf_op jit(solution)/shard_map/reduce_scatter | solution.py:119
  503.5 121.6 %all-gather.9.cloned.1.call-done = bf16[4096,1024]{1,0:T(8,128)(2,1)} async-done(((bf16[512,1024]{1,0:T(8,128)(2,1)}), bf16[4096,1024]{1,0:T(8,128)(2,1)}) %all-gather.9.cloned.1.call-update) | async-done | bytes 8388624 | tf_op jit(solution)/shard_map/all_gather | solution.py:122
  625.1 11.3 fusion.103
  636.4 4.9 all-gather.13.cloned.1.call-done
  641.4 126.9 %all-gather.15.cloned.1.call-done = bf16[4096,1024]{1,0:T(8,128)(2,1)} async-done(((bf16[512,1024]{1,0:T(8,128)(2,1)}), bf16[4096,1024]{1,0:T(8,128)(2,1)}) %all-gather.15.cloned.1.call-update) | async-done | bytes 8388624 | tf_op jit(solution)/shard_map/all_gather | solution.py:131
  768.3 14.5 convert_reduce_fusion
  784.7 8.4 fusion.104
  794.4 12.3 convolution_convert_fusion
  806.8 264.1 %reduce-scatter.13.cloned.1.call-done = f32[512,1024]{1,0:T(8,128)} async-done(((f32[4096,1024]{1,0:T(8,128)}), f32[512,1024]{1,0:T(8,128)}) %reduce-scatter.13.cloned.1.call-update) | async-done | bytes 2097168 | tf_op jit(solution)/shard_map/reduce_scatter | solution.py:138
  1074.0 146.7 %reduce-scatter.11.cloned.1.call-done = bf16[512,1024]{1,0:T(8,128)(2,1)} async-done(((bf16[4096,1024]{1,0:T(8,128)(2,1)}), bf16[512,1024]{1,0:T(8,128)(2,1)}) %reduce-scatter.11.cloned.1.call-update) | async-done | bytes 1048592 | tf_op jit(solution)/shard_map/reduce_scatter | solution.py:126
  1220.7 4.0 fusion.96
  1227.3 11.4 fusion.92
  1239.2 10.3 convolution_convert_fusion.3
  1249.6 101.9 %all-gather.17.cloned.1.call-done = bf16[4096,1024]{1,0:T(8,128)(2,1)} async-done(((bf16[512,1024]{1,0:T(8,128)(2,1)}), bf16[4096,1024]{1,0:T(8,128)(2,1)}) %all-gather.17.cloned.1.call-update) | async-done | bytes 8388624 | tf_op jit(solution)/shard_map/all_gather | solution.py:140
  1351.5 5.7 convolution_convert_fusion.1
  1359.0 4.6 copy.57
  1367.0 63.0 %while.27 = (s32[]{:T(128)}, bf16[4,1024,2,64]{1,3,2,0:T(8,128)(2,1)}, bf16[4,1024,2,64]{1,3,2,0:T(8,128)(2,1)}, bf16[4,1024,2,64]{1,3,2,0:T(8,128)(2,1)}, bf16[...) while((s32[]{:T(128)}, ...), condition=%wide.region_15.16_spmd, body=%wide.region_13.15_spmd.sunk | while | flops 1377433600 | bytes 78193840 | solution.py:149
  1430.0 4.5 copy.76
  1436.4 4.5 copy.74
  1447.5 6.7 convolution_convert_fusion.4
  1457.0 9.1 fusion.89
  1466.2 7.9 bitcast_convert_fusion
  1482.9 15.9 reduce-scatter.17.cloned.1.call-done
  1500.5 149.3 %reduce-scatter.15.cloned.1.call-done = bf16[512,1024]{1,0:T(8,128)(2,1)} async-done(((bf16[4096,1024]{1,0:T(8,128)(2,1)}), bf16[512,1024]{1,0:T(8,128)(2,1)}) %reduce-scatter.15.cloned.1.call-update) | async-done | bytes 1048592 | tf_op jit(solution)/shard_map/reduce_scatter | solution.py:162
  1652.1 40.8 %all-reduce = (f32[2,1024]{1,0:T(2,128)}, f32[1024]{0:T(1024)}, f32[4096]{0:T(1024)}, f32[1024]{0:T(1024)}, f32[1024]{0:T(1024)}, /*index=5*/f32[1024]{0:T(1024)}, f32[1024]{0:T(1024)}, f32[1024]{0:T(1024)}) all-reduce(f32[2,1024]{1,0:T(2,128)S(1)} %maximum_dynamic-update-slice_fusion, ...), channel_id=1, replica_groups=mesh['fsdp'=4,'tp'=8] {'fsdp','tp'}, use_global_device_ids=true, to_apply=%region_21.22 | all-reduce | flops 12288 | bytes 98304 | tf_op jit(solution)/shard_map/psum | solution.py:191
  (237 shorter events, 171.8 us)
Async XLA Ops:
  8.0 13.4 copy-start.16
  8.0 133.7 %all-gather.7.cloned.1.call-start = ((), (), s32[]{:S(2)}) async-start(), calls=%async_computation.8 | async-start | bytes 9437184 | tf_op jit(solution)/shard_map/all_gather | solution.py:104
  14.0 483.7 %reduce-scatter.9.cloned.1.call-start = ((), (), s32[]{:S(2)}) async-start(), calls=%async_computation.9 | async-start | bytes 18874368 | tf_op jit(solution)/shard_map/reduce_scatter | solution.py:119
  30.2 118.5 %copy-start.15 = (bf16[1024,3,128]{2,0,1:T(8,128)(2,1)}, bf16[1024,3,128]{2,0,1:T(8,128)(2,1)S(1)}, u32[]{:S(2)}) copy-start(bf16[1024,3,128]{2,0,1:T(8,128)(2,1)S(1)} %all_gather.25) | copy-start | bytes 2359300
  217.0 280.6 %copy-start = (bf16[512,1024]{1,0:T(8,128)(2,1)S(1)}, bf16[512,1024]{1,0:T(8,128)(2,1)}, u32[]{:S(2)}) copy-start(bf16[512,1024]{1,0:T(8,128)(2,1)} %param.19) | copy-start | bytes 3145732
  217.0 280.6 %copy-start.32 = (f32[1024]{0:T(1024)S(1)}, f32[1024]{0:T(1024)}, u32[]{:S(2)}) copy-start(f32[1024]{0:T(1024)} %param.24) | copy-start | bytes 12292
  217.1 282.9 %copy-start.21 = (f32[1024]{0:T(1024)S(1)}, f32[1024]{0:T(1024)}, u32[]{:S(2)}) copy-start(f32[1024]{0:T(1024)} %param.31) | copy-start | bytes 12292
  217.1 282.9 %copy-start.30 = (f32[1024]{0:T(1024)S(1)}, f32[1024]{0:T(1024)}, u32[]{:S(2)}) copy-start(f32[1024]{0:T(1024)} %param.32) | copy-start | bytes 12292
  217.1 286.4 %all-gather.11.cloned.1.call-start = ((), (), s32[]{:S(2)}) async-start(), calls=%async_computation.11 | async-start | bytes 1310720 | tf_op jit(solution)/shard_map/all_gather | solution.py:92
  217.7 407.4 %all-gather.9.cloned.1.call-start = ((), (), s32[]{:S(2)}) async-start(), calls=%async_computation.10 | async-start | bytes 9437184 | tf_op jit(solution)/shard_map/all_gather | solution.py:122
  501.4 140.0 %all-gather.13.cloned.1.call-start = ((), (), s32[]{:S(2)}) async-start(), calls=%async_computation.12 | async-start | bytes 1310720 | tf_op jit(solution)/shard_map/all_gather | solution.py:93
  502.0 266.3 %all-gather.15.cloned.1.call-start = ((), (), s32[]{:S(2)}) async-start(), calls=%async_computation.14 | async-start | bytes 9437184 | tf_op jit(solution)/shard_map/all_gather | solution.py:131
  502.7 568.2 %reduce-scatter.13.cloned.1.call-start = ((), (), s32[]{:S(2)}) async-start(), calls=%async_computation.15 | async-start | bytes 18874368 | tf_op jit(solution)/shard_map/reduce_scatter | solution.py:138
  636.4 148.3 %copy-start.34 = (bf16[1024,512]{1,0:T(8,128)(2,1)S(1)}, bf16[1024,512]{1,0:T(8,128)(2,1)}, u32[]{:S(2)}) copy-start(bf16[1024,512]{1,0:T(8,128)(2,1)} %all-gather.11.cloned.1.call-done) | copy-start | bytes 3145732
  793.2 427.5 %reduce-scatter.11.cloned.1.call-start = ((), (), s32[]{:S(2)}) async-start(), calls=%async_computation.13 | async-start | bytes 9437184 | tf_op jit(solution)/shard_map/reduce_scatter | solution.py:126
  806.7 414.0 %copy-start.14 = (bf16[512,1024]{1,0:T(8,128)(2,1)S(1)}, bf16[512,1024]{1,0:T(8,128)(2,1)}, u32[]{:S(2)}) copy-start(bf16[512,1024]{1,0:T(8,128)(2,1)} %param.33) | copy-start | bytes 3145732
  806.7 414.0 %copy-start.31 = (f32[1024]{0:T(1024)S(1)}, f32[1024]{0:T(1024)}, u32[]{:S(2)}) copy-start(f32[1024]{0:T(1024)} %param.28) | copy-start | bytes 12292
  806.7 544.7 %all-gather.17.cloned.1.call-start = ((), (), s32[]{:S(2)}) async-start(), calls=%async_computation.16 | async-start | bytes 9437184 | tf_op jit(solution)/shard_map/all_gather | solution.py:140
  1227.3 247.6 %reduce-scatter.23.cloned.1.call-start = ((), (), s32[]{:S(2)}) async-start(), calls=%async_computation.21 | async-start | bytes 1310720 | tf_op jit(solution)/shard_map/reduce_scatter | solution.py:178
  1238.8 238.2 %reduce-scatter.21.cloned.1.call-start = ((), (), s32[]{:S(2)}) async-start(), calls=%async_computation.20 | async-start | bytes 1310720 | tf_op jit(solution)/shard_map/reduce_scatter | solution.py:175
  1249.6 231.8 %reduce-scatter.19.cloned.1.call-start = ((), (), s32[]{:S(2)}) async-start(), calls=%async_computation.19 | async-start | bytes 327680 | tf_op jit(solution)/shard_map/reduce_scatter | solution.py:172
  1454.2 44.6 %reduce-scatter.17.cloned.1.call-start = ((), (), s32[]{:S(2)}) async-start(), calls=%async_computation.18 | async-start | bytes 983040 | tf_op jit(solution)/shard_map/reduce_scatter | solution.py:169
  1466.1 183.6 %reduce-scatter.15.cloned.1.call-start = ((), (), s32[]{:S(2)}) async-start(), calls=%async_computation.17 | async-start | bytes 9437184 | tf_op jit(solution)/shard_map/reduce_scatter | solution.py:162
  1474.1 175.7 %copy-start.1 = (bf16[512,1024]{1,0:T(8,128)(2,1)S(1)}, bf16[512,1024]{1,0:T(8,128)(2,1)}, u32[]{:S(2)}) copy-start(bf16[512,1024]{1,0:T(8,128)(2,1)} %param.19) | copy-start | bytes 3145732
  1474.1 175.7 %copy-start.20 = (f32[512]{0:T(512)S(1)}, f32[512]{0:T(512)}, u32[]{:S(2)}) copy-start(f32[512]{0:T(512)} %copy-done.19) | copy-start | bytes 6148
  1474.1 175.7 %copy-start.22 = (f32[1024]{0:T(1024)S(1)}, f32[1024]{0:T(1024)}, u32[]{:S(2)}) copy-start(f32[1024]{0:T(1024)} %param.29) | copy-start | bytes 12292
  1474.1 175.6 %copy-start.24 = (f32[512]{0:T(512)S(1)}, f32[512]{0:T(512)}, u32[]{:S(2)}) copy-start(f32[512]{0:T(512)} %copy-done.23) | copy-start | bytes 6148
  1474.1 177.9 %copy-start.25 = (f32[1024]{0:T(1024)S(1)}, f32[1024]{0:T(1024)}, u32[]{:S(2)}) copy-start(f32[1024]{0:T(1024)} %get-tuple-element.173) | copy-start | bytes 12292
  1474.1 177.9 %copy-start.26 = (f32[1024]{0:T(1024)S(1)}, f32[1024]{0:T(1024)}, u32[]{:S(2)}) copy-start(f32[1024]{0:T(1024)} %get-tuple-element.178) | copy-start | bytes 12292
  1474.2 177.9 %copy-start.27 = (f32[1024]{0:T(1024)S(1)}, f32[1024]{0:T(1024)}, u32[]{:S(2)}) copy-start(f32[1024]{0:T(1024)} %get-tuple-element.225) | copy-start | bytes 12292
  1474.2 177.9 %copy-start.28 = (f32[1024]{0:T(1024)S(1)}, f32[1024]{0:T(1024)}, u32[]{:S(2)}) copy-start(f32[1024]{0:T(1024)} %get-tuple-element.236) | copy-start | bytes 12292
  1474.2 218.7 %copy-start.3 = (f32[512,1024]{1,0:T(8,128)S(1)}, f32[512,1024]{1,0:T(8,128)}, u32[]{:S(2)}) copy-start(f32[512,1024]{1,0:T(8,128)} %copy-done.2) | copy-start | bytes 6291460
  (25 other events, 116.0 us)
Sparse Core Ops, SparseCore 0:
  14.1 127.6 all-gather.6
  217.2 280.4 reduce-scatter.8
  1227.4 124.0 all-gather.16
Sparse Core Ops, SparseCore 1:
  219.1 14.8 all-gather.10
  501.5 123.6 all-gather.8
  626.6 14.7 all-gather.12
  643.7 124.5 all-gather.14
  793.3 277.6 reduce-scatter.12
  1074.5 146.1 reduce-scatter.10
  1238.9 23.9 reduce-scatter.22
  1265.2 24.8 reduce-scatter.20
  1454.3 18.1 reduce-scatter.18
  1475.6 23.2 reduce-scatter.16
  1502.7 147.0 reduce-scatter.14
where the time goes:
time: 1720 us; the launch traced here: 1700 us
  waiting for transfers between devices  1320 us (77%)
  matrix products  180 us (10%)
  local copies, waits for them, and re-layouts  67.4 us (4%)
  blocking collectives  56.7 us (3%)
  other arithmetic  56.4 us (3%)
    reduce_scatter x1, waiting for transfers between devices, per_device(): lax.psum_scatter(branch_part, 'tp', scatter_dimension=0, tiled=True)  280 us
    reduce_scatter x1, waiting for transfers between devices, per_device(): lax.psum_scatter(second_part, 'tp', scatter_dimension=0, tiled=True)  264 us
    reduce_scatter x1, waiting for transfers between devices, per_device(): lax.psum_scatter(first_part.astype(jnp.bfloat16), 'tp', scatter_dimension...  149 us
    reduce_scatter x1, waiting for transfers between devices, per_device(): lax.psum_scatter(down_part.astype(jnp.bfloat16), 'tp', scatter_dimension=...  147 us
    all_gather x1, waiting for transfers between devices, per_device(): grad_all = lax.all_gather(grad_out, 'tp', axis=0, tiled=True)  127 us
    all_gather x1, waiting for transfers between devices, per_device(): lax.all_gather(second_norm.astype(jnp.bfloat16), 'tp', axis=0, tiled=True)  122 us
    all_gather x1, waiting for transfers between devices, per_device(): first_all = lax.all_gather(first_low, 'tp', axis=0, tiled=True)  112 us
    all_gather x1, waiting for transfers between devices, per_device(): lax.all_gather(middle_grad.astype(jnp.bfloat16), 'tp', axis=0, tiled=True)  102 us
  transfers between devices with their start and end apart: 14, of which 10 were waited for; matrix products, arithmetic and copies ran while one was open for 11% of the time, Pallas kernels for 0%

commit v1 on v0

v1 whole, which is shorter than its diff:
```python
import functools

import jax
import jax.numpy as jnp
from jax import lax
from jax.experimental import pallas as pl
from jax.experimental.pallas import tpu as pltpu
from jax.sharding import Mesh, PartitionSpec as P

HEAD_DIM = 64
EPS = 1e-05
BF = jnp.bfloat16
F32 = jnp.float32
NT = (((1,), (1,)), ((), ()))
MIB = 1 << 20


def dot(a, b):
    return jnp.dot(a, b, preferred_element_type=F32)


def dot_nt(a, b):
    return lax.dot_general(a, b, NT, preferred_element_type=F32)


def aligned(value, multiple):
    return pl.multiple_of(value, multiple)


class Layout:
    def __init__(self, ny, nz, rows):
        self.ny, self.nz, self.rows = ny, nz, rows
        self.a = max(16, rows * 5 // 8 // 16 * 16)
        self.b = rows - self.a

    def row_block(self, pos, dy, dc):
        return lax.rem(pos[0] + dy, self.ny) * 2 + lax.rem(pos[1] + dc, 2)

    def col_block(self, pos, dz, dx):
        return lax.rem(pos[2] + dz, self.nz) * 2 + lax.rem(pos[3] + dx, 2)


def fetch(value, axis, size, shift):
    return lax.ppermute(value, axis, [(s, (s - shift) % size) for s in range(size)])


def deliver(value, axis, size, shift):
    return lax.ppermute(value, axis, [(s, (s + shift) % size) for s in range(size)])


def around(value, axis, size):
    return [value] + [fetch(value, axis, size, shift) for shift in range(1, size)]


def gather_group(lay, shard):
    top, low = shard[: lay.a], shard[lay.a :]
    top = jnp.stack(around(top, "tz", lay.nz))
    low = jnp.stack(around(low, "fy", lay.ny))
    top = jnp.stack(around(top, "tx", 2))
    low = jnp.stack(around(low, "tz", lay.nz))
    own = around(top, "fy", lay.ny) + around(low, "tx", 2)
    return own + [fetch(t, "c", 2, 1) for t in own]


def start_loads(lay, pos, refs, first, width, whole, sem):
    for dc in range(2):
        mine = refs[dc * (lay.ny + 2) : (dc + 1) * (lay.ny + 2)]
        for dz in range(lay.nz):
            for dx in range(2):
                k = lay.col_block(pos, dz, dx)
                cols = pl.ds(aligned(k * width, width), width)
                for dy in range(lay.ny):
                    start = aligned(lay.row_block(pos, dy, dc) * lay.rows, lay.rows)
                    pltpu.make_async_copy(
                        mine[dy].at[dx, dz, :, pl.ds(first, width)],
                        whole.at[pl.ds(start, lay.a), cols],
                        sem.at[k],
                    ).start()
                    pltpu.make_async_copy(
                        mine[lay.ny + dx].at[dz, dy, :, pl.ds(first, width)],
                        whole.at[pl.ds(aligned(start + lay.a, 16), lay.b), cols],
                        sem.at[k],
                    ).start()


def wait_load(k, width, whole, sem):
    cols = pl.ds(aligned(k * width, width), width)
    pltpu.make_async_copy(whole.at[:, cols], whole.at[:, cols], sem.at[k]).wait()


def kernel_call(body, pos, grid, ins, in_specs, outs, out_specs, scratch, flops, moved):
    return pl.pallas_call(
        body,
        out_shape=outs,
        grid_spec=pltpu.PrefetchScalarGridSpec(
            num_scalar_prefetch=1,
            grid=grid,
            in_specs=in_specs,
            out_specs=out_specs,
            scratch_shapes=scratch,
        ),
        compiler_params=pltpu.CompilerParams(
            dimension_semantics=("arbitrary",) * len(grid), vmem_limit_bytes=60 * MIB
        ),
        cost_estimate=pl.CostEstimate(flops=flops, bytes_accessed=moved, transcendentals=0),
    )(pos, *ins)


def shape(dims, dtype):
    return jax.ShapeDtypeStruct(dims, dtype)


def full(dims):
    return pl.BlockSpec(dims, lambda *_: (0,) * len(dims))


def at_cols(rows, width):
    return pl.BlockSpec((rows, width), lambda k, *_: (0, k))


def at_lead(*dims):
    return pl.BlockSpec((1,) + dims, lambda k, *_: (k,) + (0,) * len(dims))


ANY = pl.BlockSpec(memory_space=pl.ANY)


def norm_parts(values):
    centred = values - jnp.mean(values, axis=-1, keepdims=True)
    inverse = lax.rsqrt(jnp.mean(centred * centred, axis=-1, keepdims=True) + EPS)
    return centred * inverse, inverse


def norm_backward(grad, unit, inverse, gain):
    scaled = grad * gain
    return inverse * (
        scaled
        - jnp.mean(scaled, axis=-1, keepdims=True)
        - unit * jnp.mean(scaled * unit, axis=-1, keepdims=True)
    )


def qkv_call(lay, pos, first, bias_q, bias_v, weights, width):
    both, dim = first.shape
    rows = both // 2
    blocks = 2 * lay.nz
    n = len(weights)

    def body(pos_ref, first_ref, bq_ref, bv_ref, *rest):
        refs, (q_ref, k_ref, v_ref, whole, sem) = rest[:n], rest[n:]
        k = pl.program_id(0)

        @pl.when(k == 0)
        def _():
            start_loads(lay, pos_ref, refs, 0, 3 * width, whole, sem)

        wait_load(k, 3 * width, whole, sem)
        start = k * (3 * width)
        own = dot(first_ref[rows:], whole[:, pl.ds(aligned(start, width), 3 * width)])
        q_ref[0] = ((own[:, :width] + bq_ref[...]).astype(BF) * HEAD_DIM**-0.5).astype(BF)
        k_ref[0, rows:] = own[:, width : 2 * width].astype(BF)
        v_ref[0, rows:] = (own[:, 2 * width :] + bv_ref[...]).astype(BF)
        prev = dot(first_ref[:rows], whole[:, pl.ds(aligned(start + width, width), 2 * width)])
        k_ref[0, :rows] = prev[:, :width].astype(BF)
        v_ref[0, :rows] = (prev[:, width:] + bv_ref[...]).astype(BF)

    return kernel_call(
        body,
        pos,
        (blocks,),
        (first, bias_q, bias_v, *weights),
        [full((both, dim)), at_cols(1, width), at_cols(1, width)] + [ANY] * n,
        [
            shape((blocks, rows, width), BF),
            shape((blocks, both, width), BF),
            shape((blocks, both, width), BF),
        ],
        [at_lead(rows, width), at_lead(both, width), at_lead(both, width)],
        [pltpu.VMEM((dim, blocks * 3 * width), BF), pltpu.SemaphoreType.DMA((blocks,))],
        2 * dim * blocks * width * rows * 5,
        14 * MIB,
    )


def mask_bias(seg_k, seg_q, rows):
    both = seg_k.shape[0]
    key_at = lax.broadcasted_iota(jnp.int32, (both, rows), 0) - (both - rows)
    query_at = lax.broadcasted_iota(jnp.int32, (both, rows), 1)
    return jnp.where((seg_k == seg_q) & (key_at <= query_at), 0.0, -1e30).astype(F32)


def head_only(block, head):
    lane = lax.broadcasted_iota(jnp.int32, block.shape, 1)
    inside = (lane >= head * HEAD_DIM) & (lane < (head + 1) * HEAD_DIM)
    return jnp.where(inside, block, jnp.zeros_like(block))


def attend_call(pos, query, key, value, seg_k, seg_q):
    blocks, both, width = key.shape
    rows = query.shape[1]
    heads = width // HEAD_DIM
    step = min(rows, 256)

    def body(pos_ref, q_ref, k_ref, v_ref, sk_ref, sq_ref, mixed_ref, lse_ref, bias, out_t):
        @pl.when(pl.program_id(0) == 0)
        def _():
            bias[...] = mask_bias(sk_ref[...], sq_ref[...], rows)

        value_t = v_ref[0].T
        for tile in range(rows // step):
            here = slice(tile * step, (tile + 1) * step)
            keys = both - rows + (tile + 1) * step
            for head in range(heads):
                lanes = slice(head * HEAD_DIM, (head + 1) * HEAD_DIM)
                scores = dot_nt(k_ref[0, :keys], head_only(q_ref[0, here], head))
                scores = scores + bias[:keys, here]
                top = jnp.max(scores, axis=0, keepdims=True)
                expo = jnp.exp(scores - top)
                total = jnp.sum(expo, axis=0, keepdims=True)
                out = dot(value_t[lanes, :keys], expo.astype(BF))
                out_t[lanes, here] = out * (1.0 / total)
                lse_ref[0, head : head + 1, here] = top + jnp.log(total)
        mixed_ref[...] = out_t[...].T.astype(BF)

    return kernel_call(
        body,
        pos,
        (blocks,),
        (query, key, value, seg_k, seg_q),
        [at_lead(rows, width), at_lead(both, width), at_lead(both, width), full((both, 1)), full((1, rows))],
        [shape((rows, blocks * width), BF), shape((blocks, heads, rows), F32)],
        [at_cols(rows, width), at_lead(heads, rows)],
        [pltpu.VMEM((both, rows), F32), pltpu.VMEM((width, rows), F32)],
        blocks * heads * rows * both * 256 * 4,
        8 * MIB,
    )


def branch_call(lay, pos, mixed, tokens, b_out, gain, shift, weights, first, width):
    rows, dim = tokens.shape
    blocks = 2 * lay.nz
    n = len(weights)

    def body(pos_ref, mixed_ref, tok_ref, bias_ref, gain_ref, shift_ref, *rest):
        refs, (middle_ref, second_ref, whole, sem) = rest[:n], rest[n:]
        start_loads(lay, pos_ref, refs, first, width, whole, sem)
        for k in range(blocks):
            wait_load(k, width, whole, sem)
        branch = dot_nt(mixed_ref[...], whole[...])
        middle = tok_ref[...].astype(F32) + branch + bias_ref[...]
        middle_ref[...] = middle
        second_ref[...] = (norm_parts(middle)[0] * gain_ref[...] + shift_ref[...]).astype(BF)

    return kernel_call(
        body,
        pos,
        (),
        (mixed, tokens, b_out, gain, shift, *weights),
        [full(mixed.shape), full(tokens.shape)] + [full((1, dim))] * 3 + [ANY] * n,
        [shape((rows, dim), F32), shape((rows, dim), BF)],
        [full((rows, dim)), full((rows, dim))],
        [pltpu.VMEM((dim, blocks * width), BF), pltpu.SemaphoreType.DMA((blocks,))],
        2 * rows * dim * blocks * width,
        7 * MIB,
    )


def up_call(lay, pos, second, b_up, weights, width):
    rows, dim = second.shape
    blocks = 2 * lay.nz
    n = len(weights)

    def body(pos_ref, second_ref, bias_ref, *rest):
        refs, (gelu_ref, slope_ref, whole, sem) = rest[:n], rest[n:]
        k = pl.program_id(0)

        @pl.when(k == 0)
        def _():
            start_loads(lay, pos_ref, refs, 0, width, whole, sem)

        wait_load(k, width, whole, sem)
        u = dot(second_ref[...], whole[:, pl.ds(aligned(k * width, width), width)]) + bias_ref[...]
        scale = 0.7978845608028654
        square = u * u
        th = jnp.tanh(u * (scale + (scale * 0.044715) * square))
        half = 0.5 + 0.5 * th
        gelu_ref[...] = (u * half).astype(BF)
        slope = half + (0.5 * u) * (1.0 - th * th) * (scale + (3.0 * scale * 0.044715) * square)
        slope_ref[...] = slope.astype(BF)

    return kernel_call(
        body,
        pos,
        (blocks,),
        (second, b_up, *weights),
        [full(second.shape), at_cols(1, width)] + [ANY] * n,
        [shape((rows, blocks * width), BF)] * 2,
        [at_cols(rows, width)] * 2,
        [pltpu.VMEM((dim, blocks * width), BF), pltpu.SemaphoreType.DMA((blocks,))],
        2 * rows * dim * blocks * width,
        17 * MIB,
    )


def ffn_back_call(lay, pos, gelu, slope, grad, middle, b_down, gain, w_down, w_up, width):
    rows, dim = middle.shape
    blocks = 2 * lay.nz
    n = len(w_down)

    def body(pos_ref, gelu_ref, slope_ref, grad_ref, middle_ref, bias_ref, gain_ref, *rest):
        down_refs, up_refs = rest[:n], rest[n : 2 * n]
        pre_ref, hidden_ref, result_ref, mgrad_ref, low_ref, sums_ref = rest[2 * n : 2 * n + 6]
        down, up, acc_down, acc_second, sem_down, sem_up = rest[2 * n + 6 :]
        k = pl.program_id(0)

        @pl.when(k == 0)
        def _():
            start_loads(lay, pos_ref, down_refs, 0, width, down, sem_down)
            start_loads(lay, pos_ref, up_refs, 0, width, up, sem_up)
            acc_down[...] = jnp.zeros_like(acc_down)
            acc_second[...] = jnp.zeros_like(acc_second)

        cols = pl.ds(aligned(k * width, width), width)
        wait_load(k, width, down, sem_down)
        acc_down[...] += dot_nt(gelu_ref[...], down[:, cols])
        pre = (dot(grad_ref[...], down[:, cols]) * slope_ref[...].astype(F32)).astype(BF)
        pre_ref[...] = pre
        hidden_ref[...] = jnp.sum(pre.astype(F32), axis=0, keepdims=True)
        wait_load(k, width, up, sem_up)
        acc_second[...] += dot_nt(pre, up[:, cols])

        @pl.when(k == blocks - 1)
        def _():
            values = middle_ref[...]
            result_ref[...] = (values + acc_down[...] + bias_ref[...]).astype(BF)
            unit, inverse = norm_parts(values)
            second_grad = acc_second[...]
            sums_ref[0:1] = jnp.sum(second_grad * unit, axis=0, keepdims=True)
            sums_ref[1:2] = jnp.sum(second_grad, axis=0, keepdims=True)
            out = grad_ref[...].astype(F32)
            sums_ref[3:4] = jnp.sum(out, axis=0, keepdims=True)
            out = out + norm_backward(second_grad, unit, inverse, gain_ref[...])
            sums_ref[2:3] = jnp.sum(out, axis=0, keepdims=True)
            mgrad_ref[...] = out
            low_ref[...] = out.astype(BF)

    return kernel_call(
        body,
        pos,
        (blocks,),
        (gelu, slope, grad, middle, b_down, gain, *w_down, *w_up),
        [at_cols(rows, width)] * 2
        + [full((rows, dim))] * 2
        + [full((1, dim))] * 2
        + [ANY] * (2 * n),
        [
            shape((rows, blocks * width), BF),
            shape((1, blocks * width), F32),
            shape((rows, dim), BF),
            shape((rows, dim), F32),
            shape((rows, dim), BF),
            shape((4, dim), F32),
        ],
        [at_cols(rows, width), at_cols(1, width)] + [full((rows, dim))] * 3 + [full((4, dim))],
        [
            pltpu.VMEM((dim, blocks * width), BF),
            pltpu.VMEM((dim, blocks * width), BF),
            pltpu.VMEM((rows, dim), F32),
            pltpu.VMEM((rows, dim), F32),
            pltpu.SemaphoreType.DMA((blocks,)),
            pltpu.SemaphoreType.DMA((blocks,)),
        ],
        6 * rows * dim * blocks * width,
        36 * MIB,
    )


def mixed_grad_call(lay, pos, low, weights, first, width):
    rows, dim = low.shape
    blocks = 2 * lay.nz
    n = len(weights)

    def body(pos_ref, low_ref, *rest):
        refs, (out_ref, whole, sem) = rest[:n], rest[n:]
        start_loads(lay, pos_ref, refs, first, width, whole, sem)
        for k in range(blocks):
            wait_load(k, width, whole, sem)
        out_ref[...] = dot(low_ref[...], whole[...]).astype(BF)

    return kernel_call(
        body,
        pos,
        (),
        (low, *weights),
        [full((rows, dim))] + [ANY] * n,
        [shape((rows, blocks * width), BF)],
        [full((rows, blocks * width))],
        [pltpu.VMEM((dim, blocks * width), BF), pltpu.SemaphoreType.DMA((blocks,))],
        2 * rows * dim * blocks * width,
        4 * MIB,
    )[0]


def attend_back_call(pos, query, key, value, seg_k, seg_q, lse, mixed_grad):
    blocks, both, width = key.shape
    rows = query.shape[1]
    heads = width // HEAD_DIM
    step = min(rows, 256)

    def body(pos_ref, q_ref, k_ref, v_ref, sk_ref, sq_ref, lse_ref, grad_ref, *rest):
        dq_ref, dk_ref, dv_ref, sums_ref, bias, dq_t, dk, dv = rest

        @pl.when(pl.program_id(0) == 0)
        def _():
            bias[...] = mask_bias(sk_ref[...], sq_ref[...], rows)

        key_t = k_ref[0].T
        dk[...] = jnp.zeros_like(dk)
        dv[...] = jnp.zeros_like(dv)
        for tile in range(rows // step):
            here = slice(tile * step, (tile + 1) * step)
            keys = both - rows + (tile + 1) * step
            for head in range(heads):
                lanes = slice(head * HEAD_DIM, (head + 1) * HEAD_DIM)
                q_head = head_only(q_ref[0, here], head)
                g_head = head_only(grad_ref[here], head)
                scores = dot_nt(k_ref[0, :keys], q_head) + bias[:keys, here]
                probs = jnp.exp(scores - lse_ref[0, head : head + 1, here])
                prob_grad = dot_nt(v_ref[0, :keys], g_head)
                inner = jnp.sum(probs * prob_grad, axis=0, keepdims=True)
                score_grad = (probs * (prob_grad - inner)).astype(BF)
                dv[:keys] += dot(probs.astype(BF), g_head)
                dk[:keys] += dot(score_grad, q_head)
                dq_t[lanes, here] = dot(key_t[lanes, :keys], score_grad)
        dq = (dq_t[...].T * HEAD_DIM**-0.5).astype(BF)
        dv_low = dv[...].astype(BF)
        dq_ref[0] = dq
        dk_ref[0] = dk[...].astype(BF)
        dv_ref[0] = dv_low
        sums_ref[0:1] = jnp.sum(dq.astype(F32), axis=0, keepdims=True)
        sums_ref[1:2] = jnp.sum(dv_low.astype(F32), axis=0, keepdims=True)

    return kernel_call(
        body,
        pos,
        (blocks,),
        (query, key, value, seg_k, seg_q, lse, mixed_grad),
        [
            at_lead(rows, width),
            at_lead(both, width),
            at_lead(both, width),
            full((both, 1)),
            full((1, rows)),
            at_lead(heads, rows),
            at_cols(rows, width),
        ],
        [
            shape((blocks, rows, width), BF),
            shape((blocks, both, width), BF),
            shape((blocks, both, width), BF),
            shape((2, blocks * width), F32),
        ],
        [at_lead(rows, width), at_lead(both, width), at_lead(both, width), at_cols(2, width)],
        [
            pltpu.VMEM((both, rows), F32),
            pltpu.VMEM((width, rows), F32),
            pltpu.VMEM((both, width), F32),
            pltpu.VMEM((both, width), F32),
        ],
        blocks * heads * rows * both * 256 * 8,
        12 * MIB,
    )


def first_grad_call(lay, pos, dq, dk, dv, prev, own, weights, width):
    rows, dim = own.shape
    blocks = 2 * lay.nz
    n = len(weights)

    def body(pos_ref, dq_ref, dk_ref, dv_ref, prev_ref, own_ref, *rest):
        refs, (back_ref, grad_ref, sums_ref, whole, acc, sem) = rest[:n], rest[n:]
        k = pl.program_id(0)

        @pl.when(k == 0)
        def _():
            start_loads(lay, pos_ref, refs, 0, 3 * width, whole, sem)
            acc[...] = jnp.zeros_like(acc)

        wait_load(k, 3 * width, whole, sem)
        start = k * (3 * width)
        part = jnp.concatenate([dk_ref[0, :rows], dv_ref[0, :rows]], axis=1)
        acc[:rows] += dot_nt(part, whole[:, pl.ds(aligned(start + width, width), 2 * width)])
        part = jnp.concatenate([dq_ref[0], dk_ref[0, rows:], dv_ref[0, rows:]], axis=1)
        acc[rows:] += dot_nt(part, whole[:, pl.ds(aligned(start, width), 3 * width)])

        @pl.when(k == blocks - 1)
        def _():
            back = acc[:rows]
            grad = acc[rows:]
            back_ref[...] = back.astype(BF)
            grad_ref[...] = grad
            unit_prev = norm_parts(prev_ref[...].astype(F32))[0]
            unit = norm_parts(own_ref[...].astype(F32))[0]
            sums_ref[0:1] = jnp.sum(back * unit_prev + grad * unit, axis=0, keepdims=True)
            sums_ref[1:2] = jnp.sum(back + grad, axis=0, keepdims=True)

    return kernel_call(
        body,
        pos,
        (blocks,),
        (dq, dk, dv, prev, own, *weights),
        [at_lead(rows, width), at_lead(2 * rows, width), at_lead(2 * rows, width)]
        + [full((rows, dim))] * 2
        + [ANY] * n,
        [shape((rows, dim), BF), shape((rows, dim), F32), shape((2, dim), F32)],
        [full((rows, dim)), full((rows, dim)), full((2, dim))],
        [
            pltpu.VMEM((dim, blocks * 3 * width), BF),
            pltpu.VMEM((2 * rows, dim), F32),
            pltpu.SemaphoreType.DMA((blocks,)),
        ],
        2 * dim * blocks * width * rows * 5,
        16 * MIB,
    )


def spans(lay):
    tops = [dy * 2 * lay.nz * lay.a for dy in range(lay.ny + 1)]
    lows = [tops[-1] + dx * lay.nz * lay.ny * lay.b for dx in range(3)]
    return tops, lows


def half_grad_call(lay, pos, half, columns, lefts, tile, operands, specs, received, flops):
    tops, lows = spans(lay)
    ny, nz, a, b = lay.ny, lay.nz, lay.a, lay.b
    n = len(operands)

    def body(pos_ref, *refs):
        ins, rest = refs[:n], refs[n:]
        got, rest = (rest[0], rest[1:]) if half == 0 else (None, rest)
        outs, scratch = rest[: ny + 2] if half == 0 else rest[:1], rest[(ny + 2) if half == 0 else 1 :]
        turned = []
        for index, ref in zip(lefts, scratch):
            ref[...] = ins[index][...].T
            turned.append(ref)

        def column(dz, dx):
            k = lay.col_block(pos_ref, dz, dx)
            for dy in range(ny):
                start = aligned(lay.row_block(pos_ref, dy, half) * lay.rows, lay.rows)
                left = [ref[pl.ds(start, lay.rows)] for ref in turned]
                block = tile(left, ins, k)
                top_at = aligned(tops[dy] + (dx * nz + dz) * a, 16)
                low_at = aligned(lows[dx] + (dz * ny + dy) * b, 16)
                if half == 0:
                    top = block[:a] + got[pl.ds(top_at, a)].astype(F32)
                    low = block[a:] + got[pl.ds(low_at, b)].astype(F32)
                    outs[dy][dx, dz] = top.astype(BF)
                    outs[ny + dx][dz, dy] = low.astype(BF)
                else:
                    outs[0][pl.ds(top_at, a)] = block[:a].astype(BF)
                    outs[0][pl.ds(low_at, b)] = block[a:].astype(BF)

        def step(dz, carry):
            for dx in range(2):
                column(dz, dx)
            return carry

        lax.fori_loop(0, nz, step, 0)

    total = lows[2]
    if half == 0:
        operands = (*operands, received)
        specs = specs + [full((total, columns))]
        outs = [shape((2, nz, a, columns), BF)] * ny + [shape((nz, ny, b, columns), BF)] * 2
        out_specs = [full(o.shape) for o in outs]
    else:
        outs = [shape((total, columns), BF)]
        out_specs = [full((total, columns))]
    scratch = [
        pltpu.VMEM((operands[index].shape[1], operands[index].shape[0]), BF) for index in lefts
    ]
    return kernel_call(
        body, pos, (), operands, specs, outs, out_specs, scratch, flops, 12 * MIB
    )


def sum_call(pos, groups, outs, build):
    flat = [r for g in groups for r in g]

    def body(pos_ref, *refs):
        ins, given = refs[: len(flat)], refs[len(flat) :]
        at, sums = 0, []
        for g in groups:
            mine = ins[at : at + len(g)]
            at += len(g)
            sums.append(lambda index, mine=mine: sum(
                (r[index].astype(F32) for r in mine[1:]), mine[0][index].astype(F32)
            ))
        build(sums, given)

    moved = sum(2 * r.size for r in flat) + sum(2 * o.size for o in outs)
    return kernel_call(
        body, pos, (), flat, [full(r.shape) for r in flat], outs, [full(o.shape) for o in outs], [],
        moved, moved,
    )


def scatter_group(lay, pos, parts, columns):
    ny, nz, a, b = lay.ny, lay.nz, lay.a, lay.b
    tops, lows = parts[:ny], parts[ny:]
    tops = [tops[0]] + [deliver(tops[s], "fy", ny, s) for s in range(1, ny)]
    lows = [lows[0], deliver(lows[1], "tx", 2, 1)]

    def build(sums, given):
        for dx in range(2):
            given[dx][...] = sums[0](dx).astype(BF)
        for dz in range(nz):
            given[2 + dz][...] = sums[1](dz).astype(BF)

    out = sum_call(
        pos, [tops, lows],
        [shape((nz, a, columns), BF)] * 2 + [shape((ny, b, columns), BF)] * nz, build,
    )
    tops = [out[0], deliver(out[1], "tx", 2, 1)]
    lows = [out[2]] + [deliver(out[2 + s], "tz", nz, s) for s in range(1, nz)]

    def build(sums, given):
        for dz in range(nz):
            given[dz][...] = sums[0](dz).astype(BF)
        for dy in range(ny):
            given[nz + dy][...] = sums[1](dy).astype(BF)

    out = sum_call(
        pos, [tops, lows],
        [shape((a, columns), BF)] * nz + [shape((b, columns), BF)] * ny, build,
    )
    tops = [out[0]] + [deliver(out[s], "tz", nz, s) for s in range(1, nz)]
    lows = [out[nz]] + [deliver(out[nz + s], "fy", ny, s) for s in range(1, ny)]

    def build(sums, given):
        given[0][:a] = sums[0](slice(None))
        given[0][a:] = sums[1](slice(None))

    return sum_call(pos, [tops, lows], [shape((a + b, columns), F32)], build)[0]


def weight_grad(lay, pos, columns, lefts, tile, operands, specs, flops):
    away = half_grad_call(lay, pos, 1, columns, lefts, tile, operands, specs, None, flops)[0]
    received = fetch(away, "c", 2, 1)
    parts = half_grad_call(lay, pos, 0, columns, lefts, tile, operands, specs, received, flops)
    return scatter_group(lay, pos, parts, columns)


def per_device(
    sizes,
    tokens,
    segment_ids,
    w_qkv,
    b_qv,
    w_out,
    b_out,
    w_up,
    b_up,
    w_down,
    b_down,
    ln1_gain,
    ln1_shift,
    ln2_gain,
    ln2_shift,
    grad_out,
):
    ny, nz = sizes
    rows, dim = tokens.shape
    length = segment_ids.shape[1]
    width = w_qkv.shape[2]
    hidden = w_up.shape[1]
    lay = Layout(ny, nz, w_qkv.shape[0])
    axes = ("fy", "c", "tz", "tx")
    pos = jnp.stack([lax.axis_index(axis) for axis in axes]).astype(jnp.int32)
    row = lambda v: v.reshape(1, -1)

    tokens_prev = lax.ppermute(tokens, "tx", [(0, 1)])
    qkv_parts = gather_group(lay, w_qkv.reshape(lay.rows, 3 * width))
    up_shard, tied = lax.optimization_barrier(
        (jnp.concatenate([w_up, w_out], axis=1), tokens_prev)
    )
    up_parts = gather_group(lay, up_shard)
    down_parts = gather_group(lay, w_down)

    tp_index = pos[2] * 2 + pos[3]
    sequence = tp_index // 2
    later = pos[3] > 0
    ids = lax.dynamic_slice_in_dim(segment_ids, sequence, 1, 0)
    seg_q = jnp.where(later, ids[:, rows:], ids[:, :rows])
    seg_prev = jnp.where(later, ids[:, :rows], -1)
    seg_k = jnp.concatenate([seg_prev, seg_q], axis=1).reshape(length, 1)

    both = jnp.concatenate([tokens_prev, tokens], axis=0).astype(F32)
    first = (norm_parts(both)[0] * ln1_gain + ln1_shift).astype(BF)
    query, key, value = qkv_call(lay, pos, first, b_qv[0:1], b_qv[1:2], qkv_parts, width)
    mixed, lse = attend_call(pos, query, key, value, seg_k, seg_q)
    middle, second = branch_call(
        lay, pos, mixed, tokens, row(b_out), row(ln2_gain), row(ln2_shift), up_parts, hidden, width
    )
    gelu, slope = up_call(lay, pos, second, row(b_up), up_parts, hidden)

    whole = lambda v: full(v.shape)
    block = lambda ref, k, size: ref[:, pl.ds(aligned(k * size, size), size)]

    def down_tile(left, ins, k):
        return dot(left[0], block(ins[1], k, hidden))

    grad_w_down = weight_grad(
        lay, pos, hidden, (0,), down_tile, (grad_out, gelu), [whole(grad_out), whole(gelu)],
        rows * dim * gelu.shape[1],
    )

    pre, grad_b_up, result, middle_grad, middle_low, sums2 = ffn_back_call(
        lay, pos, gelu, slope, grad_out, middle, row(b_down), row(ln2_gain), down_parts, up_parts, hidden
    )

    def up_tile(left, ins, k):
        return jnp.concatenate(
            [dot(left[0], block(ins[1], k, hidden)), dot(left[1], block(ins[3], k, width))], axis=1
        )

    grad_up_out = weight_grad(
        lay, pos, hidden + width, (0, 2), up_tile, (second, pre, middle_low, mixed),
        [whole(second), whole(pre), whole(middle_low), whole(mixed)],
        rows * dim * (gelu.shape[1] + dim),
    )

    mixed_grad = mixed_grad_call(lay, pos, middle_low, up_parts, hidden, width)
    dq, dk, dv, sums_qv = attend_back_call(pos, query, key, value, seg_k, seg_q, lse, mixed_grad)

    def qkv_tile(left, ins, k):
        late = left[0][:, rows:]
        return jnp.concatenate(
            [dot(late, ins[1][k]), dot(left[0], ins[2][k]), dot(left[0], ins[3][k])], axis=1
        )

    back, first_grad, sums1 = first_grad_call(
        lay, pos, dq, dk, dv, tokens_prev, tokens, qkv_parts, width
    )
    grad_qkv = weight_grad(
        lay, pos, 3 * width, (0,), qkv_tile, (first, dq, dk, dv),
        [whole(first), whole(dq), whole(dk), whole(dv)],
        rows * dim * dim * 5,
    )

    first_grad = first_grad + lax.ppermute(back, "tx", [(1, 0)]).astype(F32)
    unit, inverse = norm_parts(tokens.astype(F32))
    token_grad = (middle_grad + norm_backward(first_grad, unit, inverse, ln1_gain)).astype(BF)

    early = lax.psum(jnp.concatenate([sums2.reshape(-1), grad_b_up.reshape(-1)]), axes)
    late = lax.psum(jnp.concatenate([sums1.reshape(-1), sums_qv.reshape(-1)]), axes)
    return (
        result,
        token_grad,
        grad_qkv.reshape(lay.rows, 3, width),
        late[2 * dim :].reshape(2, -1),
        grad_up_out[:, hidden:],
        early[2 * dim : 3 * dim],
        grad_up_out[:, :hidden],
        early[4 * dim :],
        grad_w_down,
        early[3 * dim : 4 * dim],
        late[:dim],
        late[dim : 2 * dim],
        early[:dim],
        early[dim : 2 * dim],
    )


def solution(mesh):
    n_fsdp, n_tp = mesh.devices.shape
    fine = Mesh(
        mesh.devices.reshape(n_fsdp // 2, 2, n_tp // 2, 2), ("fy", "c", "tz", "tx")
    )
    fsdp, tp, every = ("fy", "c"), ("tz", "tx"), ("fy", "c", "tz", "tx")
    tile = P(fsdp, tp)
    ins = (
        P(every, None),
        P(fsdp, None),
        P(fsdp, None, tp),
        P(),
        tile,
        P(),
        tile,
        P(),
        tile,
        P(),
        P(),
        P(),
        P(),
        P(),
        P(every, None),
    )
    outs = (
        P(every, None),
        P(every, None),
        P(fsdp, None, tp),
        P(),
        tile,
        P(),
        tile,
        P(),
        tile,
        P(),
        P(),
        P(),
        P(),
        P(),
    )
    return jax.shard_map(
        functools.partial(per_device, (n_fsdp // 2, n_tp // 2)),
        mesh=fine,
        in_specs=ins,
        out_specs=outs,
        check_vma=False,
    )
```

time: 1720 us -> 627 us (0.36)
  waiting for transfers between devices: 1320 us -> 145 us
  Pallas kernels: 0 us -> 238 us
  matrix products: 180 us -> 0 us
  starting transfers between devices: 1.18 us -> 137 us
  local copies, waits for them, and re-layouts: 67.4 us -> 17.1 us
  other arithmetic: 56.4 us -> 20 us
    reduce_scatter x8 -> x0, waiting for transfers between devices: 856 us -> none  [the longest x1 280 us: per_device(): lax.psum_scatter(branch_part, 'tp', scatter_dimension=0, tiled=True)]
    all_gather x6 -> x0, waiting for transfers between devices: 467 us -> none  [the longest x1 127 us: per_device(): grad_all = lax.all_gather(grad_out, 'tp', axis=0, tiled=True)]
    pallas_call x0 -> x23, Pallas kernels: none -> 238 us  [kernel_call(): pl.pallas_call(body, out_shape=outs, grid_spec=pltpu.PrefetchScalarGridSp...]
    dot_general x40 -> x0, matrix products: 180 us -> none  [the longest x4 15.7 us: attend_backward(): jnp.einsum('qhd,khd->hqk', mixed_grad, value, preferred_element_type=jnp....]
    ppermute x0 -> x77, waiting for transfers between devices: none -> 145 us  [the longest x45 86.6 us: fetch(): lax.ppermute(value, axis, [(s, (s - shift) % size) for s in range(size)])]
    ppermute x0 -> x77, starting transfers between devices: none -> 137 us  [the longest x45 65.6 us: fetch(): lax.ppermute(value, axis, [(s, (s - shift) % size) for s in range(size)])]
    reduce_sum x12 -> x5, other arithmetic: 25.1 us -> 3.68 us  [the longest x1 2.02 us: norm_backward(): jnp.mean(scaled, axis=-1, keepdims=True)]
    another operation x11 -> x6, local copies, waits for them, and re-layouts: 21.9 us -> 1.16 us  [the longest x3 1 us: gather_group(): low = jnp.stack(around(low, 'fy', lay.ny))]
  transfers between devices with their start and end apart: 14 -> 77, of which waited for: 10 -> 20; matrix products, arithmetic and copies ran while one was open for 11% -> 5% of each run, Pallas kernels for 0% -> 32%
where the time goes in v1:
time: 627 us; the launch traced here: 618 us
  Pallas kernels  238 us (38%)
  waiting for transfers between devices  145 us (23%)
  starting transfers between devices  137 us (22%)
  blocking collectives  59.1 us (9%)
  other arithmetic  20 us (3%)
  local copies, waits for them, and re-layouts  17.1 us (3%)
    pallas_call x23, Pallas kernels, kernel_call(): pl.pallas_call(body, out_shape=outs, grid_spec=pltpu.PrefetchScalarGridSp...  238 us
    ppermute x45, waiting for transfers between devices, fetch(): lax.ppermute(value, axis, [(s, (s - shift) % size) for s in range(size)])  86.6 us
    ppermute x45, starting transfers between devices, fetch(): lax.ppermute(value, axis, [(s, (s - shift) % size) for s in range(size)])  65.6 us
    ppermute x30, starting transfers between devices, deliver(): lax.ppermute(value, axis, [(s, (s + shift) % size) for s in range(size)])  65.2 us
    psum x1, blocking collectives, per_device(): lax.psum(jnp.concatenate([sums1.reshape(-1), sums_qv.reshape(-1)]), axes)  59.1 us
    ppermute x30, waiting for transfers between devices, deliver(): lax.ppermute(value, axis, [(s, (s + shift) % size) for s in range(size)])  45.8 us
  transfers between devices with their start and end apart: 77, of which 20 were waited for; matrix products, arithmetic and copies ran while one was open for 5% of the time, Pallas kernels for 32%

profile of v1, /device:TPU:0, one launch (start us, length us, event | category | flops | bytes accessed | tf_op | source)
XLA Modules:
  0.0 617.6 jit_solution(7583382586641721178)
XLA Ops:
  0.7 5.0 collective-permute-start
  16.1 12.3 %collective-permute-done.prev_ref = bf16[512,1024]{1,0:T(8,128)(2,1)S(1)} collective-permute-done((bf16[512,1024]{1,0:T(8,128)(2,1)}, bf16[512,1024]{1,0:T(8,128)(2,1)S(1)}, u32[]{:S(2)}, u32[]{:S(2)}) %collective-permute-start) | collective-permute-done | bytes 1048608 | tf_op jit(solution)/shard_map/ppermute | solution.py:683
  42.6 7.8 %collective-permute-done.30 = bf16[160,512]{1,0:T(8,128)(2,1)S(1)} collective-permute-done((bf16[160,512]{1,0:T(8,128)(2,1)S(1)}, bf16[160,512]{1,0:T(8,128)(2,1)S(1)}, u32[]{:S(2)}, u32[]{:S(2)}) %collective-permute-start.30) | collective-permute-done | bytes 163872 | tf_op jit(solution)/shard_map/ppermute | solution.py:44
  50.3 8.0 %collective-permute-start.8 = (bf16[2,96,384]{2,1,0:T(8,128)(2,1)S(1)}, bf16[2,96,384]{2,1,0:T(8,128)(2,1)S(1)}, u32[]{:S(2)}, u32[]{:S(2)}) collective-permute-start(bf16[2,96,384]{2,1,0:T(8,128)(2,1)S(1)} %get-tuple-element.211), channel_id=1, source_target_pairs={{0,4},{2,6},{4,0},{6,2},{1,5},{3,7},{5,1},{7,3},{8,12},{10,14},{12... | collective-permute-start | bytes 442376 | tf_op jit(solution)/shard_map/ppermute | solution.py:44
  62.3 5.0 collective-permute-done.16
  77.2 5.4 collective-permute-done.8
  82.6 4.0 collective-permute-start.35
  101.3 19.5 %collective-permute-done.10.rest_3_ = bf16[4,2,96,384]{3,2,1,0:T(8,128)(2,1)S(1)} collective-permute-done((bf16[4,2,96,384]{3,2,1,0:T(8,128)(2,1)S(1)}, bf16[4,2,96,384]{3,2,1,0:T(8,128)(2,1)S(1)}, u32[]{:S(2)}, u32[]{:S(2)}) %collective-permute-start.10) | collective-permute-done | bytes 589856 | tf_op jit(solution)/shard_map/ppermute | solution.py:44
  124.3 10.1 %collective-permute-done.32 = bf16[4,160,512]{2,1,0:T(8,128)(2,1)S(1)} collective-permute-done((bf16[4,160,512]{2,1,0:T(8,128)(2,1)S(1)}, bf16[4,160,512]{2,1,0:T(8,128)(2,1)S(1)}, u32[]{:S(2)}, u32[]{:S(2)}) %collective-permute-start.32) | collective-permute-done | bytes 655392 | tf_op jit(solution)/shard_map/ppermute | solution.py:44
  139.6 4.7 collective-permute-done.22
  157.7 14.5 %collective-permute-done.24.rest_3_.rest_11_ = bf16[4,2,96,640]{3,2,1,0:T(8,128)(2,1)} collective-permute-done((bf16[4,2,96,640]{3,2,1,0:T(8,128)(2,1)}, bf16[4,2,96,640]{3,2,1,0:T(8,128)(2,1)}, u32[]{:S(2)}, u32[]{:S(2)}) %collective-permute-start.24) | collective-permute-done | bytes 983072 | tf_op jit(solution)/shard_map/ppermute | solution.py:44
  178.6 13.7 %shard_map.254 = (bf16[8,512,128]{2,1,0:T(8,128)(2,1)}, bf16[8,1024,128]{2,1,0:T(8,128)(2,1)}, bf16[8,1024,128]{2,1,0:T(8,128)(2,1)}) custom-call(s32[4]{0:T(128)} %pad_add_fusion.pos_ref, bf16[1024,1024]{1,0:T(8,128)(2,1)} %fusion.5.first_ref.refs_0_, f32[1,1024]{1,0:T(1,128)} %get-tuple-element.221.bq_ref, f32[1,1024]{1,0:T(1,128)} %get-tuple-element.220.bv_ref, ...), custom_call_target="tpu_custom_call" | custom-call | flops 5368709120 | bytes 14680064 | tf_op jit(solution)/shard_map/pallas_call | solution.py:92
  196.2 25.1 %shard_map.255 = (bf16[512,1024]{1,0:T(8,128)(2,1)}, f32[8,2,512]{2,1,0:T(2,128)}) custom-call(s32[4]{0:T(128)} %pad_add_fusion.pos_ref, bf16[8,512,128]{2,1,0:T(8,128)(2,1)} %get-tuple-element.85.q_ref, bf16[8,1024,128]{2,1,0:T(8,128)(2,1)} %get-tuple-element.86.k_ref, bf16[8,1024,128]{2,1,0:T(8,128)(2,1)} %get-tuple-element.87.v_ref, ...), custom_call_target="tpu_custom_call" | custom-call | flops 8589934592 | bytes 8388608 | tf_op jit(solution)/shard_map/pallas_call | solution.py:92
  221.3 6.9 %shard_map.256 = (f32[512,1024]{1,0:T(8,128)}, bf16[512,1024]{1,0:T(8,128)(2,1)}) custom-call(s32[4]{0:T(128)} %pad_add_fusion.pos_ref, bf16[512,1024]{1,0:T(8,128)(2,1)} %get-tuple-element.88.mixed_ref.refs_3_, bf16[512,1024]{1,0:T(8,128)(2,1)} %own_ref.1, f32[1,1024]{1,0:T(1,128)} %bitcast.108, f32[1,1024]{1,0:T(1,128)} %bitcast.110, f32[1,1024]{1,0:T(1,128)} %bitcast.109, ...), custom_call_target="tpu_custom_call" | custom-call | flops 1073741824 | bytes 7340032 | tf_op jit(solution)/shard_map/pallas_call | solution.py:92
  228.2 15.3 %shard_map.257 = (bf16[512,4096]{1,0:T(8,128)(2,1)}, bf16[512,4096]{1,0:T(8,128)(2,1)}) custom-call(s32[4]{0:T(128)} %pad_add_fusion.pos_ref, bf16[512,1024]{1,0:T(8,128)(2,1)} %get-tuple-element.90.second_ref.refs_0_, f32[1,4096]{1,0:T(1,128)} %bitcast.112, bf16[2,4,160,640]{3,2,1,0:T(8,128)(2,1)} %copy-done.3, ...), custom_call_target="tpu_custom_call" | custom-call | flops 4294967296 | bytes 17825792 | tf_op jit(solution)/shard_map/pallas_call | solution.py:92
  243.5 8.3 %shard_map.272 = bf16[4096,512]{1,0:T(8,128)(2,1)} custom-call(s32[4]{0:T(128)} %pad_add_fusion.pos_ref, bf16[512,1024]{1,0:T(8,128)(2,1)} %refs_0_.3, bf16[512,4096]{1,0:T(8,128)(2,1)} %get-tuple-element.91.gelu_ref.refs_1_), custom_call_target="tpu_custom_call" | custom-call | flops 2147483648 | bytes 12582912 | tf_op jit(solution)/shard_map/pallas_call | solution.py:92
  253.4 28.2 %shard_map.258 = (bf16[512,4096]{1,0:T(8,128)(2,1)}, f32[1,4096]{1,0:T(1,128)}, bf16[512,1024]{1,0:T(8,128)(2,1)}, f32[512,1024]{1,0:T(8,128)}, bf16[512,1024]{1,0:T(8,128)(2,1)}, /*index=5*/f32[4,1024]{1,0:T(4,128)}) custom-call(s32[4]{0:T(128)} %pad_add_fusion.pos_ref, bf16[512,4096]{1,0:T(8,128)(2,1)} %get-tuple-element.91.gelu_ref.refs_1_, ...), custom_call_target="tpu_custom_call" | custom-call | flops 12884901888 | bytes 37748736 | tf_op jit(solution)/shard_map/pallas_call | solution.py:92
  281.6 10.7 %shard_map.267 = bf16[4096,640]{1,0:T(8,128)(2,1)} custom-call(s32[4]{0:T(128)} %pad_add_fusion.pos_ref, bf16[512,1024]{1,0:T(8,128)(2,1)} %get-tuple-element.90.second_ref.refs_0_, bf16[512,4096]{1,0:T(8,128)(2,1)} %get-tuple-element.121.refs_1_, bf16[512,1024]{1,0:T(8,128)(2,1)} %get-tuple-element.97.low_ref.refs_2_, ...), custom_call_target="tpu_custom_call" | custom-call | flops 2684354560 | bytes 12582912 | tf_op jit(solution)/shard_map/pallas_call | solution.py:92
  292.8 5.8 shard_map.259.grad_ref
  298.6 29.5 %shard_map.260 = (bf16[8,512,128]{2,1,0:T(8,128)(2,1)}, bf16[8,1024,128]{2,1,0:T(8,128)(2,1)}, bf16[8,1024,128]{2,1,0:T(8,128)(2,1)}, f32[2,1024]{1,0:T(2,128)}) custom-call(s32[4]{0:T(128)} %pad_add_fusion.pos_ref, bf16[8,512,128]{2,1,0:T(8,128)(2,1)} %get-tuple-element.85.q_ref, bf16[8,1024,128]{2,1,0:T(8,128)(2,1)} %get-tuple-element.86.k_ref, ...), custom_call_target="tpu_custom_call" | custom-call | flops 17179869184 | bytes 12582912 | tf_op jit(solution)/shard_map/pallas_call | solution.py:92
  328.0 12.7 %shard_map.262 = bf16[4096,384]{1,0:T(8,128)(2,1)} custom-call(s32[4]{0:T(128)} %pad_add_fusion.pos_ref, bf16[1024,1024]{1,0:T(8,128)(2,1)} %fusion.5.first_ref.refs_0_, bf16[8,512,128]{2,1,0:T(8,128)(2,1)} %get-tuple-element.98.dq_ref.refs_1_, bf16[8,1024,128]{2,1,0:T(8,128)(2,1)} %get-tuple-element.99.dk_ref.refs_2_, ...), custom_call_target="tpu_custom_call" | custom-call | flops 2684354560 | bytes 12582912 | tf_op jit(solution)/shard_map/pallas_call | solution.py:92
  340.8 5.9 collective-permute-done.44.refs_4_
  346.7 12.8 %shard_map.263 = (bf16[2,4,160,384]{3,2,1,0:T(8,128)(2,1)}, bf16[2,4,160,384]{3,2,1,0:T(8,128)(2,1)}, bf16[4,2,96,384]{3,2,1,0:T(8,128)(2,1)}, bf16[4,2,96,384]{3,2,1,0:T(8,128)(2,1)}) custom-call(s32[4]{0:T(128)} %pad_add_fusion.pos_ref, bf16[1024,1024]{1,0:T(8,128)(2,1)} %fusion.5.first_ref.refs_0_, bf16[8,512,128]{2,1,0:T(8,128)(2,1)} %get-tuple-element.98.dq_ref.refs_1_, ...), custom_call_target="tpu_custom_call" | custom-call | flops 2684354560 | bytes 12582912 | tf_op jit(solution)/shard_map/pallas_call | solution.py:92
  363.1 12.1 %shard_map.268 = (bf16[2,4,160,640]{3,2,1,0:T(8,128)(2,1)}, bf16[2,4,160,640]{3,2,1,0:T(8,128)(2,1)}, bf16[4,2,96,640]{3,2,1,0:T(8,128)(2,1)}, bf16[4,2,96,640]{3,2,1,0:T(8,128)(2,1)}) custom-call(s32[4]{0:T(128)} %pad_add_fusion.pos_ref, bf16[512,1024]{1,0:T(8,128)(2,1)} %get-tuple-element.90.second_ref.refs_0_, ...), custom_call_target="tpu_custom_call" | custom-call | flops 2684354560 | bytes 12582912 | tf_op jit(solution)/shard_map/pallas_call | solution.py:92
  375.7 9.5 %shard_map.273 = (bf16[2,4,160,512]{3,2,1,0:T(8,128)(2,1)}, bf16[2,4,160,512]{3,2,1,0:T(8,128)(2,1)}, bf16[4,2,96,512]{3,2,1,0:T(8,128)(2,1)}, bf16[4,2,96,512]{3,2,1,0:T(8,128)(2,1)}) custom-call(s32[4]{0:T(128)} %pad_add_fusion.pos_ref, bf16[512,1024]{1,0:T(8,128)(2,1)} %refs_0_.3, bf16[512,4096]{1,0:T(8,128)(2,1)} %get-tuple-element.91.gelu_ref.refs_1_, ...), custom_call_target="tpu_custom_call" | custom-call | flops 2147483648 | bytes 12582912 | tf_op jit(solution)/shard_map/pallas_call | solution.py:92
  394.3 16.7 %shard_map.261 = (bf16[512,1024]{1,0:T(8,128)(2,1)}, f32[512,1024]{1,0:T(8,128)}, f32[2,1024]{1,0:T(2,128)}) custom-call(s32[4]{0:T(128)} %pad_add_fusion.pos_ref, bf16[8,512,128]{2,1,0:T(8,128)(2,1)} %get-tuple-element.98.dq_ref.refs_1_, bf16[8,1024,128]{2,1,0:T(8,128)(2,1)} %get-tuple-element.99.dk_ref.refs_2_, ...), custom_call_target="tpu_custom_call" | custom-call | flops 5368709120 | bytes 16777216 | tf_op jit(solution)/shard_map/pallas_call | solution.py:92
  416.4 30.3 %collective-permute-done.67.refs_1_ = bf16[2,4,160,512]{3,2,1,0:T(8,128)(2,1)S(1)} collective-permute-done((bf16[2,4,160,512]{3,2,1,0:T(8,128)(2,1)}, bf16[2,4,160,512]{3,2,1,0:T(8,128)(2,1)S(1)}, u32[]{:S(2)}, u32[]{:S(2)}) %collective-permute-start.67) | collective-permute-done | bytes 1310752 | tf_op jit(solution)/shard_map/ppermute | solution.py:48
  448.9 4.5 shard_map.274
  457.9 5.0 shard_map.269
  464.1 59.1 %all-reduce = (f32[4096]{0:T(1024)S(1)}, f32[8192]{0:T(1024)S(1)}) all-reduce(f32[4096]{0:T(1024)S(1)} %pad_maximum_fusion.15, f32[8192]{0:T(1024)S(1)} %pad_maximum_fusion.14), channel_id=1, replica_groups=mesh['fy'=2,'c'=2,'tz'=4,'tx'=2] {'fy','c','tz','tx'}, use_global_device_ids=true, to_apply=%region_6.7 | all-reduce | flops 12288 | bytes 98304 | tf_op jit(solution)/shard_map/psum | solution.py:757
  540.9 7.1 %collective-permute-start.51 = (bf16[160,384]{1,0:T(8,128)(2,1)}, bf16[160,384]{1,0:T(8,128)(2,1)S(1)}, u32[]{:S(2)}, u32[]{:S(2)}) collective-permute-start(bf16[160,384]{1,0:T(8,128)(2,1)} %get-tuple-element.114), channel_id=1, source_target_pairs={{0,2},{2,4},{4,6},{6,0},{1,3},{3,5},{5,7},{7,1},{8,10},{10,12},{12... | collective-permute-start | bytes 368648 | tf_op jit(solution)/shard_map/ppermute | solution.py:48
  570.0 9.6 %collective-permute-start.73 = (bf16[160,512]{1,0:T(8,128)(2,1)}, bf16[160,512]{1,0:T(8,128)(2,1)}, u32[]{:S(2)}, u32[]{:S(2)}) collective-permute-start(bf16[160,512]{1,0:T(8,128)(2,1)} %get-tuple-element.151), channel_id=1, source_target_pairs={{0,2},{2,4},{4,6},{6,0},{1,3},{3,5},{5,7},{7,1},{8,10},{10,12},{12... | collective-permute-start | bytes 491528 | tf_op jit(solution)/shard_map/ppermute | solution.py:48
  (285 shorter events, 191.0 us)
Async XLA Ops:
  0.7 27.7 %collective-permute-start = (bf16[512,1024]{1,0:T(8,128)(2,1)}, bf16[512,1024]{1,0:T(8,128)(2,1)S(1)}, u32[]{:S(2)}, u32[]{:S(2)}) collective-permute-start(bf16[512,1024]{1,0:T(8,128)(2,1)} %own_ref.1), channel_id=1, source_target_pairs={{0,1},{2,3},{4,5},{6,7},{8,9},{10,11},{12,13},{14,15},{16,17},{18,... | collective-permute-start | bytes 3145736 | tf_op jit(solution)/shard_map/ppermute | solution.py:683
  6.7 30.5 %collective-permute-start.3 = (bf16[160,384]{1,0:T(8,128)(2,1)S(1)}, bf16[160,384]{1,0:T(8,128)(2,1)S(1)}, u32[]{:S(2)}, u32[]{:S(2)}) collective-permute-start(bf16[160,384]{1,0:T(8,128)(2,1)S(1)} %bitcast.96), channel_id=1, source_target_pairs={{0,2},{2,4},{4,6},{6,0},{1,3},{3,5},{5,7},{7,1},{8,10},{10,12},{12... | collective-permute-start | bytes 368648 | tf_op jit(solution)/shard_map/ppermute | solution.py:44
  8.3 30.2 %collective-permute-start.2 = (bf16[160,384]{1,0:T(8,128)(2,1)S(1)}, bf16[160,384]{1,0:T(8,128)(2,1)S(1)}, u32[]{:S(2)}, u32[]{:S(2)}) collective-permute-start(bf16[160,384]{1,0:T(8,128)(2,1)S(1)} %bitcast.97), channel_id=1, source_target_pairs={{0,4},{2,6},{4,0},{6,2},{1,5},{3,7},{5,1},{7,3},{8,12},{10,14},{12... | collective-permute-start | bytes 368648 | tf_op jit(solution)/shard_map/ppermute | solution.py:44
  10.9 28.3 %collective-permute-start.1 = (bf16[160,384]{1,0:T(8,128)(2,1)S(1)}, bf16[160,384]{1,0:T(8,128)(2,1)S(1)}, u32[]{:S(2)}, u32[]{:S(2)}) collective-permute-start(bf16[160,384]{1,0:T(8,128)(2,1)S(1)} %bitcast.98), channel_id=1, source_target_pairs={{0,6},{2,0},{4,2},{6,4},{1,7},{3,1},{5,3},{7,5},{8,14},{10,8},{12,... | collective-permute-start | bytes 368648 | tf_op jit(solution)/shard_map/ppermute | solution.py:44
  39.2 28.1 %collective-permute-start.16 = (bf16[160,640]{1,0:T(8,128)(2,1)S(1)}, bf16[160,640]{1,0:T(8,128)(2,1)S(1)}, u32[]{:S(2)}, u32[]{:S(2)}) collective-permute-start(bf16[160,640]{1,0:T(8,128)(2,1)S(1)} %get-tuple-element.197), channel_id=1, source_target_pairs={{0,4},{2,6},{4,0},{6,2},{1,5},{3,7},{5,1},{7,3},{8,12},{10,14},{12... | collective-permute-start | bytes 614408 | tf_op jit(solution)/shard_map/ppermute | solution.py:44
  39.6 31.5 %collective-permute-start.15 = (bf16[160,640]{1,0:T(8,128)(2,1)S(1)}, bf16[160,640]{1,0:T(8,128)(2,1)S(1)}, u32[]{:S(2)}, u32[]{:S(2)}) collective-permute-start(bf16[160,640]{1,0:T(8,128)(2,1)S(1)} %get-tuple-element.197), channel_id=1, source_target_pairs={{0,6},{2,0},{4,2},{6,4},{1,7},{3,1},{5,3},{7,5},{8,14},{10,8},{12,... | collective-permute-start | bytes 614408 | tf_op jit(solution)/shard_map/ppermute | solution.py:44
  50.3 32.3 %collective-permute-start.8 = (bf16[2,96,384]{2,1,0:T(8,128)(2,1)S(1)}, bf16[2,96,384]{2,1,0:T(8,128)(2,1)S(1)}, u32[]{:S(2)}, u32[]{:S(2)}) collective-permute-start(bf16[2,96,384]{2,1,0:T(8,128)(2,1)S(1)} %get-tuple-element.211), channel_id=1, source_target_pairs={{0,4},{2,6},{4,0},{6,2},{1,5},{3,7},{5,1},{7,3},{8,12},{10,14},{12... | collective-permute-start | bytes 442376 | tf_op jit(solution)/shard_map/ppermute | solution.py:44
  58.3 28.3 %collective-permute-start.7 = (bf16[2,96,384]{2,1,0:T(8,128)(2,1)S(1)}, bf16[2,96,384]{2,1,0:T(8,128)(2,1)S(1)}, u32[]{:S(2)}, u32[]{:S(2)}) collective-permute-start(bf16[2,96,384]{2,1,0:T(8,128)(2,1)S(1)} %get-tuple-element.211), channel_id=1, source_target_pairs={{0,6},{2,0},{4,2},{6,4},{1,7},{3,1},{5,3},{7,5},{8,14},{10,8},{12,... | collective-permute-start | bytes 442376 | tf_op jit(solution)/shard_map/ppermute | solution.py:44
  86.6 47.7 %collective-permute-start.18 = (bf16[4,160,640]{2,1,0:T(8,128)(2,1)S(1)}, bf16[4,160,640]{2,1,0:T(8,128)(2,1)S(1)}, u32[]{:S(2)}, u32[]{:S(2)}) collective-permute-start(bf16[4,160,640]{2,1,0:T(8,128)(2,1)S(1)} %get-tuple-element.189), channel_id=1, source_target_pairs={{0,1},{1,0},{2,3},{3,2},{4,5},{5,4},{6,7},{7,6},{8,9},{9,8},{10,11... | collective-permute-start | bytes 2457608 | tf_op jit(solution)/shard_map/ppermute | solution.py:44
  89.1 31.7 %collective-permute-start.10 = (bf16[4,2,96,384]{3,2,1,0:T(8,128)(2,1)S(1)}, bf16[4,2,96,384]{3,2,1,0:T(8,128)(2,1)S(1)}, u32[]{:S(2)}, u32[]{:S(2)}) collective-permute-start(bf16[4,2,96,384]{3,2,1,0:T(8,128)(2,1)S(1)} %pad_maximum_fusion.8.rest_2_), channel_id=1, source_target_pairs={{0,1},{1,0},{2,3},{3,2},{4,5},{5,4},{6,7},{7,6},{8,9},{9,8},{10,11... | collective-permute-start | bytes 1769480 | tf_op jit(solution)/shard_map/ppermute | solution.py:44
  90.7 43.6 %collective-permute-start.32 = (bf16[4,160,512]{2,1,0:T(8,128)(2,1)S(1)}, bf16[4,160,512]{2,1,0:T(8,128)(2,1)S(1)}, u32[]{:S(2)}, u32[]{:S(2)}) collective-permute-start(bf16[4,160,512]{2,1,0:T(8,128)(2,1)S(1)} %get-tuple-element.191), channel_id=1, source_target_pairs={{0,1},{1,0},{2,3},{3,2},{4,5},{5,4},{6,7},{7,6},{8,9},{9,8},{10,11... | collective-permute-start | bytes 1966088 | tf_op jit(solution)/shard_map/ppermute | solution.py:44
  93.1 29.1 %collective-permute-start.13 = (bf16[4,2,96,384]{3,2,1,0:T(8,128)(2,1)S(1)}, bf16[4,2,96,384]{3,2,1,0:T(8,128)(2,1)S(1)}, u32[]{:S(2)}, u32[]{:S(2)}) collective-permute-start(bf16[4,2,96,384]{3,2,1,0:T(8,128)(2,1)S(1)} %pad_maximum_fusion.8.rest_2_), channel_id=1, source_target_pairs={{0,8},{8,0},{1,9},{9,1},{2,10},{10,2},{3,11},{11,3},{4,12},{12,4},... | collective-permute-start | bytes 1769480 | tf_op jit(solution)/shard_map/ppermute | solution.py:44
  98.9 51.0 %collective-permute-start.5 = (bf16[2,4,160,384]{3,2,1,0:T(8,128)(2,1)}, bf16[2,4,160,384]{3,2,1,0:T(8,128)(2,1)}, u32[]{:S(2)}, u32[]{:S(2)}) collective-permute-start(bf16[2,4,160,384]{3,2,1,0:T(8,128)(2,1)} %pad_maximum_fusion.3.rest_0_), channel_id=1, source_target_pairs={{0,16},{16,0},{1,17},{17,1},{2,18},{18,2},{3,19},{19,3},{4,20},{20... | collective-permute-start | bytes 2949128 | tf_op jit(solution)/shard_map/ppermute | solution.py:44
  138.0 37.7 %collective-permute-start.19 = (bf16[2,4,160,640]{3,2,1,0:T(8,128)(2,1)S(1)}, bf16[2,4,160,640]{3,2,1,0:T(8,128)(2,1)}, u32[]{:S(2)}, u32[]{:S(2)}) collective-permute-start(bf16[2,4,160,640]{3,2,1,0:T(8,128)(2,1)S(1)} %pad_maximum_fusion.1.rest_0_.rest_8_), channel_id=1, source_target_pairs={{0,16},{16,0},{1,17},{17,1},{2,18},{18,2},{3,19},{19,3},{4,20},{20... | collective-permute-start | bytes 4915208 | tf_op jit(solution)/shard_map/ppermute | solution.py:44
  152.2 43.6 %collective-permute-start.25 = (bf16[2,4,160,640]{3,2,1,0:T(8,128)(2,1)S(1)}, bf16[2,4,160,640]{3,2,1,0:T(8,128)(2,1)}, u32[]{:S(2)}, u32[]{:S(2)}) collective-permute-start(bf16[2,4,160,640]{3,2,1,0:T(8,128)(2,1)S(1)} %pad_maximum_fusion.1.rest_0_.rest_8_), channel_id=1, source_target_pairs={{0,8},{8,0},{1,9},{9,1},{2,10},{10,2},{3,11},{11,3},{4,12},{12,4},... | collective-permute-start | bytes 4915208 | tf_op jit(solution)/shard_map/ppermute | solution.py:44
  155.4 39.8 %collective-permute-start.33 = (bf16[2,4,160,512]{3,2,1,0:T(8,128)(2,1)}, bf16[2,4,160,512]{3,2,1,0:T(8,128)(2,1)}, u32[]{:S(2)}, u32[]{:S(2)}) collective-permute-start(bf16[2,4,160,512]{3,2,1,0:T(8,128)(2,1)} %pad_maximum_fusion.2.rest_0_), channel_id=1, source_target_pairs={{0,16},{16,0},{1,17},{17,1},{2,18},{18,2},{3,19},{19,3},{4,20},{20... | collective-permute-start | bytes 3932168 | tf_op jit(solution)/shard_map/ppermute | solution.py:44
  175.7 45.6 %collective-permute-start.26 = (bf16[2,4,160,640]{3,2,1,0:T(8,128)(2,1)}, bf16[2,4,160,640]{3,2,1,0:T(8,128)(2,1)}, u32[]{:S(2)}, u32[]{:S(2)}) collective-permute-start(bf16[2,4,160,640]{3,2,1,0:T(8,128)(2,1)} %collective-permute-done.19.rest_1_.rest_9_), channel_id=1, source_target_pairs={{0,8},{8,0},{1,9},{9,1},{2,10},{10,2},{3,11},{11,3},{4,12},{12,4},... | collective-permute-start | bytes 4915208 | tf_op jit(solution)/shard_map/ppermute | solution.py:44
  195.2 56.7 %collective-permute-start.41 = (bf16[4,2,96,512]{3,2,1,0:T(8,128)(2,1)}, bf16[4,2,96,512]{3,2,1,0:T(8,128)(2,1)S(1)}, u32[]{:S(2)}, u32[]{:S(2)}) collective-permute-start(bf16[4,2,96,512]{3,2,1,0:T(8,128)(2,1)} %pad_maximum_fusion.6.rest_2_), channel_id=1, source_target_pairs={{0,8},{8,0},{1,9},{9,1},{2,10},{10,2},{3,11},{11,3},{4,12},{12,4},... | collective-permute-start | bytes 2359304 | tf_op jit(solution)/shard_map/ppermute | solution.py:44
  195.2 56.7 %collective-permute-start.39 = (bf16[2,4,160,512]{3,2,1,0:T(8,128)(2,1)}, bf16[2,4,160,512]{3,2,1,0:T(8,128)(2,1)}, u32[]{:S(2)}, u32[]{:S(2)}) collective-permute-start(bf16[2,4,160,512]{3,2,1,0:T(8,128)(2,1)} %pad_maximum_fusion.2.rest_0_), channel_id=1, source_target_pairs={{0,8},{8,0},{1,9},{9,1},{2,10},{10,2},{3,11},{11,3},{4,12},{12,4},... | collective-permute-start | bytes 3932168 | tf_op jit(solution)/shard_map/ppermute | solution.py:44
  195.7 56.2 %collective-permute-start.42 = (bf16[4,2,96,512]{3,2,1,0:T(8,128)(2,1)}, bf16[4,2,96,512]{3,2,1,0:T(8,128)(2,1)S(1)}, u32[]{:S(2)}, u32[]{:S(2)}) collective-permute-start(bf16[4,2,96,512]{3,2,1,0:T(8,128)(2,1)} %collective-permute-done.38.rest_3_), channel_id=1, source_target_pairs={{0,8},{8,0},{1,9},{9,1},{2,10},{10,2},{3,11},{11,3},{4,12},{12,4},... | collective-permute-start | bytes 2359304 | tf_op jit(solution)/shard_map/ppermute | solution.py:44
  195.8 56.1 %collective-permute-start.40 = (bf16[2,4,160,512]{3,2,1,0:T(8,128)(2,1)}, bf16[2,4,160,512]{3,2,1,0:T(8,128)(2,1)S(1)}, u32[]{:S(2)}, u32[]{:S(2)}) collective-permute-start(bf16[2,4,160,512]{3,2,1,0:T(8,128)(2,1)} %collective-permute-done.33.rest_1_), channel_id=1, source_target_pairs={{0,8},{8,0},{1,9},{9,1},{2,10},{10,2},{3,11},{11,3},{4,12},{12,4},... | collective-permute-start | bytes 3932168 | tf_op jit(solution)/shard_map/ppermute | solution.py:44
  292.3 70.8 %collective-permute-start.55 = (bf16[4096,640]{1,0:T(8,128)(2,1)}, bf16[4096,640]{1,0:T(8,128)(2,1)}, u32[]{:S(2)}, u32[]{:S(2)}) collective-permute-start(bf16[4096,640]{1,0:T(8,128)(2,1)} %shard_map.267), channel_id=1, source_target_pairs={{0,8},{8,0},{1,9},{9,1},{2,10},{10,2},{3,11},{11,3},{4,12},{12,4},... | collective-permute-start | bytes 15728648 | tf_op jit(solution)/shard_map/ppermute | solution.py:44
  292.3 83.3 %collective-permute-start.66 = (bf16[4096,512]{1,0:T(8,128)(2,1)}, bf16[4096,512]{1,0:T(8,128)(2,1)}, u32[]{:S(2)}, u32[]{:S(2)}) collective-permute-start(bf16[4096,512]{1,0:T(8,128)(2,1)} %shard_map.272), channel_id=1, source_target_pairs={{0,8},{8,0},{1,9},{9,1},{2,10},{10,2},{3,11},{11,3},{4,12},{12,4},... | collective-permute-start | bytes 12582920 | tf_op jit(solution)/shard_map/ppermute | solution.py:44
  359.5 27.5 %collective-permute-start.45 = (bf16[2,4,160,384]{3,2,1,0:T(8,128)(2,1)}, bf16[2,4,160,384]{3,2,1,0:T(8,128)(2,1)}, u32[]{:S(2)}, u32[]{:S(2)}) collective-permute-start(bf16[2,4,160,384]{3,2,1,0:T(8,128)(2,1)} %get-tuple-element.104), channel_id=1, source_target_pairs={{0,16},{16,0},{1,17},{17,1},{2,18},{18,2},{3,19},{19,3},{4,20},{20... | collective-permute-start | bytes 2949128 | tf_op jit(solution)/shard_map/ppermute | solution.py:48
  375.2 80.8 %collective-permute-start.56 = (bf16[2,4,160,640]{3,2,1,0:T(8,128)(2,1)}, bf16[2,4,160,640]{3,2,1,0:T(8,128)(2,1)S(1)}, u32[]{:S(2)}, u32[]{:S(2)}) collective-permute-start(bf16[2,4,160,640]{3,2,1,0:T(8,128)(2,1)} %get-tuple-element.123), channel_id=1, source_target_pairs={{0,16},{16,0},{1,17},{17,1},{2,18},{18,2},{3,19},{19,3},{4,20},{20... | collective-permute-start | bytes 4915208 | tf_op jit(solution)/shard_map/ppermute | solution.py:48
  385.2 61.6 %collective-permute-start.67 = (bf16[2,4,160,512]{3,2,1,0:T(8,128)(2,1)}, bf16[2,4,160,512]{3,2,1,0:T(8,128)(2,1)S(1)}, u32[]{:S(2)}, u32[]{:S(2)}) collective-permute-start(bf16[2,4,160,512]{3,2,1,0:T(8,128)(2,1)} %get-tuple-element.141), channel_id=1, source_target_pairs={{0,16},{16,0},{1,17},{17,1},{2,18},{18,2},{3,19},{19,3},{4,20},{20... | collective-permute-start | bytes 3932168 | tf_op jit(solution)/shard_map/ppermute | solution.py:48
  392.4 61.0 %collective-permute-start.57 = (bf16[4,2,96,640]{3,2,1,0:T(8,128)(2,1)}, bf16[4,2,96,640]{3,2,1,0:T(8,128)(2,1)}, u32[]{:S(2)}, u32[]{:S(2)}) collective-permute-start(bf16[4,2,96,640]{3,2,1,0:T(8,128)(2,1)} %get-tuple-element.125), channel_id=1, source_target_pairs={{0,1},{1,0},{2,3},{3,2},{4,5},{5,4},{6,7},{7,6},{8,9},{9,8},{10,11... | collective-permute-start | bytes 2949128 | tf_op jit(solution)/shard_map/ppermute | solution.py:48
  411.0 121.5 %collective-permute-start.43 = (bf16[512,1024]{1,0:T(8,128)(2,1)}, bf16[512,1024]{1,0:T(8,128)(2,1)}, u32[]{:S(2)}, u32[]{:S(2)}) collective-permute-start(bf16[512,1024]{1,0:T(8,128)(2,1)} %get-tuple-element.102), channel_id=1, source_target_pairs={{1,0},{3,2},{5,4},{7,6},{9,8},{11,10},{13,12},{15,14},{17,16},{19,... | collective-permute-start | bytes 3145736 | tf_op jit(solution)/shard_map/ppermute | solution.py:752
  412.7 110.5 %collective-permute-start.47 = (bf16[4,160,384]{2,1,0:T(8,128)(2,1)}, bf16[4,160,384]{2,1,0:T(8,128)(2,1)}, u32[]{:S(2)}, u32[]{:S(2)}) collective-permute-start(bf16[4,160,384]{2,1,0:T(8,128)(2,1)} %get-tuple-element.108), channel_id=1, source_target_pairs={{0,1},{1,0},{2,3},{3,2},{4,5},{5,4},{6,7},{7,6},{8,9},{9,8},{10,11... | collective-permute-start | bytes 1474568 | tf_op jit(solution)/shard_map/ppermute | solution.py:48
  453.3 69.9 %collective-permute-start.50 = (bf16[2,96,384]{2,1,0:T(8,128)(2,1)}, bf16[2,96,384]{2,1,0:T(8,128)(2,1)S(1)}, u32[]{:S(2)}, u32[]{:S(2)}) collective-permute-start(bf16[2,96,384]{2,1,0:T(8,128)(2,1)} %get-tuple-element.112), channel_id=1, source_target_pairs={{0,6},{2,0},{4,2},{6,4},{1,7},{3,1},{5,3},{7,5},{8,14},{10,8},{12,... | collective-permute-start | bytes 442376 | tf_op jit(solution)/shard_map/ppermute | solution.py:48
  456.0 100.7 %collective-permute-start.69 = (bf16[4,160,512]{2,1,0:T(8,128)(2,1)}, bf16[4,160,512]{2,1,0:T(8,128)(2,1)}, u32[]{:S(2)}, u32[]{:S(2)}) collective-permute-start(bf16[4,160,512]{2,1,0:T(8,128)(2,1)} %get-tuple-element.145), channel_id=1, source_target_pairs={{0,1},{1,0},{2,3},{3,2},{4,5},{5,4},{6,7},{7,6},{8,9},{9,8},{10,11... | collective-permute-start | bytes 1966088 | tf_op jit(solution)/shard_map/ppermute | solution.py:48
  462.9 120.0 %collective-permute-start.58 = (bf16[4,160,640]{2,1,0:T(8,128)(2,1)}, bf16[4,160,640]{2,1,0:T(8,128)(2,1)}, u32[]{:S(2)}, u32[]{:S(2)}) collective-permute-start(bf16[4,160,640]{2,1,0:T(8,128)(2,1)} %get-tuple-element.127), channel_id=1, source_target_pairs={{0,1},{1,0},{2,3},{3,2},{4,5},{5,4},{6,7},{7,6},{8,9},{9,8},{10,11... | collective-permute-start | bytes 2457608 | tf_op jit(solution)/shard_map/ppermute | solution.py:48
  (87 other events, 1776.9 us)

commit v2 on v1

v2 whole, which is shorter than its diff:
```python
import functools

import jax
import jax.numpy as jnp
from jax import lax
from jax.experimental import pallas as pl
from jax.experimental.pallas import tpu as pltpu
from jax.sharding import Mesh, PartitionSpec as P

HEAD_DIM = 64
EPS = 1e-05
BF = jnp.bfloat16
F32 = jnp.float32
NT = (((1,), (1,)), ((), ()))
TN = (((0,), (0,)), ((), ()))
MIB = 1 << 20


def dot(a, b):
    return jnp.dot(a, b, preferred_element_type=F32)


def dot_nt(a, b):
    return lax.dot_general(a, b, NT, preferred_element_type=F32)


def dot_tn(a, b):
    return lax.dot_general(a, b, TN, preferred_element_type=F32)


def aligned(value, multiple):
    return pl.multiple_of(value, multiple)


class Layout:
    def __init__(self, ny, nz, rows):
        self.ny, self.nz, self.rows = ny, nz, rows
        self.near = nz // 2

    def row_start(self, pos, dy, dc):
        block = lax.bitwise_xor(pos[0], jnp.int32(dy)) * 2 + lax.bitwise_xor(pos[1], jnp.int32(dc))
        return pl.multiple_of(block * self.rows, self.rows)

    def z_block(self, pos, dz):
        return lax.bitwise_xor(pos[2], jnp.int32(dz))

    def x_block(self, pos, dx):
        return lax.bitwise_xor(pos[3], jnp.int32(dx))


def trade(value, axis, size, distance):
    return lax.ppermute(value, axis, [(s, s ^ distance) for s in range(size)])


def around(value, axis, size):
    return [value] + [trade(value, axis, size, d) for d in range(1, size)]


class Gather:
    def __init__(self, lay, shard):
        self.lay, self.top, self.low = lay, [shard], []

    def one(self):
        near = self.lay.near
        pieces = around(self.top[0], "tz", self.lay.nz)
        self.top, self.low = pieces[:near], pieces[near:]

    def two(self):
        self.top = around(jnp.stack(self.top), "tx", 2)
        self.low = around(jnp.stack(self.low), "fy", self.lay.ny)

    def three(self):
        self.top = around(jnp.stack(self.top), "fy", self.lay.ny)
        self.low = around(jnp.stack(self.low), "tx", 2)

    def swap(self, which):
        if which == 0:
            self.twin = [trade(self.top[0], "c", 2, 1), trade(self.low[0], "c", 2, 1)]
        else:
            late = [trade(t, "c", 2, 1) for t in self.top[1:] + self.low[1:]]
            ny = self.lay.ny
            self.parts = self.top + self.low + [
                self.twin[0], *late[: ny - 1], self.twin[1], *late[ny - 1 :]
            ]


def stage(*things):
    values = []
    for thing in things:
        values.append((thing.top, thing.low) if isinstance(thing, (Gather, Scatter)) else thing)
    values = lax.optimization_barrier(values)
    back = []
    for thing, value in zip(things, values):
        if isinstance(thing, (Gather, Scatter)):
            thing.top, thing.low = value
        else:
            back.append(value)
    return back[0] if len(back) == 1 else back


def start_loads(lay, pos, refs, wants, sem):
    for dz in range(lay.nz):
        for dx in range(2):
            k = lay.z_block(pos, dz) * 2 + lay.x_block(pos, dx)
            for dc in range(2):
                mine = refs[dc * (lay.ny + 2) : (dc + 1) * (lay.ny + 2)]
                for dy in range(lay.ny):
                    start = lay.row_start(pos, dy, dc)
                    if len(refs) == 1:
                        block = refs[0].at[start // lay.rows * (2 * lay.nz) + k]
                    elif dz < lay.near:
                        block = mine[dy].at[dx, dz]
                    else:
                        block = mine[lay.ny + dx].at[dy, dz - lay.near]
                    for i, (first, width, whole) in enumerate(wants):
                        pltpu.make_async_copy(
                            block.at[:, pl.ds(first, width)],
                            whole.at[pl.ds(start, lay.rows), pl.ds(aligned(k * width, width), width)],
                            sem.at[dz, i],
                        ).start()


def wait_loads(lay, pos, dz, wants, sem):
    for i, (first, width, whole) in enumerate(wants):
        start = lax.bitwise_xor(pos[2], jnp.int32(dz)) * (2 * width)
        cols = whole.at[:, pl.ds(aligned(start, width), 2 * width)]
        pltpu.make_async_copy(cols, cols, sem.at[dz, i]).wait()


def kernel_call(body, pos, grid, ins, in_specs, outs, out_specs, scratch, aliases={}):
    return pl.pallas_call(
        body,
        out_shape=outs,
        grid_spec=pltpu.PrefetchScalarGridSpec(
            num_scalar_prefetch=1,
            grid=grid,
            in_specs=in_specs,
            out_specs=out_specs,
            scratch_shapes=scratch,
        ),
        input_output_aliases=aliases,
        compiler_params=pltpu.CompilerParams(
            dimension_semantics=("arbitrary",) * len(grid), vmem_limit_bytes=60 * MIB
        ),
        cost_estimate=pl.CostEstimate(flops=1000, bytes_accessed=1000, transcendentals=0),
    )(pos, *ins)


def shape(dims, dtype):
    return jax.ShapeDtypeStruct(dims, dtype)


def full(dims):
    return pl.BlockSpec(dims, lambda *_: (0,) * len(dims))


def at_cols(rows, width, place=lambda k, pos: k):
    return pl.BlockSpec((rows, width), lambda k, pos: (0, place(k, pos)))


def at_lead(lead, *dims, place=lambda k, pos: k):
    return pl.BlockSpec((lead,) + dims, lambda k, pos: (place(k, pos),) + (0,) * len(dims))


def z_place(k, pos):
    return lax.bitwise_xor(pos[2], k)


ANY = pl.BlockSpec(memory_space=pl.ANY)


def norm_parts(values):
    centred = values - jnp.mean(values, axis=-1, keepdims=True)
    inverse = lax.rsqrt(jnp.mean(centred * centred, axis=-1, keepdims=True) + EPS)
    return centred * inverse, inverse


def norm_backward(grad, unit, inverse, gain):
    scaled = grad * gain
    return inverse * (
        scaled
        - jnp.mean(scaled, axis=-1, keepdims=True)
        - unit * jnp.mean(scaled * unit, axis=-1, keepdims=True)
    )


def qkv_call(lay, pos, first, bias_q, bias_v, weights, width):
    both, dim = first.shape
    rows = both // 2
    blocks = 2 * lay.nz
    n = len(weights)

    def body(pos_ref, first_ref, bq_ref, bv_ref, *rest):
        refs, (q_ref, k_ref, v_ref, whole_q, whole_kv, sem) = rest[:n], rest[n:]
        wants = ((0, width, whole_q), (width, 2 * width, whole_kv))
        dz = pl.program_id(0)

        @pl.when(dz == 0)
        def _():
            start_loads(lay, pos_ref, refs, wants, sem)

        wait_loads(lay, pos_ref, dz, wants, sem)
        z = z_place(dz, pos_ref)
        kv = dot(first_ref[...], whole_kv[:, pl.ds(aligned(z * 4 * width, width), 4 * width)])
        q = dot(first_ref[rows:], whole_q[:, pl.ds(aligned(z * 2 * width, width), 2 * width)])
        q = ((q + bq_ref[...]).astype(BF) * HEAD_DIM**-0.5).astype(BF)
        for x in range(2):
            q_ref[x] = q[:, x * width : (x + 1) * width]
            k_ref[x] = kv[:, 2 * x * width : (2 * x + 1) * width].astype(BF)
            bias = bv_ref[:, x * width : (x + 1) * width]
            v_ref[x] = (kv[:, (2 * x + 1) * width : (2 * x + 2) * width] + bias).astype(BF)

    return kernel_call(
        body,
        pos,
        (lay.nz,),
        (first, bias_q, bias_v, *weights),
        [full((both, dim)), at_cols(1, 2 * width, z_place), at_cols(1, 2 * width, z_place)] + [ANY] * n,
        [
            shape((blocks, rows, width), BF),
            shape((blocks, both, width), BF),
            shape((blocks, both, width), BF),
        ],
        [
            at_lead(2, rows, width, place=z_place),
            at_lead(2, both, width, place=z_place),
            at_lead(2, both, width, place=z_place),
        ],
        [
            pltpu.VMEM((dim, blocks * width), BF),
            pltpu.VMEM((dim, blocks * 2 * width), BF),
            pltpu.SemaphoreType.DMA((lay.nz, 2)),
        ],
    )


def mask_bias(seg_k, seg_q, rows):
    both = seg_k.shape[0]
    key_at = lax.broadcasted_iota(jnp.int32, (both, rows), 0) - (both - rows)
    query_at = lax.broadcasted_iota(jnp.int32, (both, rows), 1)
    return jnp.where((seg_k == seg_q) & (key_at <= query_at), 0.0, -1e30).astype(F32)


def head_only(block, head):
    lane = lax.broadcasted_iota(jnp.int32, block.shape, 1)
    inside = (lane >= head * HEAD_DIM) & (lane < (head + 1) * HEAD_DIM)
    return jnp.where(inside, block, jnp.zeros_like(block))


def attend_call(pos, query, key, value, seg_k, seg_q):
    blocks, both, width = key.shape
    rows = query.shape[1]
    heads = width // HEAD_DIM
    step = min(rows, 128)

    def body(pos_ref, q_ref, k_ref, v_ref, sk_ref, sq_ref, mixed_ref, exact_ref, lse_ref, bias):
        @pl.when(pl.program_id(0) == 0)
        def _():
            bias[...] = mask_bias(sk_ref[...], sq_ref[...], rows)

        for tile in range(rows // step):
            here = slice(tile * step, (tile + 1) * step)
            keys = both - rows + (tile + 1) * step
            outs = []
            for head in range(heads):
                scores = dot_nt(k_ref[0, :keys], head_only(q_ref[0, here], head)) + bias[:keys, here]
                top = jnp.max(scores, axis=0, keepdims=True)
                expo = jnp.exp(scores - top)
                total = jnp.sum(expo, axis=0, keepdims=True)
                share = jnp.broadcast_to(1.0 / total, (8, step)).T[:, :1]
                outs.append(dot_tn(expo.astype(BF), v_ref[0, :keys]) * share)
                lse_ref[0, head : head + 1, here] = top + jnp.log(total)
            lane = lax.broadcasted_iota(jnp.int32, outs[0].shape, 1)
            out = outs[0]
            for head in range(1, heads):
                out = jnp.where(lane < head * HEAD_DIM, out, outs[head])
            exact_ref[here] = out
            mixed_ref[here] = out.astype(BF)

    return kernel_call(
        body,
        pos,
        (blocks,),
        (query, key, value, seg_k, seg_q),
        [at_lead(1, rows, width), at_lead(1, both, width), at_lead(1, both, width), full((both, 1)), full((1, rows))],
        [
            shape((rows, blocks * width), BF),
            shape((rows, blocks * width), F32),
            shape((blocks, heads, rows), F32),
        ],
        [at_cols(rows, width), at_cols(rows, width), at_lead(1, heads, rows)],
        [pltpu.VMEM((both, rows), F32)],
    )


def branch_call(lay, pos, mixed, tokens, b_out, gain, shift, weights, first, width):
    rows, dim = tokens.shape
    blocks = 2 * lay.nz
    n = len(weights)

    def body(pos_ref, mixed_ref, tok_ref, bias_ref, gain_ref, shift_ref, *rest):
        refs, (middle_ref, second_ref, whole, sem) = rest[:n], rest[n:]
        wants = ((first, width, whole),)
        start_loads(lay, pos_ref, refs, wants, sem)
        for dz in range(lay.nz):
            wait_loads(lay, pos_ref, dz, wants, sem)
        branch = dot_nt(mixed_ref[...], whole[...])
        middle = tok_ref[...].astype(F32) + branch + bias_ref[...]
        middle_ref[...] = middle
        second_ref[...] = (norm_parts(middle)[0] * gain_ref[...] + shift_ref[...]).astype(BF)

    return kernel_call(
        body,
        pos,
        (),
        (mixed, tokens, b_out, gain, shift, *weights),
        [full(mixed.shape), full(tokens.shape)] + [full((1, dim))] * 3 + [ANY] * n,
        [shape((rows, dim), F32), shape((rows, dim), BF)],
        [full((rows, dim)), full((rows, dim))],
        [pltpu.VMEM((dim, blocks * width), BF), pltpu.SemaphoreType.DMA((lay.nz, 1))],
    )


def up_call(lay, pos, second, b_up, weights, width):
    rows, dim = second.shape
    blocks = 2 * lay.nz
    n = len(weights)

    def body(pos_ref, second_ref, bias_ref, *rest):
        refs, (gelu_ref, slope_ref, whole, sem) = rest[:n], rest[n:]
        wants = ((0, width, whole),)
        dz = pl.program_id(0)

        @pl.when(dz == 0)
        def _():
            start_loads(lay, pos_ref, refs, wants, sem)

        wait_loads(lay, pos_ref, dz, wants, sem)
        z = z_place(dz, pos_ref)
        for x in range(2):
            here = slice(x * width, (x + 1) * width)
            cols = pl.ds(aligned((z * 2 + x) * width, width), width)
            u = dot(second_ref[...], whole[:, cols]) + bias_ref[:, here]
            scale = 0.7978845608028654
            square = u * u
            half = 0.5 + 0.5 * jnp.tanh(u * (scale + (scale * 0.044715) * square))
            gelu = u * half
            gelu_ref[:, here] = gelu.astype(BF)
            bend = 2.0 * scale + (6.0 * scale * 0.044715) * square
            slope_ref[:, here] = (half + gelu * (1.0 - half) * bend).astype(BF)

    return kernel_call(
        body,
        pos,
        (lay.nz,),
        (second, b_up, *weights),
        [full(second.shape), at_cols(1, 2 * width, z_place)] + [ANY] * n,
        [shape((rows, blocks * width), BF)] * 2,
        [at_cols(rows, 2 * width, z_place)] * 2,
        [pltpu.VMEM((dim, blocks * width), BF), pltpu.SemaphoreType.DMA((lay.nz, 1))],
    )


def result_call(lay, pos, gelu, middle, b_down, weights, width):
    rows, dim = middle.shape
    blocks = 2 * lay.nz
    n = len(weights)

    def body(pos_ref, gelu_ref, middle_ref, bias_ref, *rest):
        refs, (result_ref, whole, acc, sem) = rest[:n], rest[n:]
        wants = ((0, width, whole),)
        dz = pl.program_id(0)

        @pl.when(dz == 0)
        def _():
            start_loads(lay, pos_ref, refs, wants, sem)
            acc[...] = middle_ref[...] + bias_ref[...]

        wait_loads(lay, pos_ref, dz, wants, sem)
        cols = pl.ds(aligned(z_place(dz, pos_ref) * 2 * width, width), 2 * width)
        acc[...] += dot_nt(gelu_ref[...], whole[:, cols])

        @pl.when(dz == lay.nz - 1)
        def _():
            result_ref[...] = acc[...].astype(BF)

    return kernel_call(
        body,
        pos,
        (lay.nz,),
        (gelu, middle, b_down, *weights),
        [at_cols(rows, 2 * width, z_place), full((rows, dim)), full((1, dim))] + [ANY] * n,
        [shape((rows, dim), BF)],
        [full((rows, dim))],
        [
            pltpu.VMEM((dim, blocks * width), BF),
            pltpu.VMEM((rows, dim), F32),
            pltpu.SemaphoreType.DMA((lay.nz, 1)),
        ],
    )[0]


def pre_call(lay, pos, slope, grad, weights, width):
    rows, dim = grad.shape
    blocks = 2 * lay.nz
    n = len(weights)

    def body(pos_ref, slope_ref, grad_ref, *rest):
        refs, (pre_ref, hidden_ref, whole, sem) = rest[:n], rest[n:]
        wants = ((0, width, whole),)
        dz = pl.program_id(0)

        @pl.when(dz == 0)
        def _():
            start_loads(lay, pos_ref, refs, wants, sem)

        wait_loads(lay, pos_ref, dz, wants, sem)
        cols = pl.ds(aligned(z_place(dz, pos_ref) * 2 * width, width), 2 * width)
        pre = (dot(grad_ref[...], whole[:, cols]) * slope_ref[...].astype(F32)).astype(BF)
        pre_ref[...] = pre
        hidden_ref[...] = jnp.sum(pre.astype(F32), axis=0, keepdims=True)

    return kernel_call(
        body,
        pos,
        (lay.nz,),
        (slope, grad, *weights),
        [at_cols(rows, 2 * width, z_place), full((rows, dim))] + [ANY] * n,
        [shape((rows, blocks * width), BF), shape((1, blocks * width), F32)],
        [at_cols(rows, 2 * width, z_place), at_cols(1, 2 * width, z_place)],
        [pltpu.VMEM((dim, blocks * width), BF), pltpu.SemaphoreType.DMA((lay.nz, 1))],
    )


def second_back_call(lay, pos, pre, grad, middle, gain, weights, width):
    rows, dim = middle.shape
    blocks = 2 * lay.nz
    n = len(weights)

    def body(pos_ref, pre_ref, grad_ref, middle_ref, gain_ref, *rest):
        refs, (mgrad_ref, low_ref, sums_ref, whole, acc, sem) = rest[:n], rest[n:]
        wants = ((0, width, whole),)
        dz = pl.program_id(0)

        @pl.when(dz == 0)
        def _():
            start_loads(lay, pos_ref, refs, wants, sem)
            acc[...] = jnp.zeros_like(acc)

        wait_loads(lay, pos_ref, dz, wants, sem)
        cols = pl.ds(aligned(z_place(dz, pos_ref) * 2 * width, width), 2 * width)
        acc[...] += dot_nt(pre_ref[...], whole[:, cols])

        @pl.when(dz == lay.nz - 1)
        def _():
            unit, inverse = norm_parts(middle_ref[...])
            second_grad = acc[...]
            sums_ref[0:1] = jnp.sum(second_grad * unit, axis=0, keepdims=True)
            sums_ref[1:2] = jnp.sum(second_grad, axis=0, keepdims=True)
            out = grad_ref[...].astype(F32)
            sums_ref[3:4] = jnp.sum(out, axis=0, keepdims=True)
            out = out + norm_backward(second_grad, unit, inverse, gain_ref[...])
            sums_ref[2:3] = jnp.sum(out, axis=0, keepdims=True)
            mgrad_ref[...] = out
            low_ref[...] = out.astype(BF)

    return kernel_call(
        body,
        pos,
        (lay.nz,),
        (pre, grad, middle, gain, *weights),
        [at_cols(rows, 2 * width, z_place)] + [full((rows, dim))] * 2 + [full((1, dim))] + [ANY] * n,
        [shape((rows, dim), F32), shape((rows, dim), BF), shape((4, dim), F32)],
        [full((rows, dim))] * 2 + [full((4, dim))],
        [
            pltpu.VMEM((dim, blocks * width), BF),
            pltpu.VMEM((rows, dim), F32),
            pltpu.SemaphoreType.DMA((lay.nz, 1)),
        ],
    )


def mixed_grad_call(lay, pos, low, weights, first, width):
    rows, dim = low.shape
    blocks = 2 * lay.nz
    n = len(weights)

    def body(pos_ref, low_ref, *rest):
        refs, (out_ref, whole, sem) = rest[:n], rest[n:]
        wants = ((first, width, whole),)
        start_loads(lay, pos_ref, refs, wants, sem)
        for dz in range(lay.nz):
            wait_loads(lay, pos_ref, dz, wants, sem)
        out_ref[...] = dot(low_ref[...], whole[...]).astype(BF)

    return kernel_call(
        body,
        pos,
        (),
        (low, *weights),
        [full((rows, dim))] + [ANY] * n,
        [shape((rows, blocks * width), BF)],
        [full((rows, blocks * width))],
        [pltpu.VMEM((dim, blocks * width), BF), pltpu.SemaphoreType.DMA((lay.nz, 1))],
    )[0]


def attend_back_call(pos, span, query, key, value, seg_k, seg_q, lse, mixed_grad, exact, earlier=()):
    blocks, both, width = key.shape
    rows = query.shape[1]
    heads = width // HEAD_DIM
    step = min(rows, 256)
    begin = span[0]
    n = len(earlier)

    def body(pos_ref, q_ref, k_ref, v_ref, sk_ref, sq_ref, lse_ref, grad_ref, exact_ref, *rest):
        dq_ref, dk_ref, dv_ref, sums_ref, bias, dq_t, dk, dv = rest[n:]

        @pl.when(pl.program_id(0) == 0)
        def _():
            bias[...] = mask_bias(sk_ref[...], sq_ref[...], rows)

        key_t = k_ref[0].T
        inner_t = (grad_ref[...].astype(F32) * exact_ref[...]).T
        dk[...] = jnp.zeros_like(dk)
        dv[...] = jnp.zeros_like(dv)
        for tile in range(rows // step):
            here = slice(tile * step, (tile + 1) * step)
            keys = both - rows + (tile + 1) * step
            for head in range(heads):
                lanes = slice(head * HEAD_DIM, (head + 1) * HEAD_DIM)
                q_head = head_only(q_ref[0, here], head)
                g_head = head_only(grad_ref[here], head)
                scores = dot_nt(k_ref[0, :keys], q_head) + bias[:keys, here]
                probs = jnp.exp(scores - lse_ref[0, head : head + 1, here])
                prob_grad = dot_nt(v_ref[0, :keys], g_head)
                inner = jnp.sum(inner_t[lanes, here], axis=0, keepdims=True)
                score_grad = (probs * (prob_grad - inner)).astype(BF)
                dv[:keys] += dot(probs.astype(BF), g_head)
                dk[:keys] += dot(score_grad, q_head)
                dq_t[lanes, here] = dot(key_t[lanes, :keys], score_grad)
        dq = (dq_t[...].T * HEAD_DIM**-0.5).astype(BF)
        dv_low = dv[...].astype(BF)
        dq_ref[0] = dq
        dk_ref[0] = dk[...].astype(BF)
        dv_ref[0] = dv_low
        sums_ref[0:1] = jnp.sum(dq.astype(F32), axis=0, keepdims=True)
        sums_ref[1:2] = jnp.sum(dv_low.astype(F32), axis=0, keepdims=True)

    at = lambda k, pos: k + begin
    return kernel_call(
        body,
        pos,
        (span[1] - span[0],),
        (query, key, value, seg_k, seg_q, lse, mixed_grad, exact, *earlier),
        [
            at_lead(1, rows, width, place=at),
            at_lead(1, both, width, place=at),
            at_lead(1, both, width, place=at),
            full((both, 1)),
            full((1, rows)),
            at_lead(1, heads, rows, place=at),
            at_cols(rows, width, at),
            at_cols(rows, width, at),
        ]
        + [ANY] * n,
        [
            shape((blocks, rows, width), BF),
            shape((blocks, both, width), BF),
            shape((blocks, both, width), BF),
            shape((2, blocks * width), F32),
        ],
        [
            at_lead(1, rows, width, place=at),
            at_lead(1, both, width, place=at),
            at_lead(1, both, width, place=at),
            at_cols(2, width, at),
        ],
        [
            pltpu.VMEM((both, rows), F32),
            pltpu.VMEM((width, rows), F32),
            pltpu.VMEM((both, width), F32),
            pltpu.VMEM((both, width), F32),
        ],
        {9: 0, 10: 1, 11: 2, 12: 3} if n else {},
    )


def sides(ref, which, rows):
    here = slice(0, rows) if which == 0 else slice(rows, 2 * rows)
    return [ref[x, here] for x in range(2)]


def first_grad_prev_call(lay, pos, dk, dv, tokens, weights, width):
    rows, dim = tokens.shape
    blocks = 2 * lay.nz
    n = len(weights)

    def body(pos_ref, dk_ref, dv_ref, tok_ref, *rest):
        refs, (grad_ref, sums_ref, whole, acc, sem) = rest[:n], rest[n:]
        wants = ((width, 2 * width, whole),)
        dz = pl.program_id(0)

        @pl.when(dz == 0)
        def _():
            start_loads(lay, pos_ref, refs, wants, sem)
            acc[...] = jnp.zeros_like(acc)

        wait_loads(lay, pos_ref, dz, wants, sem)
        keys, values = sides(dk_ref, 0, rows), sides(dv_ref, 0, rows)
        part = jnp.concatenate([keys[0], values[0], keys[1], values[1]], axis=1)
        cols = pl.ds(aligned(z_place(dz, pos_ref) * 4 * width, width), 4 * width)
        acc[...] += dot_nt(part, whole[:, cols])

        @pl.when(dz == lay.nz - 1)
        def _():
            grad = acc[...]
            grad_ref[...] = grad.astype(BF)
            unit = norm_parts(tok_ref[...].astype(F32))[0]
            sums_ref[0:1] = jnp.sum(grad * unit, axis=0, keepdims=True)
            sums_ref[1:2] = jnp.sum(grad, axis=0, keepdims=True)

    both = at_lead(2, rows, width, place=z_place)
    return kernel_call(
        body,
        pos,
        (lay.nz,),
        (dk, dv, tokens, *weights),
        [both, both, full((rows, dim))] + [ANY] * n,
        [shape((rows, dim), BF), shape((2, dim), F32)],
        [full((rows, dim)), full((2, dim))],
        [
            pltpu.VMEM((dim, blocks * 2 * width), BF),
            pltpu.VMEM((rows, dim), F32),
            pltpu.SemaphoreType.DMA((lay.nz, 1)),
        ],
    )


def first_grad_own_call(lay, pos, dq, dk, dv, tokens, weights, width):
    rows, dim = tokens.shape
    blocks = 2 * lay.nz
    n = len(weights)

    def body(pos_ref, dq_ref, dk_ref, dv_ref, tok_ref, *rest):
        refs, (grad_ref, sums_ref, whole_q, whole_kv, sem) = rest[:n], rest[n:]
        wants = ((0, width, whole_q), (width, 2 * width, whole_kv))
        dz = pl.program_id(0)

        @pl.when(dz == 0)
        def _():
            start_loads(lay, pos_ref, refs, wants, sem)
            grad_ref[...] = jnp.zeros_like(grad_ref)

        wait_loads(lay, pos_ref, dz, wants, sem)
        z = z_place(dz, pos_ref)
        keys, values = sides(dk_ref, 1, rows), sides(dv_ref, 1, rows)
        part = jnp.concatenate([keys[0], values[0], keys[1], values[1]], axis=1)
        more = dot_nt(part, whole_kv[:, pl.ds(aligned(z * 4 * width, width), 4 * width)])
        part = jnp.concatenate([dq_ref[0], dq_ref[1]], axis=1)
        more += dot_nt(part, whole_q[:, pl.ds(aligned(z * 2 * width, width), 2 * width)])
        grad_ref[...] += more

        @pl.when(dz == lay.nz - 1)
        def _():
            grad = grad_ref[...]
            unit = norm_parts(tok_ref[...].astype(F32))[0]
            sums_ref[0:1] = jnp.sum(grad * unit, axis=0, keepdims=True)
            sums_ref[1:2] = jnp.sum(grad, axis=0, keepdims=True)

    both = at_lead(2, 2 * rows, width, place=z_place)
    return kernel_call(
        body,
        pos,
        (lay.nz,),
        (dq, dk, dv, tokens, *weights),
        [at_lead(2, rows, width, place=z_place), both, both, full((rows, dim))] + [ANY] * n,
        [shape((rows, dim), F32), shape((2, dim), F32)],
        [full((rows, dim)), full((2, dim))],
        [
            pltpu.VMEM((dim, blocks * width), BF),
            pltpu.VMEM((dim, blocks * 2 * width), BF),
            pltpu.SemaphoreType.DMA((lay.nz, 2)),
        ],
    )


def half_grad_call(lay, pos, *, half, columns, lefts, tile, operands, specs, received):
    ny, nz, near, rows = lay.ny, lay.nz, lay.near, lay.rows
    n = len(operands)

    def body(pos_ref, *refs):
        ins, rest = refs[:n], refs[n:]
        got, rest = (rest[0], rest[1:]) if half == 0 else (None, rest)
        count = ny + 2 if half == 0 else 1
        outs, turned, spare = rest[:count], rest[count : count + len(lefts)], rest[count + len(lefts) :]
        dz = pl.program_id(0)

        @pl.when(dz == 0)
        def _():
            for index, ref in zip(lefts, turned):
                if rows % 128:
                    spare[0][...] = ins[index][...].T
                for dy in range(ny):
                    span = pl.ds(lay.row_start(pos_ref, dy, half), rows)
                    piece = spare[0][span] if rows % 128 else ins[index][:, span].T
                    ref[dy * rows : (dy + 1) * rows] = piece

        def make(put):
            blocks = tile(turned, ins, [lay.x_block(pos_ref, dx) for dx in range(2)])
            for dx in range(2):
                for dy in range(ny):
                    block = blocks[dx][dy * rows : (dy + 1) * rows]
                    if half == 0:
                        block = block + got[0, dx, dy].astype(F32)
                    put(dx, dy, block.astype(BF))

        if half == 1:

            def put(dx, dy, block):
                outs[0][0, dx, dy] = block

            make(put)
            return

        @pl.when(dz < near)
        def _():
            def put(dx, dy, block):
                outs[dy][0, dx] = block

            make(put)

        @pl.when(dz >= near)
        def _():
            def put(dx, dy, block):
                outs[ny + dx][0, dy] = block

            make(put)

    def step(*dims, at=lambda dz: dz):
        return pl.BlockSpec((1,) + dims, lambda dz, pos: (at(dz),) + (0,) * len(dims))

    if half == 0:
        operands = (*operands, received)
        specs = [*specs, step(2, ny, rows, columns)]
        outs = [shape((near, 2, rows, columns), BF)] * ny + [shape((nz - near, ny, rows, columns), BF)] * 2
        out_specs = [step(2, rows, columns, at=lambda dz: jnp.minimum(dz, near - 1))] * ny
        out_specs += [step(ny, rows, columns, at=lambda dz: jnp.maximum(dz - near, 0))] * 2
    else:
        outs = [shape((nz, 2, ny, rows, columns), BF)]
        out_specs = [step(2, ny, rows, columns)]
    scratch = [pltpu.VMEM((ny * rows, operands[index].shape[0]), BF) for index in lefts]
    if rows % 128:
        scratch.append(pltpu.VMEM(operands[lefts[0]].shape[::-1], BF))
    return kernel_call(body, pos, (nz,), operands, specs, outs, out_specs, scratch)


def sum_call(pos, groups, outs, build, steps=1):
    cut = lambda dims: (dims[0] // steps,) + dims[1:]
    spec = lambda r: pl.BlockSpec(cut(r.shape), lambda k, pos: (k,) + (0,) * (len(r.shape) - 1))
    flat = [r for g in groups for r in g]

    def body(pos_ref, *refs):
        ins, given = refs[: len(flat)], refs[len(flat) :]
        at, sums = 0, []
        for g in groups:
            mine = ins[at : at + len(g)]
            at += len(g)
            sums.append(lambda index, mine=mine: sum(
                (r[index].astype(F32) for r in mine[1:]), mine[0][index].astype(F32)
            ))
        build(sums, given)

    return kernel_call(
        body, pos, (steps,), flat, [spec(r) for r in flat], outs, [spec(o) for o in outs], []
    )


class Scatter:
    def __init__(self, lay, pos, columns, lefts, tile, operands, specs):
        self.lay, self.pos, self.columns = lay, pos, columns
        self.half = functools.partial(
            half_grad_call, lay, pos, columns=columns, lefts=lefts, tile=tile, operands=operands,
            specs=specs,
        )

    def away(self):
        self.sent = self.half(half=1, received=None)[0]

    def swap(self):
        self.received = trade(self.sent, "c", 2, 1)

    def own(self):
        parts = self.half(half=0, received=self.received)
        self.top, self.low = parts[: self.lay.ny], parts[self.lay.ny :]

    def send_one(self):
        self.top = [self.top[0]] + [trade(self.top[d], "fy", self.lay.ny, d) for d in range(1, self.lay.ny)]
        self.low = [self.low[0], trade(self.low[1], "tx", 2, 1)]

    def sum_one(self):
        ny, rows, near, far = self.lay.ny, self.lay.rows, self.lay.near, self.lay.nz - self.lay.near

        def build(sums, given):
            for dx in range(2):
                given[dx][...] = sums[0]((slice(None), dx)).astype(BF)
            for dy in range(ny):
                given[2 + dy][...] = sums[1]((slice(None), dy)).astype(BF)

        outs = [shape((near, rows, self.columns), BF)] * 2 + [shape((far, rows, self.columns), BF)] * ny
        out = sum_call(self.pos, [self.top, self.low], outs, build, near if near == far else 1)
        self.top, self.low = out[:2], out[2:]

    def send_two(self):
        self.top = [self.top[0], trade(self.top[1], "tx", 2, 1)]
        self.low = [self.low[0]] + [trade(self.low[d], "fy", self.lay.ny, d) for d in range(1, self.lay.ny)]

    def sum_two(self):
        near, nz = self.lay.near, self.lay.nz

        def build(sums, given):
            for dz in range(nz):
                given[dz][...] = (sums[0](dz) if dz < near else sums[1](dz - near)).astype(BF)

        outs = [shape((self.lay.rows, self.columns), BF)] * nz
        self.top = sum_call(self.pos, [self.top, self.low], outs, build)
        self.low = []

    def send_three(self):
        self.top = [self.top[0]] + [trade(self.top[d], "tz", self.lay.nz, d) for d in range(1, self.lay.nz)]

    def sum_three(self, cuts):
        outs = [shape((self.lay.rows, *c) if isinstance(c, tuple) else (self.lay.rows, c), F32) for c in cuts]

        def build(sums, given):
            at = 0
            for ref, c in zip(given, cuts):
                if isinstance(c, tuple):
                    for i in range(c[0]):
                        ref[:, i, :] = sums[0]((slice(None), slice(at, at + c[1])))
                        at += c[1]
                else:
                    ref[...] = sums[0]((slice(None), slice(at, at + c)))
                    at += c

        self.out = sum_call(self.pos, [self.top], outs, build)


def per_device(
    sizes,
    tokens,
    segment_ids,
    w_qkv,
    b_qv,
    w_out,
    b_out,
    w_up,
    b_up,
    w_down,
    b_down,
    ln1_gain,
    ln1_shift,
    ln2_gain,
    ln2_shift,
    grad_out,
):
    ny, nz = sizes
    rows, dim = tokens.shape
    length = segment_ids.shape[1]
    width = w_qkv.shape[2]
    hidden = w_up.shape[1]
    lay = Layout(ny, nz, w_qkv.shape[0])
    axes = ("fy", "c", "tz", "tx")
    pos = jnp.stack([lax.axis_index(axis) for axis in axes]).astype(jnp.int32)
    row = lambda v: v.reshape(1, -1)

    blocks = 2 * nz
    half = nz
    up_parts = [lax.all_gather(jnp.concatenate([w_up, w_out], axis=1), axes, axis=0, tiled=False)]
    qkv = Gather(lay, w_qkv.reshape(lay.rows, 3 * width))
    down = Gather(lay, w_down)
    qkv.one()
    tokens_prev = lax.ppermute(tokens, "tx", [(0, 1)])
    qkv.low, tokens_prev = stage(qkv.low, tokens_prev)
    qkv.two()
    qkv.three()
    qkv.swap(0)

    sequence = (pos[2] * 2 + pos[3]) // 2
    later = pos[3] > 0
    ids = lax.dynamic_slice_in_dim(segment_ids, sequence, 1, 0)
    seg_q = jnp.where(later, ids[:, rows:], ids[:, :rows])
    seg_prev = jnp.where(later, ids[:, :rows], -1)
    seg_k = jnp.concatenate([seg_prev, seg_q], axis=1).reshape(length, 1)
    both = jnp.concatenate([tokens_prev, tokens], axis=0).astype(F32)
    first = (norm_parts(both)[0] * ln1_gain + ln1_shift).astype(BF)
    first, seg_k, seg_q = stage(qkv, down, first, seg_k, seg_q)
    qkv.swap(1)
    down.one()
    qkv.parts, first = stage(qkv.parts, first)
    query, key, value = qkv_call(lay, pos, first, b_qv[0:1], b_qv[1:2], qkv.parts, width)
    mixed, exact, lse = attend_call(pos, query, key, value, seg_k, seg_q)
    mixed, up_parts = stage(down, mixed, up_parts)
    down.two()
    middle, second = branch_call(
        lay, pos, mixed, tokens, row(b_out), row(ln2_gain), row(ln2_shift), up_parts, hidden, width
    )
    middle, second = stage(down, middle, second)
    down.three()
    down.swap(0)
    gelu, slope = up_call(lay, pos, second, row(b_up), up_parts, hidden)

    whole = lambda v: full(v.shape)
    at_z = lambda size: at_cols(rows, 2 * size, z_place)
    block = lambda ref, x, size: ref[:, pl.ds(aligned(x * size, size), size)]

    def down_tile(left, ins, xs):
        return [dot(left[0][...], block(ins[1], x, hidden)) for x in xs]

    grad_down = Scatter(
        lay, pos, hidden, (0,), down_tile, (grad_out, gelu), [whole(grad_out), at_z(hidden)]
    )
    grad_down.away()
    grad_down.swap()
    grad_down.own()
    slope = stage(grad_down, down, slope)
    down.swap(1)
    grad_down.send_one()
    pre, grad_b_up = pre_call(lay, pos, slope, grad_out, down.parts, hidden)
    middle_grad, middle_low, sums2 = second_back_call(
        lay, pos, pre, grad_out, middle, row(ln2_gain), up_parts, hidden
    )

    def up_tile(left, ins, xs):
        return [
            jnp.concatenate(
                [dot(left[0][...], block(ins[1], x, hidden)), dot(left[1][...], block(ins[3], x, width))],
                axis=1,
            )
            for x in xs
        ]

    grad_up = Scatter(
        lay, pos, hidden + width, (0, 2), up_tile, (second, pre, middle_low, mixed),
        [whole(second), at_z(hidden), whole(middle_low), at_z(width)],
    )
    mixed_grad = mixed_grad_call(lay, pos, middle_low, up_parts, hidden, width)
    grad_up.away()
    grad_up.sent, mixed_grad = stage(grad_down, grad_up.sent, mixed_grad)
    grad_down.sum_one()
    grad_up.sent, mixed_grad = stage(grad_down, grad_up.sent, mixed_grad)
    grad_down.send_two()
    grad_up.swap()
    partial = attend_back_call(pos, (0, half), query, key, value, seg_k, seg_q, lse, mixed_grad, exact)
    partial, grad_up.received = stage(grad_down, partial, grad_up.received)
    grad_down.sum_two()
    grad_up.own()
    partial = stage(grad_up, grad_down, partial)
    grad_up.send_one()
    grad_down.send_three()
    dq, dk, dv, sums_qv = attend_back_call(
        pos, (half, blocks), query, key, value, seg_k, seg_q, lse, mixed_grad, exact, partial
    )
    back, sums_prev = first_grad_prev_call(lay, pos, dk, dv, tokens_prev, qkv.parts, width)

    def qkv_tile(left, ins, xs):
        late = left[0][:, rows:]
        q = dot(late, jnp.concatenate([ins[1][x] for x in xs], axis=1))
        out = []
        for i, x in enumerate(xs):
            kv = dot(left[0][...], jnp.concatenate([ins[2][x], ins[3][x]], axis=1))
            out.append(jnp.concatenate([q[:, i * width : (i + 1) * width], kv], axis=1))
        return out

    grad_qkv = Scatter(
        lay, pos, 3 * width, (0,), qkv_tile, (first, dq, dk, dv),
        [
            whole(first),
            at_lead(2, rows, width, place=z_place),
            at_lead(2, 2 * rows, width, place=z_place),
            at_lead(2, 2 * rows, width, place=z_place),
        ],
    )
    grad_qkv.away()
    grad_qkv.sent, dq, dk, dv = stage(grad_up, grad_down, grad_qkv.sent, dq, dk, dv)
    grad_up.sum_one()
    grad_qkv.sent, dq, dk, dv = stage(grad_up, grad_qkv.sent, dq, dk, dv)
    grad_up.send_two()
    grad_qkv.swap()
    grad_down.sum_three((hidden,))
    grad_qkv.received, dq, dk, dv, grad_down.out = stage(grad_qkv.received, dq, dk, dv, grad_down.out)
    grad_qkv.own()
    dq, dk, dv, sums_prev = stage(grad_qkv, dq, dk, dv, sums_prev)
    grad_qkv.send_one()
    dq, dk, dv, sums_prev = stage(grad_up, dq, dk, dv, sums_prev)
    grad_up.sum_two()
    dq, dk, dv, sums_prev = stage(grad_up, dq, dk, dv, sums_prev)
    grad_up.send_three()
    first_grad, sums1 = first_grad_own_call(lay, pos, dq, dk, dv, tokens, qkv.parts, width)
    small = jnp.concatenate(
        [v.reshape(-1) for v in (sums2, grad_b_up, sums1 + sums_prev, sums_qv)]
    ).reshape(-1, 128)
    small = small + trade(small, "c", 2, 1)
    result = result_call(lay, pos, gelu, middle, row(b_down), down.parts, hidden)
    first_grad, small, result, back = stage(grad_qkv, first_grad, small, result, back)
    grad_qkv.sum_one()
    first_grad, small, back = stage(grad_qkv, first_grad, small, back)
    small = small + trade(small, "tx", 2, 1)
    grad_qkv.send_two()
    small, back = stage(small, back)
    back = lax.ppermute(back, "tx", [(1, 0)])
    small = sum(around(small, "fy", ny))
    small = stage(grad_up, small)
    grad_up.sum_three((hidden, width))
    small, grad_up.out = stage(grad_qkv, small, grad_up.out)
    grad_qkv.sum_two()
    small = stage(grad_qkv, small)
    small = around(small, "tz", nz)
    grad_qkv.send_three()
    back = stage(grad_qkv, back)
    small = sum(small).reshape(-1)
    grad_qkv.sum_three(((3, width),))
    unit, inverse = norm_parts(tokens.astype(F32))
    first_grad = first_grad + back.astype(F32)
    token_grad = (middle_grad + norm_backward(first_grad, unit, inverse, ln1_gain)).astype(BF)
    at = 4 * dim
    late = small[at + gelu.shape[1] :]
    return (
        result,
        token_grad,
        grad_qkv.out[0],
        late[2 * dim :].reshape(2, -1),
        grad_up.out[1],
        small[2 * dim : 3 * dim],
        grad_up.out[0],
        small[at : at + gelu.shape[1]],
        grad_down.out[0],
        small[3 * dim : at],
        late[:dim],
        late[dim : 2 * dim],
        small[:dim],
        small[dim : 2 * dim],
    )


def solution(mesh):
    n_fsdp, n_tp = mesh.devices.shape
    fine = Mesh(
        mesh.devices.reshape(n_fsdp // 2, 2, n_tp // 2, 2), ("fy", "c", "tz", "tx")
    )
    fsdp, tp, every = ("fy", "c"), ("tz", "tx"), ("fy", "c", "tz", "tx")
    tile = P(fsdp, tp)
    ins = (
        P(every, None),
        P(fsdp, None),
        P(fsdp, None, tp),
        P(),
        tile,
        P(),
        tile,
        P(),
        tile,
        P(),
        P(),
        P(),
        P(),
        P(),
        P(every, None),
    )
    outs = (
        P(every, None),
        P(every, None),
        P(fsdp, None, tp),
        P(),
        tile,
        P(),
        tile,
        P(),
        tile,
        P(),
        P(),
        P(),
        P(),
        P(),
    )
    return jax.shard_map(
        functools.partial(per_device, (n_fsdp // 2, n_tp // 2)),
        mesh=fine,
        in_specs=ins,
        out_specs=outs,
        check_vma=False,
    )
```

time: 627 us -> 451 us (0.72)
  starting transfers between devices: 137 us -> 70.9 us
  blocking collectives: 59.1 us -> 0 us
  waiting for transfers between devices: 145 us -> 106 us
  Pallas kernels: 238 us -> 221 us
  between operations: 1.56 us -> 15 us
    ppermute x76 -> x53, starting transfers between devices: 132 us -> 66 us  [the longest x52 64.7 us: trade(): return lax.ppermute(value, axis, [(s, s ^ distance) for s in range(size)])]
    psum x1 -> x0, blocking collectives: 59.1 us -> none  [per_device(): lax.psum(jnp.concatenate([sums1.reshape(-1), sums_qv.reshape(-1)]), axes)]
    ppermute x76 -> x53, waiting for transfers between devices: 132 us -> 102 us  [the longest x52 102 us: trade(): return lax.ppermute(value, axis, [(s, s ^ distance) for s in range(size)])]
    pallas_call x23 -> x27, Pallas kernels: 238 us -> 221 us  [kernel_call(): pl.pallas_call(body, out_shape=outs, grid_spec=pltpu.PrefetchScalarGridSp...]
    ppermute x1, waiting for transfers between devices: 12.3 us -> 0.01 us  [per_device(): tokens_prev = lax.ppermute(tokens, 'tx', [(0, 1)])]
  transfers between devices with their start and end apart: 77 -> 55, of which waited for: 20 -> 21; matrix products, arithmetic and copies ran while one was open for 5% -> 4% of each run, Pallas kernels for 32% -> 38%
where the time goes in v2:
time: 451 us; the launch traced here: 446 us
  Pallas kernels  221 us (49%)
  waiting for transfers between devices  106 us (24%)
  starting transfers between devices  70.9 us (16%)
  other arithmetic  17.4 us (4%)
  local copies, waits for them, and re-layouts  16.2 us (4%)
  between operations  15 us (3%)
    pallas_call x27, Pallas kernels, kernel_call(): pl.pallas_call(body, out_shape=outs, grid_spec=pltpu.PrefetchScalarGridSp...  221 us
    ppermute x52, waiting for transfers between devices, trade(): return lax.ppermute(value, axis, [(s, s ^ distance) for s in range(size)])  102 us
    ppermute x52, starting transfers between devices, trade(): return lax.ppermute(value, axis, [(s, s ^ distance) for s in range(size)])  64.7 us
    unnamed x83, local copies, waits for them, and re-layouts  10.2 us
  transfers between devices with their start and end apart: 55, of which 21 were waited for; matrix products, arithmetic and copies ran while one was open for 4% of the time, Pallas kernels for 38%

profile of v2, /device:TPU:0, one launch (start us, length us, event | category | flops | bytes accessed | tf_op | source)
XLA Modules:
  0.0 446.3 jit_solution(8096552206997371866)
XLA Ops:
  9.0 4.9 %collective-permute-start.5 = (bf16[512,1024]{1,0:T(8,128)(2,1)}, bf16[512,1024]{1,0:T(8,128)(2,1)S(1)}, u32[]{:S(2)}, u32[]{:S(2)}) collective-permute-start(bf16[512,1024]{1,0:T(8,128)(2,1)} %tok_ref.3), channel_id=1, source_target_pairs={{0,1},{2,3},{4,5},{6,7},{8,9},{10,11},{12,13},{14,15},{16,17},{18,... | collective-permute-start | bytes 3145736 | tf_op jit(solution)/shard_map/ppermute | solution.py:883
  17.0 4.6 %collective-permute-done = bf16[256,384]{1,0:T(8,128)(2,1)S(1)} collective-permute-done((bf16[256,384]{1,0:T(8,128)(2,1)S(1)}, bf16[256,384]{1,0:T(8,128)(2,1)S(1)}, u32[]{:S(2)}, u32[]{:S(2)}) %collective-permute-start) | collective-permute-done | bytes 196640 | tf_op jit(solution)/shard_map/ppermute | solution.py:52
  26.5 18.1 %collective-permute-done.3 = bf16[256,384]{1,0:T(8,128)(2,1)S(1)} collective-permute-done((bf16[256,384]{1,0:T(8,128)(2,1)S(1)}, bf16[256,384]{1,0:T(8,128)(2,1)S(1)}, u32[]{:S(2)}, u32[]{:S(2)}) %collective-permute-start.3) | collective-permute-done | bytes 196640 | tf_op jit(solution)/shard_map/ppermute | solution.py:52
  50.3 6.9 %collective-permute-done.6 = bf16[2,256,384]{2,1,0:T(8,128)(2,1)S(1)} collective-permute-done((bf16[2,256,384]{2,1,0:T(8,128)(2,1)S(1)}, bf16[2,256,384]{2,1,0:T(8,128)(2,1)S(1)}, u32[]{:S(2)}, u32[]{:S(2)}) %collective-permute-start.6) | collective-permute-done | bytes 393248 | tf_op jit(solution)/shard_map/ppermute | solution.py:52
  62.1 12.1 %collective-permute-done.2.rest_1_ = bf16[2,2,256,384]{3,2,1,0:T(8,128)(2,1)} collective-permute-done((bf16[2,2,256,384]{3,2,1,0:T(8,128)(2,1)S(1)}, bf16[2,2,256,384]{3,2,1,0:T(8,128)(2,1)}, u32[]{:S(2)}, u32[]{:S(2)}) %collective-permute-start.2) | collective-permute-done | bytes 786464 | tf_op jit(solution)/shard_map/ppermute | solution.py:52
  74.2 5.0 %collective-permute-done.7.rest_3_ = bf16[2,2,256,384]{3,2,1,0:T(8,128)(2,1)} collective-permute-done((bf16[2,2,256,384]{3,2,1,0:T(8,128)(2,1)}, bf16[2,2,256,384]{3,2,1,0:T(8,128)(2,1)}, u32[]{:S(2)}, u32[]{:S(2)}) %collective-permute-start.7) | collective-permute-done | bytes 786464 | tf_op jit(solution)/shard_map/ppermute | solution.py:52
  79.7 9.0 %collective-permute-start.12 = (bf16[256,512]{1,0:T(8,128)(2,1)S(1)}, bf16[256,512]{1,0:T(8,128)(2,1)S(1)}, u32[]{:S(2)}, u32[]{:S(2)}) collective-permute-start(bf16[256,512]{1,0:T(8,128)(2,1)S(1)} %copy-done.25), channel_id=1, source_target_pairs={{0,2},{2,0},{4,6},{6,4},{1,3},{3,1},{5,7},{7,5},{8,10},{10,8},{12,... | collective-permute-start | bytes 786440 | tf_op jit(solution)/shard_map/ppermute | solution.py:52
  88.7 4.6 %collective-permute-start.13 = (bf16[256,512]{1,0:T(8,128)(2,1)S(1)}, bf16[256,512]{1,0:T(8,128)(2,1)S(1)}, u32[]{:S(2)}, u32[]{:S(2)}) collective-permute-start(bf16[256,512]{1,0:T(8,128)(2,1)S(1)} %copy-done.25), channel_id=1, source_target_pairs={{0,4},{2,6},{4,0},{6,2},{1,5},{3,7},{5,1},{7,3},{8,12},{10,14},{12... | collective-permute-start | bytes 786440 | tf_op jit(solution)/shard_map/ppermute | solution.py:52
  98.0 11.3 %shard_map.254 = (bf16[8,512,128]{2,1,0:T(8,128)(2,1)}, bf16[8,1024,128]{2,1,0:T(8,128)(2,1)}, bf16[8,1024,128]{2,1,0:T(8,128)(2,1)}) custom-call(s32[4]{0:T(128)} %pad_add_fusion.pos_ref, bf16[1024,1024]{1,0:T(8,128)(2,1)} %fusion.5.first_ref.refs_0_, f32[1,1024]{1,0:T(1,128)} %get-tuple-element.511.bq_ref, f32[1,1024]{1,0:T(1,128)} %get-tuple-element.510.bv_ref, ...), custom_call_target="tpu_custom_call" | custom-call | flops 1000 | bytes 1000 | tf_op jit(solution)/shard_map/pallas_call | solution.py:131
  109.3 20.6 %shard_map.255 = (bf16[512,1024]{1,0:T(8,128)(2,1)}, f32[512,1024]{1,0:T(8,128)}, f32[8,2,512]{2,1,0:T(2,128)}) custom-call(s32[4]{0:T(128)} %pad_add_fusion.pos_ref, bf16[8,512,128]{2,1,0:T(8,128)(2,1)} %get-tuple-element.258.q_ref, bf16[8,1024,128]{2,1,0:T(8,128)(2,1)} %get-tuple-element.259.k_ref, bf16[8,1024,128]{2,1,0:T(8,128)(2,1)} %get-tuple-element.260.v_ref, ...), custom_call_target="tpu_custom_call" | custom-call | flops 1000 | bytes 1000 | tf_op jit(solution)/shard_map/pallas_call | solution.py:131
  136.6 7.0 %shard_map.256 = (f32[512,1024]{1,0:T(8,128)}, bf16[512,1024]{1,0:T(8,128)(2,1)}) custom-call(s32[4]{0:T(128)} %pad_add_fusion.pos_ref, bf16[512,1024]{1,0:T(8,128)(2,1)} %get-tuple-element.270.mixed_ref.refs_3_, bf16[512,1024]{1,0:T(8,128)(2,1)} %tok_ref.3, f32[1,1024]{1,0:T(1,128)} %bitcast.88, f32[1,1024]{1,0:T(1,128)} %bitcast.86, f32[1,1024]{1,0:T(1,128)} %bitcast.89, ...), custom_call_target="tpu_custom_call" | custom-call | flops 1000 | bytes 1000 | tf_op jit(solution)/shard_map/pallas_call | solution.py:131
  149.3 13.4 %shard_map.257 = (bf16[512,4096]{1,0:T(8,128)(2,1)}, bf16[512,4096]{1,0:T(8,128)(2,1)}) custom-call(s32[4]{0:T(128)} %pad_add_fusion.pos_ref, bf16[512,1024]{1,0:T(8,128)(2,1)} %get-tuple-element.274.second_ref.refs_0_, f32[1,4096]{1,0:T(1,128)} %bitcast.84, bf16[32,256,640]{2,1,0:T(8,128)(2,1)} %bitcast.62), custom_call_target="tpu_custom_call" | custom-call | flops 1000 | bytes 1000 | tf_op jit(solution)/shard_map/pallas_call | solution.py:131
  162.8 7.2 %shard_map.258 = bf16[4,2,2,256,512]{4,3,2,1,0:T(8,128)(2,1)} custom-call(s32[4]{0:T(128)} %pad_add_fusion.pos_ref, bf16[512,1024]{1,0:T(8,128)(2,1)} %grad_ref.3, bf16[512,4096]{1,0:T(8,128)(2,1)} %get-tuple-element.275.refs_1_.gelu_ref), custom_call_target="tpu_custom_call" | custom-call | flops 1000 | bytes 1000 | tf_op jit(solution)/shard_map/pallas_call | solution.py:131
  172.5 5.0 %collective-permute-done.17.refs_2_ = bf16[4,2,2,256,512]{4,3,2,1,0:T(8,128)(2,1)} collective-permute-done((bf16[4,2,2,256,512]{4,3,2,1,0:T(8,128)(2,1)}, bf16[4,2,2,256,512]{4,3,2,1,0:T(8,128)(2,1)}, u32[]{:S(2)}, u32[]{:S(2)}) %collective-permute-start.17) | collective-permute-done | bytes 4194336 | tf_op jit(solution)/shard_map/ppermute | solution.py:52
  177.5 8.5 %shard_map.259 = (bf16[2,2,256,512]{3,2,1,0:T(8,128)(2,1)}, bf16[2,2,256,512]{3,2,1,0:T(8,128)(2,1)}, bf16[2,2,256,512]{3,2,1,0:T(8,128)(2,1)}, bf16[2,2,256,512]{3,2,1,0:T(8,128)(2,1)}) custom-call(s32[4]{0:T(128)} %pad_add_fusion.pos_ref, bf16[512,1024]{1,0:T(8,128)(2,1)} %grad_ref.3, bf16[512,4096]{1,0:T(8,128)(2,1)} %get-tuple-element.275.refs_1_.gelu_ref, ...), custom_call_target="tpu_custom_call" | custom-call | flops 1000 | bytes 1000 | tf_op jit(solution)/shard_map/pallas_call | solution.py:131
  186.1 9.7 %collective-permute-done.19.rest_3_ = bf16[2,2,256,512]{3,2,1,0:T(8,128)(2,1)S(1)} collective-permute-done((bf16[2,2,256,512]{3,2,1,0:T(8,128)(2,1)S(1)}, bf16[2,2,256,512]{3,2,1,0:T(8,128)(2,1)S(1)}, u32[]{:S(2)}, u32[]{:S(2)}) %collective-permute-start.19) | collective-permute-done | bytes 1048608 | tf_op jit(solution)/shard_map/ppermute | solution.py:52
  201.3 10.7 %shard_map.260 = (bf16[512,4096]{1,0:T(8,128)(2,1)}, f32[1,4096]{1,0:T(1,128)}) custom-call(s32[4]{0:T(128)} %pad_add_fusion.pos_ref, bf16[512,4096]{1,0:T(8,128)(2,1)} %get-tuple-element.289.slope_ref, bf16[512,1024]{1,0:T(8,128)(2,1)} %grad_ref.3, bf16[2,2,256,512]{3,2,1,0:T(8,128)(2,1)} %copy-done.5, ...), custom_call_target="tpu_custom_call" | custom-call | flops 1000 | bytes 1000 | tf_op jit(solution)/shard_map/pallas_call | solution.py:131
  212.0 13.2 %shard_map.261 = (f32[512,1024]{1,0:T(8,128)}, bf16[512,1024]{1,0:T(8,128)(2,1)}, f32[4,1024]{1,0:T(4,128)}) custom-call(s32[4]{0:T(128)} %pad_add_fusion.pos_ref, bf16[512,4096]{1,0:T(8,128)(2,1)} %get-tuple-element.294.pre_ref.refs_1_, bf16[512,1024]{1,0:T(8,128)(2,1)} %grad_ref.3, f32[512,1024]{1,0:T(8,128)} %get-tuple-element.295.middle_ref, ...), custom_call_target="tpu_custom_call" | custom-call | flops 1000 | bytes 1000 | tf_op jit(solution)/shard_map/pallas_call | solution.py:131
  225.1 5.8 %shard_map.263.grad_ref = bf16[512,1024]{1,0:T(8,128)(2,1)} custom-call(s32[4]{0:T(128)} %pad_add_fusion.pos_ref, bf16[512,1024]{1,0:T(8,128)(2,1)} %get-tuple-element.296.refs_2_.low_ref, bf16[32,256,640]{2,1,0:T(8,128)(2,1)} %bitcast.64), custom_call_target="tpu_custom_call" | custom-call | flops 1000 | bytes 1000 | tf_op jit(solution)/shard_map/pallas_call | solution.py:131
  230.9 8.9 %shard_map.262 = bf16[4,2,2,256,640]{4,3,2,1,0:T(8,128)(2,1)} custom-call(s32[4]{0:T(128)} %pad_add_fusion.pos_ref, bf16[512,1024]{1,0:T(8,128)(2,1)} %get-tuple-element.274.second_ref.refs_0_, bf16[512,4096]{1,0:T(8,128)(2,1)} %get-tuple-element.294.pre_ref.refs_1_, bf16[512,1024]{1,0:T(8,128)(2,1)} %get-tuple-element.296.refs_2_.low_ref, ...), custom_call_target="tpu_custom_call" | custom-call | flops 1000 | bytes 1000 | tf_op jit(solution)/shard_map/pallas_call | solution.py:131
  246.3 13.2 %shard_map.265 = (bf16[8,512,128]{2,1,0:T(8,128)(2,1)}, bf16[8,1024,128]{2,1,0:T(8,128)(2,1)}, bf16[8,1024,128]{2,1,0:T(8,128)(2,1)}, f32[2,1024]{1,0:T(2,128)}) custom-call(s32[4]{0:T(128)} %pad_add_fusion.pos_ref, bf16[8,512,128]{2,1,0:T(8,128)(2,1)} %get-tuple-element.258.q_ref, bf16[8,1024,128]{2,1,0:T(8,128)(2,1)} %get-tuple-element.259.k_ref, ...), custom_call_target="tpu_custom_call" | custom-call | flops 1000 | bytes 1000 | tf_op jit(solution)/shard_map/pallas_call | solution.py:131
  260.0 10.7 %shard_map.266 = (bf16[2,2,256,640]{3,2,1,0:T(8,128)(2,1)}, bf16[2,2,256,640]{3,2,1,0:T(8,128)(2,1)}, bf16[2,2,256,640]{3,2,1,0:T(8,128)(2,1)}, bf16[2,2,256,640]{3,2,1,0:T(8,128)(2,1)}) custom-call(s32[4]{0:T(128)} %pad_add_fusion.pos_ref, bf16[512,1024]{1,0:T(8,128)(2,1)} %get-tuple-element.274.second_ref.refs_0_, ...), custom_call_target="tpu_custom_call" | custom-call | flops 1000 | bytes 1000 | tf_op jit(solution)/shard_map/pallas_call | solution.py:131
  280.4 13.2 %shard_map.268 = (bf16[8,512,128]{2,1,0:T(8,128)(2,1)}, bf16[8,1024,128]{2,1,0:T(8,128)(2,1)}, bf16[8,1024,128]{2,1,0:T(8,128)(2,1)}, f32[2,1024]{1,0:T(2,128)}) custom-call(s32[4]{0:T(128)} %pad_add_fusion.pos_ref, bf16[8,512,128]{2,1,0:T(8,128)(2,1)} %get-tuple-element.258.q_ref, ...), custom_call_target="tpu_custom_call", output_to_operand_aliasing={{0}: (9, {}), {1}: (10, {}), {2}: (11, {}), {3}: (12, {})} | custom-call | flops 1000 | bytes 1000 | tf_op jit(solution)/shard_map/pallas_call | solution.py:131
  293.6 8.4 %shard_map.269 = bf16[4,2,2,256,384]{4,3,2,1,0:T(8,128)(2,1)} custom-call(s32[4]{0:T(128)} %pad_add_fusion.pos_ref, bf16[1024,1024]{1,0:T(8,128)(2,1)} %fusion.5.first_ref.refs_0_, bf16[8,512,128]{2,1,0:T(8,128)(2,1)} %get-tuple-element.403.refs_1_.dq_ref, bf16[8,1024,128]{2,1,0:T(8,128)(2,1)} %get-tuple-element.404.refs_2_.dk_ref, ...), custom_call_target="tpu_custom_call" | custom-call | flops 1000 | bytes 1000 | tf_op jit(solution)/shard_map/pallas_call | solution.py:131
  311.8 8.6 %shard_map.273 = (bf16[512,1024]{1,0:T(8,128)(2,1)}, f32[2,1024]{1,0:T(2,128)}) custom-call(s32[4]{0:T(128)} %pad_add_fusion.pos_ref, bf16[8,1024,128]{2,1,0:T(8,128)(2,1)} %get-tuple-element.404.refs_2_.dk_ref, bf16[8,1024,128]{2,1,0:T(8,128)(2,1)} %get-tuple-element.405.refs_3_.dv_ref, bf16[512,1024]{1,0:T(8,128)(2,1)} %copy-done.2, ...), custom_call_target="tpu_custom_call" | custom-call | flops 1000 | bytes 1000 | tf_op jit(solution)/shard_map/pallas_call | solution.py:131
  323.2 9.1 %shard_map.272 = (bf16[2,2,256,384]{3,2,1,0:T(8,128)(2,1)}, bf16[2,2,256,384]{3,2,1,0:T(8,128)(2,1)}, bf16[2,2,256,384]{3,2,1,0:T(8,128)(2,1)}, bf16[2,2,256,384]{3,2,1,0:T(8,128)(2,1)}) custom-call(s32[4]{0:T(128)} %pad_add_fusion.pos_ref, bf16[1024,1024]{1,0:T(8,128)(2,1)} %fusion.5.first_ref.refs_0_, ...), custom_call_target="tpu_custom_call" | custom-call | flops 1000 | bytes 1000 | tf_op jit(solution)/shard_map/pallas_call | solution.py:131
  339.1 10.6 %shard_map.275 = (f32[512,1024]{1,0:T(8,128)}, f32[2,1024]{1,0:T(2,128)}) custom-call(s32[4]{0:T(128)} %pad_add_fusion.pos_ref, bf16[8,512,128]{2,1,0:T(8,128)(2,1)} %get-tuple-element.403.refs_1_.dq_ref, bf16[8,1024,128]{2,1,0:T(8,128)(2,1)} %get-tuple-element.404.refs_2_.dk_ref, bf16[8,1024,128]{2,1,0:T(8,128)(2,1)} %get-tuple-element.405.refs_3_.dv_ref, ...), custom_call_target="tpu_custom_call" | custom-call | flops 1000 | bytes 1000 | tf_op jit(solution)/shard_map/pallas_call | solution.py:131
  350.6 10.7 %shard_map.276 = bf16[512,1024]{1,0:T(8,128)(2,1)} custom-call(s32[4]{0:T(128)} %pad_add_fusion.pos_ref, bf16[512,4096]{1,0:T(8,128)(2,1)} %get-tuple-element.275.refs_1_.gelu_ref, f32[512,1024]{1,0:T(8,128)} %get-tuple-element.295.middle_ref, f32[1,1024]{1,0:T(1,128)} %bitcast.90, bf16[2,2,256,512]{3,2,1,0:T(8,128)(2,1)} %copy-done.5, ...), custom_call_target="tpu_custom_call" | custom-call | flops 1000 | bytes 1000 | tf_op jit(solution)/shard_map/pallas_call | solution.py:131
  374.9 9.2 %collective-permute-done.46 = f32[96,128]{1,0:T(8,128)S(1)} collective-permute-done((f32[96,128]{1,0:T(8,128)S(1)}, f32[96,128]{1,0:T(8,128)S(1)}, u32[]{:S(2)}, u32[]{:S(2)}) %collective-permute-start.46) | collective-permute-done | bytes 49184 | tf_op jit(solution)/shard_map/ppermute | solution.py:52
  385.8 7.3 %collective-permute-done.43.refs_2_ = bf16[256,640]{1,0:T(8,128)(2,1)S(1)} collective-permute-done((bf16[256,640]{1,0:T(8,128)(2,1)}, bf16[256,640]{1,0:T(8,128)(2,1)S(1)}, u32[]{:S(2)}, u32[]{:S(2)}) %collective-permute-start.43) | collective-permute-done | bytes 327712 | tf_op jit(solution)/shard_map/ppermute | solution.py:52
  401.5 6.1 %collective-permute-start.51 = (f32[96,128]{1,0:T(8,128)S(1)}, f32[96,128]{1,0:T(8,128)S(1)}, u32[]{:S(2)}, u32[]{:S(2)}) collective-permute-start(f32[96,128]{1,0:T(8,128)S(1)} %add.75), channel_id=1, source_target_pairs={{0,2},{2,0},{4,6},{6,4},{1,3},{3,1},{5,7},{7,5},{8,10},{10,8},{12,... | collective-permute-start | bytes 147464 | tf_op jit(solution)/shard_map/ppermute | solution.py:52
  421.1 7.6 %collective-permute-done.48.refs_2_ = bf16[256,384]{1,0:T(8,128)(2,1)S(1)} collective-permute-done((bf16[256,384]{1,0:T(8,128)(2,1)}, bf16[256,384]{1,0:T(8,128)(2,1)S(1)}, u32[]{:S(2)}, u32[]{:S(2)}) %collective-permute-start.48) | collective-permute-done | bytes 196640 | tf_op jit(solution)/shard_map/ppermute | solution.py:52
  (229 shorter events, 130.3 us)
Async XLA Ops:
  7.2 126.5 %all-gather.3.cloned.1.call-start = ((), (), s32[]{:S(2)}) async-start(), calls=%async_computation | async-start | bytes 10813440 | tf_op jit(solution)/shard_map/all_gather | solution.py:879
  9.0 35.6 %collective-permute-start.5 = (bf16[512,1024]{1,0:T(8,128)(2,1)}, bf16[512,1024]{1,0:T(8,128)(2,1)S(1)}, u32[]{:S(2)}, u32[]{:S(2)}) collective-permute-start(bf16[512,1024]{1,0:T(8,128)(2,1)} %tok_ref.3), channel_id=1, source_target_pairs={{0,1},{2,3},{4,5},{6,7},{8,9},{10,11},{12,13},{14,15},{16,17},{18,... | collective-permute-start | bytes 3145736 | tf_op jit(solution)/shard_map/ppermute | solution.py:883
  21.6 25.6 %collective-permute-start.1 = (bf16[2,256,384]{2,1,0:T(8,128)(2,1)S(1)}, bf16[2,256,384]{2,1,0:T(8,128)(2,1)}, u32[]{:S(2)}, u32[]{:S(2)}) collective-permute-start(bf16[2,256,384]{2,1,0:T(8,128)(2,1)S(1)} %get-tuple-element.501), channel_id=1, source_target_pairs={{0,1},{1,0},{2,3},{3,2},{4,5},{5,4},{6,7},{7,6},{8,9},{9,8},{10,11... | collective-permute-start | bytes 1179656 | tf_op jit(solution)/shard_map/ppermute | solution.py:52
  21.7 22.9 %collective-permute-start.3 = (bf16[256,384]{1,0:T(8,128)(2,1)S(1)}, bf16[256,384]{1,0:T(8,128)(2,1)S(1)}, u32[]{:S(2)}, u32[]{:S(2)}) collective-permute-start(bf16[256,384]{1,0:T(8,128)(2,1)S(1)} %copy.38), channel_id=1, source_target_pairs={{0,4},{2,6},{4,0},{6,2},{1,5},{3,7},{5,1},{7,3},{8,12},{10,14},{12... | collective-permute-start | bytes 589832 | tf_op jit(solution)/shard_map/ppermute | solution.py:52
  24.4 20.2 %collective-permute-start.4 = (bf16[256,384]{1,0:T(8,128)(2,1)S(1)}, bf16[256,384]{1,0:T(8,128)(2,1)S(1)}, u32[]{:S(2)}, u32[]{:S(2)}) collective-permute-start(bf16[256,384]{1,0:T(8,128)(2,1)S(1)} %copy.38), channel_id=1, source_target_pairs={{0,6},{2,4},{4,2},{6,0},{1,7},{3,5},{5,3},{7,1},{8,14},{10,12},{12... | collective-permute-start | bytes 589832 | tf_op jit(solution)/shard_map/ppermute | solution.py:52
  48.3 25.8 %collective-permute-start.2 = (bf16[2,2,256,384]{3,2,1,0:T(8,128)(2,1)S(1)}, bf16[2,2,256,384]{3,2,1,0:T(8,128)(2,1)}, u32[]{:S(2)}, u32[]{:S(2)}) collective-permute-start(bf16[2,2,256,384]{3,2,1,0:T(8,128)(2,1)S(1)} %pad_maximum_fusion.3.rest_0_), channel_id=1, source_target_pairs={{0,16},{16,0},{1,17},{17,1},{2,18},{18,2},{3,19},{19,3},{4,20},{20... | collective-permute-start | bytes 2359304 | tf_op jit(solution)/shard_map/ppermute | solution.py:52
  49.9 38.7 %collective-permute-start.8 = (bf16[2,2,256,384]{3,2,1,0:T(8,128)(2,1)S(1)}, bf16[2,2,256,384]{3,2,1,0:T(8,128)(2,1)}, u32[]{:S(2)}, u32[]{:S(2)}) collective-permute-start(bf16[2,2,256,384]{3,2,1,0:T(8,128)(2,1)S(1)} %pad_maximum_fusion.3.rest_0_), channel_id=1, source_target_pairs={{0,8},{8,0},{1,9},{9,1},{2,10},{10,2},{3,11},{11,3},{4,12},{12,4},... | collective-permute-start | bytes 2359304 | tf_op jit(solution)/shard_map/ppermute | solution.py:52
  58.3 20.9 %collective-permute-start.7 = (bf16[2,2,256,384]{3,2,1,0:T(8,128)(2,1)}, bf16[2,2,256,384]{3,2,1,0:T(8,128)(2,1)}, u32[]{:S(2)}, u32[]{:S(2)}) collective-permute-start(bf16[2,2,256,384]{3,2,1,0:T(8,128)(2,1)} %pad_maximum_fusion.4.rest_2_), channel_id=1, source_target_pairs={{0,1},{1,0},{2,3},{3,2},{4,5},{5,4},{6,7},{7,6},{8,9},{9,8},{10,11... | collective-permute-start | bytes 2359304 | tf_op jit(solution)/shard_map/ppermute | solution.py:52
  59.0 34.3 %collective-permute-start.10 = (bf16[2,2,256,384]{3,2,1,0:T(8,128)(2,1)}, bf16[2,2,256,384]{3,2,1,0:T(8,128)(2,1)}, u32[]{:S(2)}, u32[]{:S(2)}) collective-permute-start(bf16[2,2,256,384]{3,2,1,0:T(8,128)(2,1)} %pad_maximum_fusion.4.rest_2_), channel_id=1, source_target_pairs={{0,8},{8,0},{1,9},{9,1},{2,10},{10,2},{3,11},{11,3},{4,12},{12,4},... | collective-permute-start | bytes 2359304 | tf_op jit(solution)/shard_map/ppermute | solution.py:52
  79.7 50.3 %collective-permute-start.12 = (bf16[256,512]{1,0:T(8,128)(2,1)S(1)}, bf16[256,512]{1,0:T(8,128)(2,1)S(1)}, u32[]{:S(2)}, u32[]{:S(2)}) collective-permute-start(bf16[256,512]{1,0:T(8,128)(2,1)S(1)} %copy-done.25), channel_id=1, source_target_pairs={{0,2},{2,0},{4,6},{6,4},{1,3},{3,1},{5,7},{7,5},{8,10},{10,8},{12,... | collective-permute-start | bytes 786440 | tf_op jit(solution)/shard_map/ppermute | solution.py:52
  88.7 41.3 %collective-permute-start.13 = (bf16[256,512]{1,0:T(8,128)(2,1)S(1)}, bf16[256,512]{1,0:T(8,128)(2,1)S(1)}, u32[]{:S(2)}, u32[]{:S(2)}) collective-permute-start(bf16[256,512]{1,0:T(8,128)(2,1)S(1)} %copy-done.25), channel_id=1, source_target_pairs={{0,4},{2,6},{4,0},{6,2},{1,5},{3,7},{5,1},{7,3},{8,12},{10,14},{12... | collective-permute-start | bytes 786440 | tf_op jit(solution)/shard_map/ppermute | solution.py:52
  93.2 36.7 %collective-permute-start.14 = (bf16[256,512]{1,0:T(8,128)(2,1)S(1)}, bf16[256,512]{1,0:T(8,128)(2,1)S(1)}, u32[]{:S(2)}, u32[]{:S(2)}) collective-permute-start(bf16[256,512]{1,0:T(8,128)(2,1)S(1)} %copy-done.25), channel_id=1, source_target_pairs={{0,6},{2,4},{4,2},{6,0},{1,7},{3,5},{5,3},{7,1},{8,14},{10,12},{12... | collective-permute-start | bytes 786440 | tf_op jit(solution)/shard_map/ppermute | solution.py:52
  170.1 25.6 %collective-permute-start.19 = (bf16[2,2,256,512]{3,2,1,0:T(8,128)(2,1)S(1)}, bf16[2,2,256,512]{3,2,1,0:T(8,128)(2,1)S(1)}, u32[]{:S(2)}, u32[]{:S(2)}) collective-permute-start(bf16[2,2,256,512]{3,2,1,0:T(8,128)(2,1)S(1)} %pad_maximum_fusion.2.rest_2_), channel_id=1, source_target_pairs={{0,1},{1,0},{2,3},{3,2},{4,5},{5,4},{6,7},{7,6},{8,9},{9,8},{10,11... | collective-permute-start | bytes 3145736 | tf_op jit(solution)/shard_map/ppermute | solution.py:52
  171.4 25.5 %collective-permute-start.18 = (bf16[2,2,256,512]{3,2,1,0:T(8,128)(2,1)S(1)}, bf16[2,2,256,512]{3,2,1,0:T(8,128)(2,1)}, u32[]{:S(2)}, u32[]{:S(2)}) collective-permute-start(bf16[2,2,256,512]{3,2,1,0:T(8,128)(2,1)S(1)} %pad_maximum_fusion.1.rest_0_), channel_id=1, source_target_pairs={{0,16},{16,0},{1,17},{17,1},{2,18},{18,2},{3,19},{19,3},{4,20},{20... | collective-permute-start | bytes 3145736 | tf_op jit(solution)/shard_map/ppermute | solution.py:52
  172.0 25.9 %collective-permute-start.24 = (bf16[2,2,256,512]{3,2,1,0:T(8,128)(2,1)S(1)}, bf16[2,2,256,512]{3,2,1,0:T(8,128)(2,1)}, u32[]{:S(2)}, u32[]{:S(2)}) collective-permute-start(bf16[2,2,256,512]{3,2,1,0:T(8,128)(2,1)S(1)} %pad_maximum_fusion.2.rest_2_), channel_id=1, source_target_pairs={{0,8},{8,0},{1,9},{9,1},{2,10},{10,2},{3,11},{11,3},{4,12},{12,4},... | collective-permute-start | bytes 3145736 | tf_op jit(solution)/shard_map/ppermute | solution.py:52
  172.0 26.8 %collective-permute-start.22 = (bf16[2,2,256,512]{3,2,1,0:T(8,128)(2,1)S(1)}, bf16[2,2,256,512]{3,2,1,0:T(8,128)(2,1)}, u32[]{:S(2)}, u32[]{:S(2)}) collective-permute-start(bf16[2,2,256,512]{3,2,1,0:T(8,128)(2,1)S(1)} %pad_maximum_fusion.1.rest_0_), channel_id=1, source_target_pairs={{0,8},{8,0},{1,9},{9,1},{2,10},{10,2},{3,11},{11,3},{4,12},{12,4},... | collective-permute-start | bytes 3145736 | tf_op jit(solution)/shard_map/ppermute | solution.py:52
  197.3 42.5 %collective-permute-start.20 = (bf16[2,2,256,512]{3,2,1,0:T(8,128)(2,1)}, bf16[2,2,256,512]{3,2,1,0:T(8,128)(2,1)}, u32[]{:S(2)}, u32[]{:S(2)}) collective-permute-start(bf16[2,2,256,512]{3,2,1,0:T(8,128)(2,1)} %get-tuple-element.286), channel_id=1, source_target_pairs={{0,16},{16,0},{1,17},{17,1},{2,18},{18,2},{3,19},{19,3},{4,20},{20... | collective-permute-start | bytes 3145736 | tf_op jit(solution)/shard_map/ppermute | solution.py:52
  197.9 41.9 %collective-permute-start.21 = (bf16[2,2,256,512]{3,2,1,0:T(8,128)(2,1)}, bf16[2,2,256,512]{3,2,1,0:T(8,128)(2,1)S(1)}, u32[]{:S(2)}, u32[]{:S(2)}) collective-permute-start(bf16[2,2,256,512]{3,2,1,0:T(8,128)(2,1)} %get-tuple-element.288), channel_id=1, source_target_pairs={{0,1},{1,0},{2,3},{3,2},{4,5},{5,4},{6,7},{7,6},{8,9},{9,8},{10,11... | collective-permute-start | bytes 3145736 | tf_op jit(solution)/shard_map/ppermute | solution.py:52
  273.9 30.4 %collective-permute-start.29 = (bf16[2,2,256,640]{3,2,1,0:T(8,128)(2,1)}, bf16[2,2,256,640]{3,2,1,0:T(8,128)(2,1)}, u32[]{:S(2)}, u32[]{:S(2)}) collective-permute-start(bf16[2,2,256,640]{3,2,1,0:T(8,128)(2,1)} %get-tuple-element.343), channel_id=1, source_target_pairs={{0,16},{16,0},{1,17},{17,1},{2,18},{18,2},{3,19},{19,3},{4,20},{20... | collective-permute-start | bytes 3932168 | tf_op jit(solution)/shard_map/ppermute | solution.py:52
  275.0 30.5 %collective-permute-start.30 = (bf16[2,2,256,640]{3,2,1,0:T(8,128)(2,1)}, bf16[2,2,256,640]{3,2,1,0:T(8,128)(2,1)}, u32[]{:S(2)}, u32[]{:S(2)}) collective-permute-start(bf16[2,2,256,640]{3,2,1,0:T(8,128)(2,1)} %get-tuple-element.345), channel_id=1, source_target_pairs={{0,1},{1,0},{2,3},{3,2},{4,5},{5,4},{6,7},{7,6},{8,9},{9,8},{10,11... | collective-permute-start | bytes 3932168 | tf_op jit(solution)/shard_map/ppermute | solution.py:52
  276.0 26.0 %collective-permute-start.31 = (bf16[256,512]{1,0:T(8,128)(2,1)}, bf16[256,512]{1,0:T(8,128)(2,1)S(1)}, u32[]{:S(2)}, u32[]{:S(2)}) collective-permute-start(bf16[256,512]{1,0:T(8,128)(2,1)} %get-tuple-element.347), channel_id=1, source_target_pairs={{0,2},{2,0},{4,6},{6,4},{1,3},{3,1},{5,7},{7,5},{8,10},{10,8},{12,... | collective-permute-start | bytes 786440 | tf_op jit(solution)/shard_map/ppermute | solution.py:52
  276.1 26.0 %collective-permute-start.32 = (bf16[256,512]{1,0:T(8,128)(2,1)}, bf16[256,512]{1,0:T(8,128)(2,1)S(1)}, u32[]{:S(2)}, u32[]{:S(2)}) collective-permute-start(bf16[256,512]{1,0:T(8,128)(2,1)} %get-tuple-element.348), channel_id=1, source_target_pairs={{0,4},{2,6},{4,0},{6,2},{1,5},{3,7},{5,1},{7,3},{8,12},{10,14},{12... | collective-permute-start | bytes 786440 | tf_op jit(solution)/shard_map/ppermute | solution.py:52
  277.4 24.6 %collective-permute-start.33 = (bf16[256,512]{1,0:T(8,128)(2,1)}, bf16[256,512]{1,0:T(8,128)(2,1)S(1)}, u32[]{:S(2)}, u32[]{:S(2)}) collective-permute-start(bf16[256,512]{1,0:T(8,128)(2,1)} %get-tuple-element.349), channel_id=1, source_target_pairs={{0,6},{2,4},{4,2},{6,0},{1,7},{3,5},{5,3},{7,1},{8,14},{10,12},{12... | collective-permute-start | bytes 786440 | tf_op jit(solution)/shard_map/ppermute | solution.py:52
  310.1 22.2 %collective-permute-start.37 = (bf16[2,256,640]{2,1,0:T(8,128)(2,1)}, bf16[2,256,640]{2,1,0:T(8,128)(2,1)S(1)}, u32[]{:S(2)}, u32[]{:S(2)}) collective-permute-start(bf16[2,256,640]{2,1,0:T(8,128)(2,1)} %get-tuple-element.384), channel_id=1, source_target_pairs={{0,1},{1,0},{2,3},{3,2},{4,5},{5,4},{6,7},{7,6},{8,9},{9,8},{10,11... | collective-permute-start | bytes 1966088 | tf_op jit(solution)/shard_map/ppermute | solution.py:52
  311.2 21.1 %collective-permute-start.38 = (bf16[2,256,640]{2,1,0:T(8,128)(2,1)}, bf16[2,256,640]{2,1,0:T(8,128)(2,1)}, u32[]{:S(2)}, u32[]{:S(2)}) collective-permute-start(bf16[2,256,640]{2,1,0:T(8,128)(2,1)} %get-tuple-element.386), channel_id=1, source_target_pairs={{0,16},{16,0},{1,17},{17,1},{2,18},{18,2},{3,19},{19,3},{4,20},{20... | collective-permute-start | bytes 1966088 | tf_op jit(solution)/shard_map/ppermute | solution.py:52
  336.7 24.8 %collective-permute-start.35 = (bf16[2,2,256,384]{3,2,1,0:T(8,128)(2,1)}, bf16[2,2,256,384]{3,2,1,0:T(8,128)(2,1)S(1)}, u32[]{:S(2)}, u32[]{:S(2)}) collective-permute-start(bf16[2,2,256,384]{3,2,1,0:T(8,128)(2,1)} %get-tuple-element.380), channel_id=1, source_target_pairs={{0,16},{16,0},{1,17},{17,1},{2,18},{18,2},{3,19},{19,3},{4,20},{20... | collective-permute-start | bytes 2359304 | tf_op jit(solution)/shard_map/ppermute | solution.py:52
  338.1 23.3 %collective-permute-start.36 = (bf16[2,2,256,384]{3,2,1,0:T(8,128)(2,1)}, bf16[2,2,256,384]{3,2,1,0:T(8,128)(2,1)S(1)}, u32[]{:S(2)}, u32[]{:S(2)}) collective-permute-start(bf16[2,2,256,384]{3,2,1,0:T(8,128)(2,1)} %get-tuple-element.382), channel_id=1, source_target_pairs={{0,1},{1,0},{2,3},{3,2},{4,5},{5,4},{6,7},{7,6},{8,9},{9,8},{10,11... | collective-permute-start | bytes 2359304 | tf_op jit(solution)/shard_map/ppermute | solution.py:52
  367.3 25.8 %collective-permute-start.43 = (bf16[256,640]{1,0:T(8,128)(2,1)}, bf16[256,640]{1,0:T(8,128)(2,1)S(1)}, u32[]{:S(2)}, u32[]{:S(2)}) collective-permute-start(bf16[256,640]{1,0:T(8,128)(2,1)} %get-tuple-element.433), channel_id=1, source_target_pairs={{0,4},{2,6},{4,0},{6,2},{1,5},{3,7},{5,1},{7,3},{8,12},{10,14},{12... | collective-permute-start | bytes 983048 | tf_op jit(solution)/shard_map/ppermute | solution.py:52
  368.8 24.4 %collective-permute-start.44 = (bf16[256,640]{1,0:T(8,128)(2,1)}, bf16[256,640]{1,0:T(8,128)(2,1)S(1)}, u32[]{:S(2)}, u32[]{:S(2)}) collective-permute-start(bf16[256,640]{1,0:T(8,128)(2,1)} %get-tuple-element.434), channel_id=1, source_target_pairs={{0,6},{2,4},{4,2},{6,0},{1,7},{3,5},{5,3},{7,1},{8,14},{10,12},{12... | collective-permute-start | bytes 983048 | tf_op jit(solution)/shard_map/ppermute | solution.py:52
  371.8 25.7 %collective-permute-start.40 = (bf16[2,256,384]{2,1,0:T(8,128)(2,1)}, bf16[2,256,384]{2,1,0:T(8,128)(2,1)S(1)}, u32[]{:S(2)}, u32[]{:S(2)}) collective-permute-start(bf16[2,256,384]{2,1,0:T(8,128)(2,1)} %get-tuple-element.428), channel_id=1, source_target_pairs={{0,1},{1,0},{2,3},{3,2},{4,5},{5,4},{6,7},{7,6},{8,9},{9,8},{10,11... | collective-permute-start | bytes 1179656 | tf_op jit(solution)/shard_map/ppermute | solution.py:52
  372.8 24.8 %collective-permute-start.41 = (bf16[2,256,384]{2,1,0:T(8,128)(2,1)}, bf16[2,256,384]{2,1,0:T(8,128)(2,1)S(1)}, u32[]{:S(2)}, u32[]{:S(2)}) collective-permute-start(bf16[2,256,384]{2,1,0:T(8,128)(2,1)} %get-tuple-element.430), channel_id=1, source_target_pairs={{0,16},{16,0},{1,17},{17,1},{2,18},{18,2},{3,19},{19,3},{4,20},{20... | collective-permute-start | bytes 1179656 | tf_op jit(solution)/shard_map/ppermute | solution.py:52
  384.1 44.5 %collective-permute-start.50 = (bf16[512,1024]{1,0:T(8,128)(2,1)}, bf16[512,1024]{1,0:T(8,128)(2,1)}, u32[]{:S(2)}, u32[]{:S(2)}) collective-permute-start(bf16[512,1024]{1,0:T(8,128)(2,1)} %get-tuple-element.458), channel_id=1, source_target_pairs={{1,0},{3,2},{5,4},{7,6},{9,8},{11,10},{13,12},{15,14},{17,16},{19,... | collective-permute-start | bytes 3145736 | tf_op jit(solution)/shard_map/ppermute | solution.py:1011
  (63 other events, 672.5 us)
Sparse Core Ops, SparseCore 0:
  11.5 122.1 all-gather.2

commit v3 on v2

--- a/solution.py
+++ b/solution.py
@@ -66,11 +66,13 @@
         self.top, self.low = pieces[:near], pieces[near:]
 
     def two(self):
+        lay = self.lay
         self.top = around(jnp.stack(self.top), "tx", 2)
-        self.low = around(jnp.stack(self.low), "fy", self.lay.ny)
+        self.low = around(jnp.stack(self.low), "fy", lay.ny)
 
     def three(self):
-        self.top = around(jnp.stack(self.top), "fy", self.lay.ny)
+        lay = self.lay
+        self.top = around(jnp.stack(self.top), "fy", lay.ny)
         self.low = around(jnp.stack(self.low), "tx", 2)
 
     def swap(self, which):
@@ -78,10 +80,8 @@
             self.twin = [trade(self.top[0], "c", 2, 1), trade(self.low[0], "c", 2, 1)]
         else:
             late = [trade(t, "c", 2, 1) for t in self.top[1:] + self.low[1:]]
-            ny = self.lay.ny
-            self.parts = self.top + self.low + [
-                self.twin[0], *late[: ny - 1], self.twin[1], *late[ny - 1 :]
-            ]
+            n = len(self.top) - 1
+            self.parts = self.top + self.low + [self.twin[0], *late[:n], self.twin[1], *late[n:]]
 
 
 def stage(*things):
@@ -98,26 +98,44 @@
     return back[0] if len(back) == 1 else back
 
 
-def start_loads(lay, pos, refs, wants, sem):
+def start_loads(lay, pos, refs, wants, sem, dz):
+    half = len(refs) // 2
+    for dx in range(2):
+        k = lay.z_block(pos, dz) * 2 + lay.x_block(pos, dx)
+        for dc in range(2):
+            mine = refs[dc * half : (dc + 1) * half]
+            for dy in range(lay.ny):
+                start = lay.row_start(pos, dy, dc)
+                if len(refs) == 1:
+                    block = refs[0].at[start // lay.rows * (2 * lay.nz) + k]
+                elif dz < lay.near:
+                    block = mine[dy].at[dx, dz]
+                else:
+                    block = mine[lay.ny + dx].at[dy, dz - lay.near]
+                for i, (first, width, whole) in enumerate(wants):
+                    pltpu.make_async_copy(
+                        block.at[:, pl.ds(first, width)],
+                        whole.at[pl.ds(start, lay.rows), pl.ds(aligned(k * width, width), width)],
+                        sem.at[dz, i],
+                    ).start()
+
+
+def stream_loads(lay, pos, refs, wants, sem):
+    step = pl.program_id(0)
     for dz in range(lay.nz):
-        for dx in range(2):
-            k = lay.z_block(pos, dz) * 2 + lay.x_block(pos, dx)
-            for dc in range(2):
-                mine = refs[dc * (lay.ny + 2) : (dc + 1) * (lay.ny + 2)]
-                for dy in range(lay.ny):
-                    start = lay.row_start(pos, dy, dc)
-                    if len(refs) == 1:
-                        block = refs[0].at[start // lay.rows * (2 * lay.nz) + k]
-                    elif dz < lay.near:
-                        block = mine[dy].at[dx, dz]
-                    else:
-                        block = mine[lay.ny + dx].at[dy, dz - lay.near]
-                    for i, (first, width, whole) in enumerate(wants):
-                        pltpu.make_async_copy(
-                            block.at[:, pl.ds(first, width)],
-                            whole.at[pl.ds(start, lay.rows), pl.ds(aligned(k * width, width), width)],
-                            sem.at[dz, i],
-                        ).start()
+
+        @pl.when(step == max(dz - 2, 0))
+        def _(dz=dz):
+            start_loads(lay, pos, refs, wants, sem, dz)
+
+    wait_loads(lay, pos, step, wants, sem)
+
+
+def all_loads(lay, pos, refs, wants, sem):
+    for dz in range(lay.nz):
+        start_loads(lay, pos, refs, wants, sem, dz)
+    for dz in range(lay.nz):
+        wait_loads(lay, pos, dz, wants, sem)
 
 
 def wait_loads(lay, pos, dz, wants, sem):
@@ -127,7 +145,7 @@
         pltpu.make_async_copy(cols, cols, sem.at[dz, i]).wait()
 
 
-def kernel_call(body, pos, grid, ins, in_specs, outs, out_specs, scratch, aliases={}):
+def kernel_call(body, pos, grid, ins, in_specs, outs, out_specs, scratch, aliases={}, room=60):
     return pl.pallas_call(
         body,
         out_shape=outs,
@@ -140,7 +158,7 @@
         ),
         input_output_aliases=aliases,
         compiler_params=pltpu.CompilerParams(
-            dimension_semantics=("arbitrary",) * len(grid), vmem_limit_bytes=60 * MIB
+            dimension_semantics=("arbitrary",) * len(grid), vmem_limit_bytes=room * MIB
         ),
         cost_estimate=pl.CostEstimate(flops=1000, bytes_accessed=1000, transcendentals=0),
     )(pos, *ins)
@@ -195,11 +213,7 @@
         wants = ((0, width, whole_q), (width, 2 * width, whole_kv))
         dz = pl.program_id(0)
 
-        @pl.when(dz == 0)
-        def _():
-            start_loads(lay, pos_ref, refs, wants, sem)
-
-        wait_loads(lay, pos_ref, dz, wants, sem)
+        stream_loads(lay, pos_ref, refs, wants, sem)
         z = z_place(dz, pos_ref)
         kv = dot(first_ref[...], whole_kv[:, pl.ds(aligned(z * 4 * width, width), 4 * width)])
         q = dot(first_ref[rows:], whole_q[:, pl.ds(aligned(z * 2 * width, width), 2 * width)])
@@ -301,9 +315,7 @@
     def body(pos_ref, mixed_ref, tok_ref, bias_ref, gain_ref, shift_ref, *rest):
         refs, (middle_ref, second_ref, whole, sem) = rest[:n], rest[n:]
         wants = ((first, width, whole),)
-        start_loads(lay, pos_ref, refs, wants, sem)
-        for dz in range(lay.nz):
-            wait_loads(lay, pos_ref, dz, wants, sem)
+        all_loads(lay, pos_ref, refs, wants, sem)
         branch = dot_nt(mixed_ref[...], whole[...])
         middle = tok_ref[...].astype(F32) + branch + bias_ref[...]
         middle_ref[...] = middle
@@ -331,11 +343,7 @@
         wants = ((0, width, whole),)
         dz = pl.program_id(0)
 
-        @pl.when(dz == 0)
-        def _():
-            start_loads(lay, pos_ref, refs, wants, sem)
-
-        wait_loads(lay, pos_ref, dz, wants, sem)
+        stream_loads(lay, pos_ref, refs, wants, sem)
         z = z_place(dz, pos_ref)
         for x in range(2):
             here = slice(x * width, (x + 1) * width)
@@ -371,12 +379,12 @@
         wants = ((0, width, whole),)
         dz = pl.program_id(0)
 
+        stream_loads(lay, pos_ref, refs, wants, sem)
+
         @pl.when(dz == 0)
         def _():
-            start_loads(lay, pos_ref, refs, wants, sem)
             acc[...] = middle_ref[...] + bias_ref[...]
 
-        wait_loads(lay, pos_ref, dz, wants, sem)
         cols = pl.ds(aligned(z_place(dz, pos_ref) * 2 * width, width), 2 * width)
         acc[...] += dot_nt(gelu_ref[...], whole[:, cols])
 
@@ -410,11 +418,7 @@
         wants = ((0, width, whole),)
         dz = pl.program_id(0)
 
-        @pl.when(dz == 0)
-        def _():
-            start_loads(lay, pos_ref, refs, wants, sem)
-
-        wait_loads(lay, pos_ref, dz, wants, sem)
+        stream_loads(lay, pos_ref, refs, wants, sem)
         cols = pl.ds(aligned(z_place(dz, pos_ref) * 2 * width, width), 2 * width)
         pre = (dot(grad_ref[...], whole[:, cols]) * slope_ref[...].astype(F32)).astype(BF)
         pre_ref[...] = pre
@@ -442,12 +446,12 @@
         wants = ((0, width, whole),)
         dz = pl.program_id(0)
 
+        stream_loads(lay, pos_ref, refs, wants, sem)
+
         @pl.when(dz == 0)
         def _():
-            start_loads(lay, pos_ref, refs, wants, sem)
             acc[...] = jnp.zeros_like(acc)
 
-        wait_loads(lay, pos_ref, dz, wants, sem)
         cols = pl.ds(aligned(z_place(dz, pos_ref) * 2 * width, width), 2 * width)
         acc[...] += dot_nt(pre_ref[...], whole[:, cols])
 
@@ -488,9 +492,7 @@
     def body(pos_ref, low_ref, *rest):
         refs, (out_ref, whole, sem) = rest[:n], rest[n:]
         wants = ((first, width, whole),)
-        start_loads(lay, pos_ref, refs, wants, sem)
-        for dz in range(lay.nz):
-            wait_loads(lay, pos_ref, dz, wants, sem)
+        all_loads(lay, pos_ref, refs, wants, sem)
         out_ref[...] = dot(low_ref[...], whole[...]).astype(BF)
 
     return kernel_call(
@@ -591,22 +593,22 @@
     return [ref[x, here] for x in range(2)]
 
 
-def first_grad_prev_call(lay, pos, dk, dv, tokens, weights, width):
+def first_grad_prev_call(lay, pos, dk, dv, tokens, gain, weights, width):
     rows, dim = tokens.shape
     blocks = 2 * lay.nz
     n = len(weights)
 
-    def body(pos_ref, dk_ref, dv_ref, tok_ref, *rest):
+    def body(pos_ref, dk_ref, dv_ref, tok_ref, gain_ref, *rest):
         refs, (grad_ref, sums_ref, whole, acc, sem) = rest[:n], rest[n:]
         wants = ((width, 2 * width, whole),)
         dz = pl.program_id(0)
 
+        stream_loads(lay, pos_ref, refs, wants, sem)
+
         @pl.when(dz == 0)
         def _():
-            start_loads(lay, pos_ref, refs, wants, sem)
             acc[...] = jnp.zeros_like(acc)
 
-        wait_loads(lay, pos_ref, dz, wants, sem)
         keys, values = sides(dk_ref, 0, rows), sides(dv_ref, 0, rows)
         part = jnp.concatenate([keys[0], values[0], keys[1], values[1]], axis=1)
         cols = pl.ds(aligned(z_place(dz, pos_ref) * 4 * width, width), 4 * width)
@@ -615,8 +617,8 @@
         @pl.when(dz == lay.nz - 1)
         def _():
             grad = acc[...]
-            grad_ref[...] = grad.astype(BF)
-            unit = norm_parts(tok_ref[...].astype(F32))[0]
+            unit, inverse = norm_parts(tok_ref[...].astype(F32))
+            grad_ref[...] = norm_backward(grad, unit, inverse, gain_ref[...]).astype(BF)
             sums_ref[0:1] = jnp.sum(grad * unit, axis=0, keepdims=True)
             sums_ref[1:2] = jnp.sum(grad, axis=0, keepdims=True)
 
@@ -625,8 +627,8 @@
         body,
         pos,
         (lay.nz,),
-        (dk, dv, tokens, *weights),
-        [both, both, full((rows, dim))] + [ANY] * n,
+        (dk, dv, tokens, gain, *weights),
+        [both, both, full((rows, dim)), full((1, dim))] + [ANY] * n,
         [shape((rows, dim), BF), shape((2, dim), F32)],
         [full((rows, dim)), full((2, dim))],
         [
@@ -637,22 +639,22 @@
     )
 
 
-def first_grad_own_call(lay, pos, dq, dk, dv, tokens, weights, width):
+def first_grad_own_call(lay, pos, dq, dk, dv, tokens, middle_grad, gain, weights, width):
     rows, dim = tokens.shape
     blocks = 2 * lay.nz
     n = len(weights)
 
-    def body(pos_ref, dq_ref, dk_ref, dv_ref, tok_ref, *rest):
+    def body(pos_ref, dq_ref, dk_ref, dv_ref, tok_ref, middle_ref, gain_ref, *rest):
         refs, (grad_ref, sums_ref, whole_q, whole_kv, sem) = rest[:n], rest[n:]
         wants = ((0, width, whole_q), (width, 2 * width, whole_kv))
         dz = pl.program_id(0)
 
+        stream_loads(lay, pos_ref, refs, wants, sem)
+
         @pl.when(dz == 0)
         def _():
-            start_loads(lay, pos_ref, refs, wants, sem)
             grad_ref[...] = jnp.zeros_like(grad_ref)
 
-        wait_loads(lay, pos_ref, dz, wants, sem)
         z = z_place(dz, pos_ref)
         keys, values = sides(dk_ref, 1, rows), sides(dv_ref, 1, rows)
         part = jnp.concatenate([keys[0], values[0], keys[1], values[1]], axis=1)
@@ -664,17 +666,21 @@
         @pl.when(dz == lay.nz - 1)
         def _():
             grad = grad_ref[...]
-            unit = norm_parts(tok_ref[...].astype(F32))[0]
+            unit, inverse = norm_parts(tok_ref[...].astype(F32))
             sums_ref[0:1] = jnp.sum(grad * unit, axis=0, keepdims=True)
             sums_ref[1:2] = jnp.sum(grad, axis=0, keepdims=True)
+            grad_ref[...] = middle_ref[...] + norm_backward(grad, unit, inverse, gain_ref[...])
 
     both = at_lead(2, 2 * rows, width, place=z_place)
     return kernel_call(
         body,
         pos,
         (lay.nz,),
-        (dq, dk, dv, tokens, *weights),
-        [at_lead(2, rows, width, place=z_place), both, both, full((rows, dim))] + [ANY] * n,
+        (dq, dk, dv, tokens, middle_grad, gain, *weights),
+        [at_lead(2, rows, width, place=z_place), both, both]
+        + [full((rows, dim))] * 2
+        + [full((1, dim))]
+        + [ANY] * n,
         [shape((rows, dim), F32), shape((2, dim), F32)],
         [full((rows, dim)), full((2, dim))],
         [
@@ -772,7 +778,7 @@
         build(sums, given)
 
     return kernel_call(
-        body, pos, (steps,), flat, [spec(r) for r in flat], outs, [spec(o) for o in outs], []
+        body, pos, (steps,), flat, [spec(r) for r in flat], outs, [spec(o) for o in outs], [], {}, 63
     )
 
 
@@ -830,14 +836,15 @@
         self.top = [self.top[0]] + [trade(self.top[d], "tz", self.lay.nz, d) for d in range(1, self.lay.nz)]
 
     def sum_three(self, cuts):
-        outs = [shape((self.lay.rows, *c) if isinstance(c, tuple) else (self.lay.rows, c), F32) for c in cuts]
+        rows = self.lay.rows
+        outs = [shape((c[0], rows, c[1]) if isinstance(c, tuple) else (rows, c), F32) for c in cuts]
 
         def build(sums, given):
             at = 0
             for ref, c in zip(given, cuts):
                 if isinstance(c, tuple):
                     for i in range(c[0]):
-                        ref[:, i, :] = sums[0]((slice(None), slice(at, at + c[1])))
+                        ref[i] = sums[0]((slice(None), slice(at, at + c[1])))
                         at += c[1]
                 else:
                     ref[...] = sums[0]((slice(None), slice(at, at + c)))
@@ -881,7 +888,7 @@
     down = Gather(lay, w_down)
     qkv.one()
     tokens_prev = lax.ppermute(tokens, "tx", [(0, 1)])
-    qkv.low, tokens_prev = stage(qkv.low, tokens_prev)
+    tokens_prev = stage(qkv, tokens_prev)
     qkv.two()
     qkv.three()
     qkv.swap(0)
@@ -921,12 +928,15 @@
         lay, pos, hidden, (0,), down_tile, (grad_out, gelu), [whole(grad_out), at_z(hidden)]
     )
     grad_down.away()
+    grad_down.sent, slope, down.twin = stage(down, grad_down.sent, slope, down.twin)
+    down.swap(1)
+    slope, down.parts, grad_down.sent = stage(slope, down.parts, grad_down.sent)
     grad_down.swap()
+    pre, grad_b_up = pre_call(lay, pos, slope, grad_out, down.parts, hidden)
+    grad_down.received, pre = stage(grad_down.received, pre)
     grad_down.own()
-    slope = stage(grad_down, down, slope)
-    down.swap(1)
+    pre = stage(grad_down, pre)
     grad_down.send_one()
-    pre, grad_b_up = pre_call(lay, pos, slope, grad_out, down.parts, hidden)
     middle_grad, middle_low, sums2 = second_back_call(
         lay, pos, pre, grad_out, middle, row(ln2_gain), up_parts, hidden
     )
@@ -961,7 +971,6 @@
     dq, dk, dv, sums_qv = attend_back_call(
         pos, (half, blocks), query, key, value, seg_k, seg_q, lse, mixed_grad, exact, partial
     )
-    back, sums_prev = first_grad_prev_call(lay, pos, dk, dv, tokens_prev, qkv.parts, width)
 
     def qkv_tile(left, ins, xs):
         late = left[0][:, rows:]
@@ -987,48 +996,56 @@
     grad_qkv.sent, dq, dk, dv = stage(grad_up, grad_qkv.sent, dq, dk, dv)
     grad_up.send_two()
     grad_qkv.swap()
-    grad_down.sum_three((hidden,))
-    grad_qkv.received, dq, dk, dv, grad_down.out = stage(grad_qkv.received, dq, dk, dv, grad_down.out)
+    back, sums_prev = first_grad_prev_call(
+        lay, pos, dk, dv, tokens_prev, row(ln1_gain), qkv.parts, width
+    )
+    grad_qkv.received, dq, dk, dv, back, sums_prev = stage(
+        grad_qkv.received, dq, dk, dv, back, sums_prev
+    )
     grad_qkv.own()
-    dq, dk, dv, sums_prev = stage(grad_qkv, dq, dk, dv, sums_prev)
+    dq, dk, dv, gelu = stage(grad_qkv, grad_up, dq, dk, dv, gelu)
     grad_qkv.send_one()
-    dq, dk, dv, sums_prev = stage(grad_up, dq, dk, dv, sums_prev)
     grad_up.sum_two()
-    dq, dk, dv, sums_prev = stage(grad_up, dq, dk, dv, sums_prev)
+    gelu, dq, dk, dv = stage(grad_up, gelu, dq, dk, dv)
     grad_up.send_three()
-    first_grad, sums1 = first_grad_own_call(lay, pos, dq, dk, dv, tokens, qkv.parts, width)
+    first_grad, sums1 = first_grad_own_call(
+        lay, pos, dq, dk, dv, tokens, middle_grad, row(ln1_gain), qkv.parts, width
+    )
+    result = result_call(lay, pos, gelu, middle, row(b_down), down.parts, hidden)
     small = jnp.concatenate(
         [v.reshape(-1) for v in (sums2, grad_b_up, sums1 + sums_prev, sums_qv)]
     ).reshape(-1, 128)
-    small = small + trade(small, "c", 2, 1)
-    result = result_call(lay, pos, gelu, middle, row(b_down), down.parts, hidden)
-    first_grad, small, result, back = stage(grad_qkv, first_grad, small, result, back)
+    small, first_grad, result, back = stage(grad_qkv, grad_up, small, first_grad, result, back)
     grad_qkv.sum_one()
-    first_grad, small, back = stage(grad_qkv, first_grad, small, back)
-    small = small + trade(small, "tx", 2, 1)
+    small, back = stage(grad_qkv, small, back)
     grad_qkv.send_two()
-    small, back = stage(small, back)
+    grad_down.sum_three((hidden,))
+    both_cores = [((c, x), (c ^ 1, x ^ 1)) for c in range(2) for x in range(2)]
+    both_cores = [(s[0] * 2 + s[1], t[0] * 2 + t[1]) for s, t in both_cores]
+    pieces = [
+        small,
+        trade(small, "c", 2, 1),
+        trade(small, "tx", 2, 1),
+        lax.ppermute(small, ("c", "tx"), both_cores),
+    ]
+    pieces, back, grad_down.out = stage(grad_qkv, pieces, back, grad_down.out)
+    small = (pieces[0] + pieces[1]) + (pieces[2] + pieces[3])
+    grad_qkv.sum_two()
+    small, back = stage(grad_qkv, small, back)
+    grad_qkv.send_three()
+    pieces = around(small, "fy", ny)
     back = lax.ppermute(back, "tx", [(1, 0)])
-    small = sum(around(small, "fy", ny))
-    small = stage(grad_up, small)
     grad_up.sum_three((hidden, width))
-    small, grad_up.out = stage(grad_qkv, small, grad_up.out)
-    grad_qkv.sum_two()
-    small = stage(grad_qkv, small)
-    small = around(small, "tz", nz)
-    grad_qkv.send_three()
-    back = stage(grad_qkv, back)
-    small = sum(small).reshape(-1)
+    pieces, grad_up.out = stage(grad_qkv, pieces, grad_up.out)
+    small = sum(around(sum(pieces), "tz", nz)).reshape(-1)
+    token_grad = (first_grad + back.astype(F32)).astype(BF)
     grad_qkv.sum_three(((3, width),))
-    unit, inverse = norm_parts(tokens.astype(F32))
-    first_grad = first_grad + back.astype(F32)
-    token_grad = (middle_grad + norm_backward(first_grad, unit, inverse, ln1_gain)).astype(BF)
     at = 4 * dim
     late = small[at + gelu.shape[1] :]
     return (
         result,
         token_grad,
-        grad_qkv.out[0],
+        jnp.transpose(grad_qkv.out[0], (1, 0, 2)),
         late[2 * dim :].reshape(2, -1),
         grad_up.out[1],
         small[2 * dim : 3 * dim],

time: 451 us -> 427 us (0.947)
  starting transfers between devices: 70.9 us -> 58.3 us
  waiting for transfers between devices: 106 us -> 98 us
    ppermute x52, starting transfers between devices: 64.7 us -> 52.1 us  [trade(): return lax.ppermute(value, axis, [(s, s ^ distance) for s in range(size)])]
    ppermute x52, waiting for transfers between devices: 102 us -> 91.8 us  [trade(): return lax.ppermute(value, axis, [(s, s ^ distance) for s in range(size)])]
    unnamed x83 -> x68, local copies, waits for them, and re-layouts: 10.2 us -> 8.7 us
  transfers between devices with their start and end apart: 55 -> 56, of which waited for: 21 -> 21; matrix products, arithmetic and copies ran while one was open for 4% -> 3% of each run, Pallas kernels for 38% -> 44%
where the time goes in v3:
time: 427 us; the launch traced here: 423 us
  Pallas kernels  224 us (52%)
  waiting for transfers between devices  98 us (23%)
  starting transfers between devices  58.3 us (14%)
  between operations  14.8 us (3%)
  other arithmetic  14.6 us (3%)
  local copies, waits for them, and re-layouts  12.5 us (3%)
    pallas_call x27, Pallas kernels, kernel_call(): pl.pallas_call(body, out_shape=outs, grid_spec=pltpu.PrefetchScalarGridSp...  224 us
    ppermute x52, waiting for transfers between devices, trade(): return lax.ppermute(value, axis, [(s, s ^ distance) for s in range(size)])  91.8 us
    ppermute x52, starting transfers between devices, trade(): return lax.ppermute(value, axis, [(s, s ^ distance) for s in range(size)])  52.1 us
    unnamed x68, local copies, waits for them, and re-layouts  8.7 us
  transfers between devices with their start and end apart: 56, of which 21 were waited for; matrix products, arithmetic and copies ran while one was open for 3% of the time, Pallas kernels for 44%

profile of v3, /device:TPU:0, one launch (start us, length us, event | category | flops | bytes accessed | tf_op | source)
XLA Modules:
  0.0 422.5 jit_solution(12543084770111091299)
XLA Ops:
  9.1 4.9 %collective-permute-start.3 = (bf16[512,1024]{1,0:T(8,128)(2,1)}, bf16[512,1024]{1,0:T(8,128)(2,1)S(1)}, u32[]{:S(2)}, u32[]{:S(2)}) collective-permute-start(bf16[512,1024]{1,0:T(8,128)(2,1)} %tok_ref.3), channel_id=1, source_target_pairs={{0,1},{2,3},{4,5},{6,7},{8,9},{10,11},{12,13},{14,15},{16,17},{18,... | collective-permute-start | bytes 3145736 | tf_op jit(solution)/shard_map/ppermute | solution.py:890
  15.2 3.7 collective-permute-start.2
  20.5 4.5 %collective-permute-done.2 = bf16[256,384]{1,0:T(8,128)(2,1)S(1)} collective-permute-done((bf16[256,384]{1,0:T(8,128)(2,1)S(1)}, bf16[256,384]{1,0:T(8,128)(2,1)S(1)}, u32[]{:S(2)}, u32[]{:S(2)}) %collective-permute-start.2) | collective-permute-done | bytes 196640 | tf_op jit(solution)/shard_map/ppermute | solution.py:52
  25.0 17.3 %collective-permute-done.1 = bf16[256,384]{1,0:T(8,128)(2,1)S(1)} collective-permute-done((bf16[256,384]{1,0:T(8,128)(2,1)S(1)}, bf16[256,384]{1,0:T(8,128)(2,1)S(1)}, u32[]{:S(2)}, u32[]{:S(2)}) %collective-permute-start.1) | collective-permute-done | bytes 196640 | tf_op jit(solution)/shard_map/ppermute | solution.py:52
  44.7 12.8 %collective-permute-done.6 = bf16[2,256,384]{2,1,0:T(8,128)(2,1)S(1)} collective-permute-done((bf16[2,256,384]{2,1,0:T(8,128)(2,1)S(1)}, bf16[2,256,384]{2,1,0:T(8,128)(2,1)S(1)}, u32[]{:S(2)}, u32[]{:S(2)}) %collective-permute-start.6) | collective-permute-done | bytes 393248 | tf_op jit(solution)/shard_map/ppermute | solution.py:52
  57.6 6.7 %collective-permute-done.4 = bf16[2,256,384]{2,1,0:T(8,128)(2,1)S(1)} collective-permute-done((bf16[2,256,384]{2,1,0:T(8,128)(2,1)S(1)}, bf16[2,256,384]{2,1,0:T(8,128)(2,1)S(1)}, u32[]{:S(2)}, u32[]{:S(2)}) %collective-permute-start.4) | collective-permute-done | bytes 393248 | tf_op jit(solution)/shard_map/ppermute | solution.py:52
  69.6 13.1 %collective-permute-done.7.rest_3_ = bf16[2,2,256,384]{3,2,1,0:T(8,128)(2,1)} collective-permute-done((bf16[2,2,256,384]{3,2,1,0:T(8,128)(2,1)S(1)}, bf16[2,2,256,384]{3,2,1,0:T(8,128)(2,1)}, u32[]{:S(2)}, u32[]{:S(2)}) %collective-permute-start.7) | collective-permute-done | bytes 786464 | tf_op jit(solution)/shard_map/ppermute | solution.py:52
  83.9 4.3 %collective-permute-start.12 = (bf16[256,512]{1,0:T(8,128)(2,1)S(1)}, bf16[256,512]{1,0:T(8,128)(2,1)}, u32[]{:S(2)}, u32[]{:S(2)}) collective-permute-start(bf16[256,512]{1,0:T(8,128)(2,1)S(1)} %copy-done.20), channel_id=1, source_target_pairs={{0,2},{2,0},{4,6},{6,4},{1,3},{3,1},{5,7},{7,5},{8,10},{10,8},{12,... | collective-permute-start | bytes 786440 | tf_op jit(solution)/shard_map/ppermute | solution.py:52
  91.6 11.4 %shard_map.254 = (bf16[8,512,128]{2,1,0:T(8,128)(2,1)}, bf16[8,1024,128]{2,1,0:T(8,128)(2,1)}, bf16[8,1024,128]{2,1,0:T(8,128)(2,1)}) custom-call(s32[4]{0:T(128)} %pad_add_fusion.pos_ref, bf16[1024,1024]{1,0:T(8,128)(2,1)} %fusion.5.first_ref.refs_0_, f32[1,1024]{1,0:T(1,128)} %get-tuple-element.517.bq_ref, f32[1,1024]{1,0:T(1,128)} %get-tuple-element.516.bv_ref, ...), custom_call_target="tpu_custom_call" | custom-call | flops 1000 | bytes 1000 | tf_op jit(solution)/shard_map/pallas_call | solution.py:149
  103.0 20.6 %shard_map.255 = (bf16[512,1024]{1,0:T(8,128)(2,1)}, f32[512,1024]{1,0:T(8,128)}, f32[8,2,512]{2,1,0:T(2,128)}) custom-call(s32[4]{0:T(128)} %pad_add_fusion.pos_ref, bf16[8,512,128]{2,1,0:T(8,128)(2,1)} %get-tuple-element.278.q_ref, bf16[8,1024,128]{2,1,0:T(8,128)(2,1)} %get-tuple-element.279.k_ref, bf16[8,1024,128]{2,1,0:T(8,128)(2,1)} %get-tuple-element.280.v_ref, ...), custom_call_target="tpu_custom_call" | custom-call | flops 1000 | bytes 1000 | tf_op jit(solution)/shard_map/pallas_call | solution.py:149
  123.6 5.8 %collective-permute-done.13 = bf16[256,512]{1,0:T(8,128)(2,1)S(1)} collective-permute-done((bf16[256,512]{1,0:T(8,128)(2,1)S(1)}, bf16[256,512]{1,0:T(8,128)(2,1)S(1)}, u32[]{:S(2)}, u32[]{:S(2)}) %collective-permute-start.13) | collective-permute-done | bytes 262176 | tf_op jit(solution)/shard_map/ppermute | solution.py:52
  136.9 6.9 %shard_map.256 = (f32[512,1024]{1,0:T(8,128)}, bf16[512,1024]{1,0:T(8,128)(2,1)}) custom-call(s32[4]{0:T(128)} %pad_add_fusion.pos_ref, bf16[512,1024]{1,0:T(8,128)(2,1)} %get-tuple-element.290.mixed_ref.refs_3_, bf16[512,1024]{1,0:T(8,128)(2,1)} %tok_ref.3, f32[1,1024]{1,0:T(1,128)} %bitcast.94, f32[1,1024]{1,0:T(1,128)} %bitcast.92, f32[1,1024]{1,0:T(1,128)} %bitcast.95, ...), custom_call_target="tpu_custom_call" | custom-call | flops 1000 | bytes 1000 | tf_op jit(solution)/shard_map/pallas_call | solution.py:149
  152.9 13.6 %shard_map.257 = (bf16[512,4096]{1,0:T(8,128)(2,1)}, bf16[512,4096]{1,0:T(8,128)(2,1)}) custom-call(s32[4]{0:T(128)} %pad_add_fusion.pos_ref, bf16[512,1024]{1,0:T(8,128)(2,1)} %get-tuple-element.294.second_ref.refs_0_, f32[1,4096]{1,0:T(1,128)} %bitcast.89, bf16[32,256,640]{2,1,0:T(8,128)(2,1)} %bitcast.64), custom_call_target="tpu_custom_call" | custom-call | flops 1000 | bytes 1000 | tf_op jit(solution)/shard_map/pallas_call | solution.py:149
  166.5 7.3 %shard_map.258 = bf16[4,2,2,256,512]{4,3,2,1,0:T(8,128)(2,1)} custom-call(s32[4]{0:T(128)} %pad_add_fusion.pos_ref, bf16[512,1024]{1,0:T(8,128)(2,1)} %grad_ref.3, bf16[512,4096]{1,0:T(8,128)(2,1)} %get-tuple-element.446.refs_1_.gelu_ref), custom_call_target="tpu_custom_call" | custom-call | flops 1000 | bytes 1000 | tf_op jit(solution)/shard_map/pallas_call | solution.py:149
  183.2 11.0 %shard_map.259 = (bf16[512,4096]{1,0:T(8,128)(2,1)}, f32[1,4096]{1,0:T(1,128)}) custom-call(s32[4]{0:T(128)} %pad_add_fusion.pos_ref, bf16[512,4096]{1,0:T(8,128)(2,1)} %get-tuple-element.310.slope_ref, bf16[512,1024]{1,0:T(8,128)(2,1)} %grad_ref.3, bf16[2,2,256,512]{3,2,1,0:T(8,128)(2,1)} %copy-done.4, ...), custom_call_target="tpu_custom_call" | custom-call | flops 1000 | bytes 1000 | tf_op jit(solution)/shard_map/pallas_call | solution.py:149
  194.2 8.3 %shard_map.260 = (bf16[2,2,256,512]{3,2,1,0:T(8,128)(2,1)}, bf16[2,2,256,512]{3,2,1,0:T(8,128)(2,1)}, bf16[2,2,256,512]{3,2,1,0:T(8,128)(2,1)}, bf16[2,2,256,512]{3,2,1,0:T(8,128)(2,1)}) custom-call(s32[4]{0:T(128)} %pad_add_fusion.pos_ref, bf16[512,1024]{1,0:T(8,128)(2,1)} %grad_ref.3, bf16[512,4096]{1,0:T(8,128)(2,1)} %get-tuple-element.446.refs_1_.gelu_ref, ...), custom_call_target="tpu_custom_call" | custom-call | flops 1000 | bytes 1000 | tf_op jit(solution)/shard_map/pallas_call | solution.py:149
  203.6 13.3 %shard_map.261 = (f32[512,1024]{1,0:T(8,128)}, bf16[512,1024]{1,0:T(8,128)(2,1)}, f32[4,1024]{1,0:T(4,128)}) custom-call(s32[4]{0:T(128)} %pad_add_fusion.pos_ref, bf16[512,4096]{1,0:T(8,128)(2,1)} %get-tuple-element.330.pre_ref.refs_1_, bf16[512,1024]{1,0:T(8,128)(2,1)} %grad_ref.3, f32[512,1024]{1,0:T(8,128)} %get-tuple-element.331.middle_ref, ...), custom_call_target="tpu_custom_call" | custom-call | flops 1000 | bytes 1000 | tf_op jit(solution)/shard_map/pallas_call | solution.py:149
  216.9 5.8 %shard_map.263.grad_ref = bf16[512,1024]{1,0:T(8,128)(2,1)} custom-call(s32[4]{0:T(128)} %pad_add_fusion.pos_ref, bf16[512,1024]{1,0:T(8,128)(2,1)} %get-tuple-element.332.refs_2_.low_ref, bf16[32,256,640]{2,1,0:T(8,128)(2,1)} %bitcast.66), custom_call_target="tpu_custom_call" | custom-call | flops 1000 | bytes 1000 | tf_op jit(solution)/shard_map/pallas_call | solution.py:149
  222.7 8.9 %shard_map.262 = bf16[4,2,2,256,640]{4,3,2,1,0:T(8,128)(2,1)} custom-call(s32[4]{0:T(128)} %pad_add_fusion.pos_ref, bf16[512,1024]{1,0:T(8,128)(2,1)} %get-tuple-element.294.second_ref.refs_0_, bf16[512,4096]{1,0:T(8,128)(2,1)} %get-tuple-element.330.pre_ref.refs_1_, bf16[512,1024]{1,0:T(8,128)(2,1)} %get-tuple-element.332.refs_2_.low_ref, ...), custom_call_target="tpu_custom_call" | custom-call | flops 1000 | bytes 1000 | tf_op jit(solution)/shard_map/pallas_call | solution.py:149
  231.7 4.0 shard_map.264
  238.6 13.2 %shard_map.265 = (bf16[8,512,128]{2,1,0:T(8,128)(2,1)}, bf16[8,1024,128]{2,1,0:T(8,128)(2,1)}, bf16[8,1024,128]{2,1,0:T(8,128)(2,1)}, f32[2,1024]{1,0:T(2,128)}) custom-call(s32[4]{0:T(128)} %pad_add_fusion.pos_ref, bf16[8,512,128]{2,1,0:T(8,128)(2,1)} %get-tuple-element.278.q_ref, bf16[8,1024,128]{2,1,0:T(8,128)(2,1)} %get-tuple-element.279.k_ref, ...), custom_call_target="tpu_custom_call" | custom-call | flops 1000 | bytes 1000 | tf_op jit(solution)/shard_map/pallas_call | solution.py:149
  251.9 10.7 %shard_map.266 = (bf16[2,2,256,640]{3,2,1,0:T(8,128)(2,1)}, bf16[2,2,256,640]{3,2,1,0:T(8,128)(2,1)}, bf16[2,2,256,640]{3,2,1,0:T(8,128)(2,1)}, bf16[2,2,256,640]{3,2,1,0:T(8,128)(2,1)}) custom-call(s32[4]{0:T(128)} %pad_add_fusion.pos_ref, bf16[512,1024]{1,0:T(8,128)(2,1)} %get-tuple-element.294.second_ref.refs_0_, ...), custom_call_target="tpu_custom_call" | custom-call | flops 1000 | bytes 1000 | tf_op jit(solution)/shard_map/pallas_call | solution.py:149
  271.8 13.2 %shard_map.268 = (bf16[8,512,128]{2,1,0:T(8,128)(2,1)}, bf16[8,1024,128]{2,1,0:T(8,128)(2,1)}, bf16[8,1024,128]{2,1,0:T(8,128)(2,1)}, f32[2,1024]{1,0:T(2,128)}) custom-call(s32[4]{0:T(128)} %pad_add_fusion.pos_ref, bf16[8,512,128]{2,1,0:T(8,128)(2,1)} %get-tuple-element.278.q_ref, ...), custom_call_target="tpu_custom_call", output_to_operand_aliasing={{0}: (9, {}), {1}: (10, {}), {2}: (11, {}), {3}: (12, {})} | custom-call | flops 1000 | bytes 1000 | tf_op jit(solution)/shard_map/pallas_call | solution.py:149
  285.0 8.3 %shard_map.269 = bf16[4,2,2,256,384]{4,3,2,1,0:T(8,128)(2,1)} custom-call(s32[4]{0:T(128)} %pad_add_fusion.pos_ref, bf16[1024,1024]{1,0:T(8,128)(2,1)} %fusion.5.first_ref.refs_0_, bf16[8,512,128]{2,1,0:T(8,128)(2,1)} %get-tuple-element.438.refs_1_.dq_ref, bf16[8,1024,128]{2,1,0:T(8,128)(2,1)} %get-tuple-element.439.refs_2_.dk_ref, ...), custom_call_target="tpu_custom_call" | custom-call | flops 1000 | bytes 1000 | tf_op jit(solution)/shard_map/pallas_call | solution.py:149
  296.9 4.4 %shard_map.270 = (bf16[2,256,640]{2,1,0:T(8,128)(2,1)}, bf16[2,256,640]{2,1,0:T(8,128)(2,1)}, bf16[2,256,640]{2,1,0:T(8,128)(2,1)}, bf16[2,256,640]{2,1,0:T(8,128)(2,1)}) custom-call(s32[4]{0:T(128)} %pad_add_fusion.pos_ref, bf16[2,2,256,640]{3,2,1,0:T(8,128)(2,1)} %get-tuple-element.386.refs_0_, bf16[2,2,256,640]{3,2,1,0:T(8,128)(2,1)} %collective-permute-done.29.refs_1_, ...), custom_call_target="tpu_custom_call" | custom-call | flops 1000 | bytes 1000 | tf_op jit(solution)/shard_map/pallas_call | solution.py:149
  303.5 9.5 %shard_map.271 = (bf16[512,1024]{1,0:T(8,128)(2,1)}, f32[2,1024]{1,0:T(2,128)}) custom-call(s32[4]{0:T(128)} %pad_add_fusion.pos_ref, bf16[8,1024,128]{2,1,0:T(8,128)(2,1)} %get-tuple-element.439.refs_2_.dk_ref, bf16[8,1024,128]{2,1,0:T(8,128)(2,1)} %get-tuple-element.440.refs_3_.dv_ref, bf16[512,1024]{1,0:T(8,128)(2,1)} %copy-done.1, f32[1,1024]{1,0:T(1,128)} %bitcast.84, ...), custom_call_target="tpu_custom_call" | custom-call | flops 1000 | bytes 1000 | tf_op jit(solution)/shard_map/pallas_call | solution.py:149
  314.6 9.2 %shard_map.272 = (bf16[2,2,256,384]{3,2,1,0:T(8,128)(2,1)}, bf16[2,2,256,384]{3,2,1,0:T(8,128)(2,1)}, bf16[2,2,256,384]{3,2,1,0:T(8,128)(2,1)}, bf16[2,2,256,384]{3,2,1,0:T(8,128)(2,1)}) custom-call(s32[4]{0:T(128)} %pad_add_fusion.pos_ref, bf16[1024,1024]{1,0:T(8,128)(2,1)} %fusion.5.first_ref.refs_0_, ...), custom_call_target="tpu_custom_call" | custom-call | flops 1000 | bytes 1000 | tf_op jit(solution)/shard_map/pallas_call | solution.py:149
  326.8 3.5 shard_map.273
  334.6 10.9 %shard_map.275 = bf16[512,1024]{1,0:T(8,128)(2,1)} custom-call(s32[4]{0:T(128)} %pad_add_fusion.pos_ref, bf16[512,4096]{1,0:T(8,128)(2,1)} %get-tuple-element.446.refs_1_.gelu_ref, f32[512,1024]{1,0:T(8,128)} %get-tuple-element.331.middle_ref, f32[1,1024]{1,0:T(1,128)} %bitcast.96, bf16[2,2,256,512]{3,2,1,0:T(8,128)(2,1)} %copy-done.4, ...), custom_call_target="tpu_custom_call" | custom-call | flops 1000 | bytes 1000 | tf_op jit(solution)/shard_map/pallas_call | solution.py:149
  345.6 12.3 %shard_map.274 = (f32[512,1024]{1,0:T(8,128)}, f32[2,1024]{1,0:T(2,128)}) custom-call(s32[4]{0:T(128)} %pad_add_fusion.pos_ref, bf16[8,512,128]{2,1,0:T(8,128)(2,1)} %get-tuple-element.438.refs_1_.dq_ref, bf16[8,1024,128]{2,1,0:T(8,128)(2,1)} %get-tuple-element.439.refs_2_.dk_ref, bf16[8,1024,128]{2,1,0:T(8,128)(2,1)} %get-tuple-element.440.refs_3_.dv_ref, ...), custom_call_target="tpu_custom_call" | custom-call | flops 1000 | bytes 1000 | tf_op jit(solution)/shard_map/pallas_call | solution.py:149
  360.3 3.4 shard_map.276
  391.4 9.7 %collective-permute-done.49.refs_2_ = bf16[256,384]{1,0:T(8,128)(2,1)S(1)} collective-permute-done((bf16[256,384]{1,0:T(8,128)(2,1)}, bf16[256,384]{1,0:T(8,128)(2,1)S(1)}, u32[]{:S(2)}, u32[]{:S(2)}) %collective-permute-start.49) | collective-permute-done | bytes 196640 | tf_op jit(solution)/shard_map/ppermute | solution.py:52
  (207 shorter events, 115.2 us)
Async XLA Ops:
  7.2 125.6 %all-gather.3.cloned.1.call-start = ((), (), s32[]{:S(2)}) async-start(), calls=%async_computation | async-start | bytes 10813440 | tf_op jit(solution)/shard_map/all_gather | solution.py:886
  9.1 33.2 %collective-permute-start.3 = (bf16[512,1024]{1,0:T(8,128)(2,1)}, bf16[512,1024]{1,0:T(8,128)(2,1)S(1)}, u32[]{:S(2)}, u32[]{:S(2)}) collective-permute-start(bf16[512,1024]{1,0:T(8,128)(2,1)} %tok_ref.3), channel_id=1, source_target_pairs={{0,1},{2,3},{4,5},{6,7},{8,9},{10,11},{12,13},{14,15},{16,17},{18,... | collective-permute-start | bytes 3145736 | tf_op jit(solution)/shard_map/ppermute | solution.py:890
  18.9 23.4 %collective-permute-start.1 = (bf16[256,384]{1,0:T(8,128)(2,1)S(1)}, bf16[256,384]{1,0:T(8,128)(2,1)S(1)}, u32[]{:S(2)}, u32[]{:S(2)}) collective-permute-start(bf16[256,384]{1,0:T(8,128)(2,1)S(1)} %copy.35), channel_id=1, source_target_pairs={{0,4},{2,6},{4,0},{6,2},{1,5},{3,7},{5,1},{7,3},{8,12},{10,14},{12... | collective-permute-start | bytes 589832 | tf_op jit(solution)/shard_map/ppermute | solution.py:52
  18.9 23.4 %collective-permute-start = (bf16[256,384]{1,0:T(8,128)(2,1)S(1)}, bf16[256,384]{1,0:T(8,128)(2,1)S(1)}, u32[]{:S(2)}, u32[]{:S(2)}) collective-permute-start(bf16[256,384]{1,0:T(8,128)(2,1)S(1)} %copy.35), channel_id=1, source_target_pairs={{0,2},{2,0},{4,6},{6,4},{1,3},{3,1},{5,7},{7,5},{8,10},{10,8},{12,... | collective-permute-start | bytes 589832 | tf_op jit(solution)/shard_map/ppermute | solution.py:52
  44.2 20.1 %collective-permute-start.4 = (bf16[2,256,384]{2,1,0:T(8,128)(2,1)S(1)}, bf16[2,256,384]{2,1,0:T(8,128)(2,1)S(1)}, u32[]{:S(2)}, u32[]{:S(2)}) collective-permute-start(bf16[2,256,384]{2,1,0:T(8,128)(2,1)S(1)} %get-tuple-element.507), channel_id=1, source_target_pairs={{0,1},{1,0},{2,3},{3,2},{4,5},{5,4},{6,7},{7,6},{8,9},{9,8},{10,11... | collective-permute-start | bytes 1179656 | tf_op jit(solution)/shard_map/ppermute | solution.py:52
  57.6 25.1 %collective-permute-start.7 = (bf16[2,2,256,384]{3,2,1,0:T(8,128)(2,1)S(1)}, bf16[2,2,256,384]{3,2,1,0:T(8,128)(2,1)}, u32[]{:S(2)}, u32[]{:S(2)}) collective-permute-start(bf16[2,2,256,384]{3,2,1,0:T(8,128)(2,1)S(1)} %pad_maximum_fusion.4.rest_2_), channel_id=1, source_target_pairs={{0,1},{1,0},{2,3},{3,2},{4,5},{5,4},{6,7},{7,6},{8,9},{9,8},{10,11... | collective-permute-start | bytes 2359304 | tf_op jit(solution)/shard_map/ppermute | solution.py:52
  65.3 18.0 %collective-permute-start.5 = (bf16[2,2,256,384]{3,2,1,0:T(8,128)(2,1)}, bf16[2,2,256,384]{3,2,1,0:T(8,128)(2,1)}, u32[]{:S(2)}, u32[]{:S(2)}) collective-permute-start(bf16[2,2,256,384]{3,2,1,0:T(8,128)(2,1)} %pad_maximum_fusion.3.rest_0_), channel_id=1, source_target_pairs={{0,16},{16,0},{1,17},{17,1},{2,18},{18,2},{3,19},{19,3},{4,20},{20... | collective-permute-start | bytes 2359304 | tf_op jit(solution)/shard_map/ppermute | solution.py:52
  66.0 17.8 %collective-permute-start.10 = (bf16[2,2,256,384]{3,2,1,0:T(8,128)(2,1)S(1)}, bf16[2,2,256,384]{3,2,1,0:T(8,128)(2,1)}, u32[]{:S(2)}, u32[]{:S(2)}) collective-permute-start(bf16[2,2,256,384]{3,2,1,0:T(8,128)(2,1)S(1)} %pad_maximum_fusion.4.rest_2_), channel_id=1, source_target_pairs={{0,8},{8,0},{1,9},{9,1},{2,10},{10,2},{3,11},{11,3},{4,12},{12,4},... | collective-permute-start | bytes 2359304 | tf_op jit(solution)/shard_map/ppermute | solution.py:52
  66.1 17.8 %collective-permute-start.8 = (bf16[2,2,256,384]{3,2,1,0:T(8,128)(2,1)}, bf16[2,2,256,384]{3,2,1,0:T(8,128)(2,1)}, u32[]{:S(2)}, u32[]{:S(2)}) collective-permute-start(bf16[2,2,256,384]{3,2,1,0:T(8,128)(2,1)} %pad_maximum_fusion.3.rest_0_), channel_id=1, source_target_pairs={{0,8},{8,0},{1,9},{9,1},{2,10},{10,2},{3,11},{11,3},{4,12},{12,4},... | collective-permute-start | bytes 2359304 | tf_op jit(solution)/shard_map/ppermute | solution.py:52
  83.8 39.7 %collective-permute-start.14 = (bf16[256,512]{1,0:T(8,128)(2,1)S(1)}, bf16[256,512]{1,0:T(8,128)(2,1)S(1)}, u32[]{:S(2)}, u32[]{:S(2)}) collective-permute-start(bf16[256,512]{1,0:T(8,128)(2,1)S(1)} %copy-done.20), channel_id=1, source_target_pairs={{0,6},{2,4},{4,2},{6,0},{1,7},{3,5},{5,3},{7,1},{8,14},{10,12},{12... | collective-permute-start | bytes 786440 | tf_op jit(solution)/shard_map/ppermute | solution.py:52
  83.8 45.5 %collective-permute-start.13 = (bf16[256,512]{1,0:T(8,128)(2,1)S(1)}, bf16[256,512]{1,0:T(8,128)(2,1)S(1)}, u32[]{:S(2)}, u32[]{:S(2)}) collective-permute-start(bf16[256,512]{1,0:T(8,128)(2,1)S(1)} %copy-done.20), channel_id=1, source_target_pairs={{0,4},{2,6},{4,0},{6,2},{1,5},{3,7},{5,1},{7,3},{8,12},{10,14},{12... | collective-permute-start | bytes 786440 | tf_op jit(solution)/shard_map/ppermute | solution.py:52
  83.9 45.4 %collective-permute-start.12 = (bf16[256,512]{1,0:T(8,128)(2,1)S(1)}, bf16[256,512]{1,0:T(8,128)(2,1)}, u32[]{:S(2)}, u32[]{:S(2)}) collective-permute-start(bf16[256,512]{1,0:T(8,128)(2,1)S(1)} %copy-done.20), channel_id=1, source_target_pairs={{0,2},{2,0},{4,6},{6,4},{1,3},{3,1},{5,7},{7,5},{8,10},{10,8},{12,... | collective-permute-start | bytes 786440 | tf_op jit(solution)/shard_map/ppermute | solution.py:52
  149.3 24.4 %collective-permute-start.20 = (bf16[2,2,256,512]{3,2,1,0:T(8,128)(2,1)S(1)}, bf16[2,2,256,512]{3,2,1,0:T(8,128)(2,1)S(1)}, u32[]{:S(2)}, u32[]{:S(2)}) collective-permute-start(bf16[2,2,256,512]{3,2,1,0:T(8,128)(2,1)S(1)} %pad_maximum_fusion.2.rest_2_), channel_id=1, source_target_pairs={{0,8},{8,0},{1,9},{9,1},{2,10},{10,2},{3,11},{11,3},{4,12},{12,4},... | collective-permute-start | bytes 3145736 | tf_op jit(solution)/shard_map/ppermute | solution.py:52
  149.4 25.7 %collective-permute-start.18 = (bf16[2,2,256,512]{3,2,1,0:T(8,128)(2,1)S(1)}, bf16[2,2,256,512]{3,2,1,0:T(8,128)(2,1)}, u32[]{:S(2)}, u32[]{:S(2)}) collective-permute-start(bf16[2,2,256,512]{3,2,1,0:T(8,128)(2,1)S(1)} %pad_maximum_fusion.2.rest_2_), channel_id=1, source_target_pairs={{0,1},{1,0},{2,3},{3,2},{4,5},{5,4},{6,7},{7,6},{8,9},{9,8},{10,11... | collective-permute-start | bytes 3145736 | tf_op jit(solution)/shard_map/ppermute | solution.py:52
  152.1 23.0 %collective-permute-start.19 = (bf16[2,2,256,512]{3,2,1,0:T(8,128)(2,1)S(1)}, bf16[2,2,256,512]{3,2,1,0:T(8,128)(2,1)}, u32[]{:S(2)}, u32[]{:S(2)}) collective-permute-start(bf16[2,2,256,512]{3,2,1,0:T(8,128)(2,1)S(1)} %pad_maximum_fusion.1.rest_0_), channel_id=1, source_target_pairs={{0,8},{8,0},{1,9},{9,1},{2,10},{10,2},{3,11},{11,3},{4,12},{12,4},... | collective-permute-start | bytes 3145736 | tf_op jit(solution)/shard_map/ppermute | solution.py:52
  152.3 25.5 %collective-permute-start.17 = (bf16[2,2,256,512]{3,2,1,0:T(8,128)(2,1)S(1)}, bf16[2,2,256,512]{3,2,1,0:T(8,128)(2,1)}, u32[]{:S(2)}, u32[]{:S(2)}) collective-permute-start(bf16[2,2,256,512]{3,2,1,0:T(8,128)(2,1)S(1)} %pad_maximum_fusion.1.rest_0_), channel_id=1, source_target_pairs={{0,16},{16,0},{1,17},{17,1},{2,18},{18,2},{3,19},{19,3},{4,20},{20... | collective-permute-start | bytes 3145736 | tf_op jit(solution)/shard_map/ppermute | solution.py:52
  202.5 29.2 %collective-permute-start.24 = (bf16[2,2,256,512]{3,2,1,0:T(8,128)(2,1)}, bf16[2,2,256,512]{3,2,1,0:T(8,128)(2,1)}, u32[]{:S(2)}, u32[]{:S(2)}) collective-permute-start(bf16[2,2,256,512]{3,2,1,0:T(8,128)(2,1)} %get-tuple-element.327), channel_id=1, source_target_pairs={{0,16},{16,0},{1,17},{17,1},{2,18},{18,2},{3,19},{19,3},{4,20},{20... | collective-permute-start | bytes 3145736 | tf_op jit(solution)/shard_map/ppermute | solution.py:52
  203.0 28.6 %collective-permute-start.25 = (bf16[2,2,256,512]{3,2,1,0:T(8,128)(2,1)}, bf16[2,2,256,512]{3,2,1,0:T(8,128)(2,1)}, u32[]{:S(2)}, u32[]{:S(2)}) collective-permute-start(bf16[2,2,256,512]{3,2,1,0:T(8,128)(2,1)} %get-tuple-element.329), channel_id=1, source_target_pairs={{0,1},{1,0},{2,3},{3,2},{4,5},{5,4},{6,7},{7,6},{8,9},{9,8},{10,11... | collective-permute-start | bytes 3145736 | tf_op jit(solution)/shard_map/ppermute | solution.py:52
  265.8 30.9 %collective-permute-start.29 = (bf16[2,2,256,640]{3,2,1,0:T(8,128)(2,1)}, bf16[2,2,256,640]{3,2,1,0:T(8,128)(2,1)}, u32[]{:S(2)}, u32[]{:S(2)}) collective-permute-start(bf16[2,2,256,640]{3,2,1,0:T(8,128)(2,1)} %get-tuple-element.379), channel_id=1, source_target_pairs={{0,16},{16,0},{1,17},{17,1},{2,18},{18,2},{3,19},{19,3},{4,20},{20... | collective-permute-start | bytes 3932168 | tf_op jit(solution)/shard_map/ppermute | solution.py:52
  266.8 30.1 %collective-permute-start.30 = (bf16[2,2,256,640]{3,2,1,0:T(8,128)(2,1)}, bf16[2,2,256,640]{3,2,1,0:T(8,128)(2,1)}, u32[]{:S(2)}, u32[]{:S(2)}) collective-permute-start(bf16[2,2,256,640]{3,2,1,0:T(8,128)(2,1)} %get-tuple-element.381), channel_id=1, source_target_pairs={{0,1},{1,0},{2,3},{3,2},{4,5},{5,4},{6,7},{7,6},{8,9},{9,8},{10,11... | collective-permute-start | bytes 3932168 | tf_op jit(solution)/shard_map/ppermute | solution.py:52
  267.4 25.9 %collective-permute-start.31 = (bf16[256,512]{1,0:T(8,128)(2,1)}, bf16[256,512]{1,0:T(8,128)(2,1)}, u32[]{:S(2)}, u32[]{:S(2)}) collective-permute-start(bf16[256,512]{1,0:T(8,128)(2,1)} %get-tuple-element.383), channel_id=1, source_target_pairs={{0,2},{2,0},{4,6},{6,4},{1,3},{3,1},{5,7},{7,5},{8,10},{10,8},{12,... | collective-permute-start | bytes 786440 | tf_op jit(solution)/shard_map/ppermute | solution.py:52
  267.4 25.9 %collective-permute-start.32 = (bf16[256,512]{1,0:T(8,128)(2,1)}, bf16[256,512]{1,0:T(8,128)(2,1)}, u32[]{:S(2)}, u32[]{:S(2)}) collective-permute-start(bf16[256,512]{1,0:T(8,128)(2,1)} %get-tuple-element.384), channel_id=1, source_target_pairs={{0,4},{2,6},{4,0},{6,2},{1,5},{3,7},{5,1},{7,3},{8,12},{10,14},{12... | collective-permute-start | bytes 786440 | tf_op jit(solution)/shard_map/ppermute | solution.py:52
  269.4 24.0 %collective-permute-start.33 = (bf16[256,512]{1,0:T(8,128)(2,1)}, bf16[256,512]{1,0:T(8,128)(2,1)}, u32[]{:S(2)}, u32[]{:S(2)}) collective-permute-start(bf16[256,512]{1,0:T(8,128)(2,1)} %get-tuple-element.385), channel_id=1, source_target_pairs={{0,6},{2,4},{4,2},{6,0},{1,7},{3,5},{5,3},{7,1},{8,14},{10,12},{12... | collective-permute-start | bytes 786440 | tf_op jit(solution)/shard_map/ppermute | solution.py:52
  301.4 22.5 %collective-permute-start.35 = (bf16[2,256,640]{2,1,0:T(8,128)(2,1)}, bf16[2,256,640]{2,1,0:T(8,128)(2,1)S(1)}, u32[]{:S(2)}, u32[]{:S(2)}) collective-permute-start(bf16[2,256,640]{2,1,0:T(8,128)(2,1)} %get-tuple-element.410), channel_id=1, source_target_pairs={{0,1},{1,0},{2,3},{3,2},{4,5},{5,4},{6,7},{7,6},{8,9},{9,8},{10,11... | collective-permute-start | bytes 1966088 | tf_op jit(solution)/shard_map/ppermute | solution.py:52
  302.0 21.9 %collective-permute-start.36 = (bf16[2,256,640]{2,1,0:T(8,128)(2,1)}, bf16[2,256,640]{2,1,0:T(8,128)(2,1)}, u32[]{:S(2)}, u32[]{:S(2)}) collective-permute-start(bf16[2,256,640]{2,1,0:T(8,128)(2,1)} %get-tuple-element.412), channel_id=1, source_target_pairs={{0,16},{16,0},{1,17},{17,1},{2,18},{18,2},{3,19},{19,3},{4,20},{20... | collective-permute-start | bytes 1966088 | tf_op jit(solution)/shard_map/ppermute | solution.py:52
  324.7 34.0 %collective-permute-start.37 = (bf16[2,2,256,384]{3,2,1,0:T(8,128)(2,1)}, bf16[2,2,256,384]{3,2,1,0:T(8,128)(2,1)S(1)}, u32[]{:S(2)}, u32[]{:S(2)}) collective-permute-start(bf16[2,2,256,384]{3,2,1,0:T(8,128)(2,1)} %get-tuple-element.417), channel_id=1, source_target_pairs={{0,16},{16,0},{1,17},{17,1},{2,18},{18,2},{3,19},{19,3},{4,20},{20... | collective-permute-start | bytes 2359304 | tf_op jit(solution)/shard_map/ppermute | solution.py:52
  325.3 34.1 %collective-permute-start.38 = (bf16[2,2,256,384]{3,2,1,0:T(8,128)(2,1)}, bf16[2,2,256,384]{3,2,1,0:T(8,128)(2,1)}, u32[]{:S(2)}, u32[]{:S(2)}) collective-permute-start(bf16[2,2,256,384]{3,2,1,0:T(8,128)(2,1)} %get-tuple-element.419), channel_id=1, source_target_pairs={{0,1},{1,0},{2,3},{3,2},{4,5},{5,4},{6,7},{7,6},{8,9},{9,8},{10,11... | collective-permute-start | bytes 2359304 | tf_op jit(solution)/shard_map/ppermute | solution.py:52
  330.3 28.4 %collective-permute-start.39 = (bf16[256,640]{1,0:T(8,128)(2,1)}, bf16[256,640]{1,0:T(8,128)(2,1)S(1)}, u32[]{:S(2)}, u32[]{:S(2)}) collective-permute-start(bf16[256,640]{1,0:T(8,128)(2,1)} %get-tuple-element.433), channel_id=1, source_target_pairs={{0,2},{2,0},{4,6},{6,4},{1,3},{3,1},{5,7},{7,5},{8,10},{10,8},{12,... | collective-permute-start | bytes 983048 | tf_op jit(solution)/shard_map/ppermute | solution.py:52
  330.3 28.4 %collective-permute-start.40 = (bf16[256,640]{1,0:T(8,128)(2,1)}, bf16[256,640]{1,0:T(8,128)(2,1)S(1)}, u32[]{:S(2)}, u32[]{:S(2)}) collective-permute-start(bf16[256,640]{1,0:T(8,128)(2,1)} %get-tuple-element.434), channel_id=1, source_target_pairs={{0,4},{2,6},{4,0},{6,2},{1,5},{3,7},{5,1},{7,3},{8,12},{10,14},{12... | collective-permute-start | bytes 983048 | tf_op jit(solution)/shard_map/ppermute | solution.py:52
  332.2 26.5 %collective-permute-start.41 = (bf16[256,640]{1,0:T(8,128)(2,1)}, bf16[256,640]{1,0:T(8,128)(2,1)S(1)}, u32[]{:S(2)}, u32[]{:S(2)}) collective-permute-start(bf16[256,640]{1,0:T(8,128)(2,1)} %get-tuple-element.435), channel_id=1, source_target_pairs={{0,6},{2,4},{4,2},{6,0},{1,7},{3,5},{5,3},{7,1},{8,14},{10,12},{12... | collective-permute-start | bytes 983048 | tf_op jit(solution)/shard_map/ppermute | solution.py:52
  380.0 32.3 %collective-permute-start.47 = (bf16[512,1024]{1,0:T(8,128)(2,1)}, bf16[512,1024]{1,0:T(8,128)(2,1)}, u32[]{:S(2)}, u32[]{:S(2)}) collective-permute-start(bf16[512,1024]{1,0:T(8,128)(2,1)} %get-tuple-element.483), channel_id=1, source_target_pairs={{1,0},{3,2},{5,4},{7,6},{9,8},{11,10},{13,12},{15,14},{17,16},{19,... | collective-permute-start | bytes 3145736 | tf_op jit(solution)/shard_map/ppermute | solution.py:1037
  384.1 17.0 %collective-permute-start.49 = (bf16[256,384]{1,0:T(8,128)(2,1)}, bf16[256,384]{1,0:T(8,128)(2,1)S(1)}, u32[]{:S(2)}, u32[]{:S(2)}) collective-permute-start(bf16[256,384]{1,0:T(8,128)(2,1)} %get-tuple-element.486), channel_id=1, source_target_pairs={{0,4},{2,6},{4,0},{6,2},{1,5},{3,7},{5,1},{7,3},{8,12},{10,14},{12... | collective-permute-start | bytes 589832 | tf_op jit(solution)/shard_map/ppermute | solution.py:52
  (56 other events, 625.0 us)
Sparse Core Ops, SparseCore 0:
  11.5 121.1 all-gather.2

commit v4 on v3

--- a/solution.py
+++ b/solution.py
@@ -942,12 +942,12 @@
     )
 
     def up_tile(left, ins, xs):
+        tail = dot(left[1][...], jnp.concatenate([block(ins[3], x, width) for x in xs], axis=1))
         return [
             jnp.concatenate(
-                [dot(left[0][...], block(ins[1], x, hidden)), dot(left[1][...], block(ins[3], x, width))],
-                axis=1,
+                [dot(left[0][...], block(ins[1], x, hidden)), tail[:, i * width : (i + 1) * width]], axis=1
             )
-            for x in xs
+            for i, x in enumerate(xs)
         ]
 
     grad_up = Scatter(
@@ -996,48 +996,44 @@
     grad_qkv.sent, dq, dk, dv = stage(grad_up, grad_qkv.sent, dq, dk, dv)
     grad_up.send_two()
     grad_qkv.swap()
-    back, sums_prev = first_grad_prev_call(
-        lay, pos, dk, dv, tokens_prev, row(ln1_gain), qkv.parts, width
-    )
-    grad_qkv.received, dq, dk, dv, back, sums_prev = stage(
-        grad_qkv.received, dq, dk, dv, back, sums_prev
+    grad_down.sum_three((hidden,))
+    grad_qkv.received, grad_down.out, dq, dk, dv = stage(
+        grad_qkv.received, grad_down.out, dq, dk, dv
     )
     grad_qkv.own()
-    dq, dk, dv, gelu = stage(grad_qkv, grad_up, dq, dk, dv, gelu)
+    dq, dk, dv = stage(grad_qkv, grad_up, dq, dk, dv)
     grad_qkv.send_one()
     grad_up.sum_two()
-    gelu, dq, dk, dv = stage(grad_up, gelu, dq, dk, dv)
+    dq, dk, dv = stage(grad_up, dq, dk, dv)
     grad_up.send_three()
     first_grad, sums1 = first_grad_own_call(
         lay, pos, dq, dk, dv, tokens, middle_grad, row(ln1_gain), qkv.parts, width
     )
-    result = result_call(lay, pos, gelu, middle, row(b_down), down.parts, hidden)
+    nearer = grad_up.top[: nz - 1]
+    nearer, first_grad, sums1, dk, dv = stage(grad_qkv, nearer, first_grad, sums1, dk, dv)
+    grad_up.top = [*nearer, grad_up.top[-1]]
+    grad_qkv.sum_one()
+    dk, dv = stage(grad_qkv, dk, dv)
+    grad_qkv.send_two()
+    back, sums_prev = first_grad_prev_call(
+        lay, pos, dk, dv, tokens_prev, row(ln1_gain), qkv.parts, width
+    )
+    back, sums_prev, gelu = stage(grad_qkv, back, sums_prev, gelu)
     small = jnp.concatenate(
         [v.reshape(-1) for v in (sums2, grad_b_up, sums1 + sums_prev, sums_qv)]
     ).reshape(-1, 128)
-    small, first_grad, result, back = stage(grad_qkv, grad_up, small, first_grad, result, back)
-    grad_qkv.sum_one()
-    small, back = stage(grad_qkv, small, back)
-    grad_qkv.send_two()
-    grad_down.sum_three((hidden,))
-    both_cores = [((c, x), (c ^ 1, x ^ 1)) for c in range(2) for x in range(2)]
-    both_cores = [(s[0] * 2 + s[1], t[0] * 2 + t[1]) for s, t in both_cores]
-    pieces = [
-        small,
-        trade(small, "c", 2, 1),
-        trade(small, "tx", 2, 1),
-        lax.ppermute(small, ("c", "tx"), both_cores),
-    ]
-    pieces, back, grad_down.out = stage(grad_qkv, pieces, back, grad_down.out)
-    small = (pieces[0] + pieces[1]) + (pieces[2] + pieces[3])
+    small = small + trade(small, "c", 2, 1)
     grad_qkv.sum_two()
-    small, back = stage(grad_qkv, small, back)
+    small, back, gelu = stage(grad_qkv, grad_up, small, back, gelu)
     grad_qkv.send_three()
     pieces = around(small, "fy", ny)
     back = lax.ppermute(back, "tx", [(1, 0)])
     grad_up.sum_three((hidden, width))
-    pieces, grad_up.out = stage(grad_qkv, pieces, grad_up.out)
-    small = sum(around(sum(pieces), "tz", nz)).reshape(-1)
+    result = result_call(lay, pos, gelu, middle, row(b_down), down.parts, hidden)
+    pieces, result, grad_up.out = stage(grad_qkv, pieces, result, grad_up.out)
+    small = sum(pieces)
+    small = small + trade(small, "tx", 2, 1)
+    small = sum(around(small, "tz", nz)).reshape(-1)
     token_grad = (first_grad + back.astype(F32)).astype(BF)
     grad_qkv.sum_three(((3, width),))
     at = 4 * dim

time: 427 us -> 415 us (0.972)
  waiting for transfers between devices: 98 us -> 91.6 us
    unnamed x68 -> x66, local copies, waits for them, and re-layouts: 8.7 us -> 4.59 us
  transfers between devices with their start and end apart: 56 -> 55, of which waited for: 21 -> 23; matrix products, arithmetic and copies ran while one was open for 3% -> 3% of each run, Pallas kernels for 44% -> 46%
where the time goes in v4:
time: 415 us; the launch traced here: 411 us
  Pallas kernels  223 us (54%)
  waiting for transfers between devices  91.6 us (22%)
  starting transfers between devices  58.3 us (14%)
  between operations  14.9 us (4%)
  other arithmetic  14.7 us (4%)
  local copies, waits for them, and re-layouts  8.37 us (2%)
    pallas_call x27, Pallas kernels, kernel_call(): pl.pallas_call(body, out_shape=outs, grid_spec=pltpu.PrefetchScalarGridSp...  223 us
    ppermute x52, waiting for transfers between devices, trade(): return lax.ppermute(value, axis, [(s, s ^ distance) for s in range(size)])  88.1 us
    ppermute x52, starting transfers between devices, trade(): return lax.ppermute(value, axis, [(s, s ^ distance) for s in range(size)])  52 us
  transfers between devices with their start and end apart: 55, of which 23 were waited for; matrix products, arithmetic and copies ran while one was open for 3% of the time, Pallas kernels for 46%

profile of v4, /device:TPU:0, one launch (start us, length us, event | category | flops | bytes accessed | tf_op | source)
XLA Modules:
  0.0 411.0 jit_solution(2059849367948247649)
XLA Ops:
  9.1 4.9 %collective-permute-start.3 = (bf16[512,1024]{1,0:T(8,128)(2,1)}, bf16[512,1024]{1,0:T(8,128)(2,1)S(1)}, u32[]{:S(2)}, u32[]{:S(2)}) collective-permute-start(bf16[512,1024]{1,0:T(8,128)(2,1)} %tok_ref.3), channel_id=1, source_target_pairs={{0,1},{2,3},{4,5},{6,7},{8,9},{10,11},{12,13},{14,15},{16,17},{18,... | collective-permute-start | bytes 3145736 | tf_op jit(solution)/shard_map/ppermute | solution.py:890
  15.2 3.7 collective-permute-start.2
  20.5 4.5 %collective-permute-done.2 = bf16[256,384]{1,0:T(8,128)(2,1)S(1)} collective-permute-done((bf16[256,384]{1,0:T(8,128)(2,1)S(1)}, bf16[256,384]{1,0:T(8,128)(2,1)S(1)}, u32[]{:S(2)}, u32[]{:S(2)}) %collective-permute-start.2) | collective-permute-done | bytes 196640 | tf_op jit(solution)/shard_map/ppermute | solution.py:52
  25.0 17.3 %collective-permute-done.1 = bf16[256,384]{1,0:T(8,128)(2,1)S(1)} collective-permute-done((bf16[256,384]{1,0:T(8,128)(2,1)S(1)}, bf16[256,384]{1,0:T(8,128)(2,1)S(1)}, u32[]{:S(2)}, u32[]{:S(2)}) %collective-permute-start.1) | collective-permute-done | bytes 196640 | tf_op jit(solution)/shard_map/ppermute | solution.py:52
  44.7 12.8 %collective-permute-done.6 = bf16[2,256,384]{2,1,0:T(8,128)(2,1)S(1)} collective-permute-done((bf16[2,256,384]{2,1,0:T(8,128)(2,1)S(1)}, bf16[2,256,384]{2,1,0:T(8,128)(2,1)S(1)}, u32[]{:S(2)}, u32[]{:S(2)}) %collective-permute-start.6) | collective-permute-done | bytes 393248 | tf_op jit(solution)/shard_map/ppermute | solution.py:52
  57.6 6.7 %collective-permute-done.4 = bf16[2,256,384]{2,1,0:T(8,128)(2,1)S(1)} collective-permute-done((bf16[2,256,384]{2,1,0:T(8,128)(2,1)S(1)}, bf16[2,256,384]{2,1,0:T(8,128)(2,1)S(1)}, u32[]{:S(2)}, u32[]{:S(2)}) %collective-permute-start.4) | collective-permute-done | bytes 393248 | tf_op jit(solution)/shard_map/ppermute | solution.py:52
  69.6 13.2 %collective-permute-done.7.rest_3_ = bf16[2,2,256,384]{3,2,1,0:T(8,128)(2,1)} collective-permute-done((bf16[2,2,256,384]{3,2,1,0:T(8,128)(2,1)S(1)}, bf16[2,2,256,384]{3,2,1,0:T(8,128)(2,1)}, u32[]{:S(2)}, u32[]{:S(2)}) %collective-permute-start.7) | collective-permute-done | bytes 786464 | tf_op jit(solution)/shard_map/ppermute | solution.py:52
  83.9 4.3 %collective-permute-start.12 = (bf16[256,512]{1,0:T(8,128)(2,1)S(1)}, bf16[256,512]{1,0:T(8,128)(2,1)}, u32[]{:S(2)}, u32[]{:S(2)}) collective-permute-start(bf16[256,512]{1,0:T(8,128)(2,1)S(1)} %copy-done.18), channel_id=1, source_target_pairs={{0,2},{2,0},{4,6},{6,4},{1,3},{3,1},{5,7},{7,5},{8,10},{10,8},{12,... | collective-permute-start | bytes 786440 | tf_op jit(solution)/shard_map/ppermute | solution.py:52
  91.6 11.4 %shard_map.254 = (bf16[8,512,128]{2,1,0:T(8,128)(2,1)}, bf16[8,1024,128]{2,1,0:T(8,128)(2,1)}, bf16[8,1024,128]{2,1,0:T(8,128)(2,1)}) custom-call(s32[4]{0:T(128)} %pad_add_fusion.pos_ref, bf16[1024,1024]{1,0:T(8,128)(2,1)} %fusion.5.first_ref.refs_0_, f32[1,1024]{1,0:T(1,128)} %get-tuple-element.515.bq_ref, f32[1,1024]{1,0:T(1,128)} %get-tuple-element.514.bv_ref, ...), custom_call_target="tpu_custom_call" | custom-call | flops 1000 | bytes 1000 | tf_op jit(solution)/shard_map/pallas_call | solution.py:149
  102.9 20.6 %shard_map.255 = (bf16[512,1024]{1,0:T(8,128)(2,1)}, f32[512,1024]{1,0:T(8,128)}, f32[8,2,512]{2,1,0:T(2,128)}) custom-call(s32[4]{0:T(128)} %pad_add_fusion.pos_ref, bf16[8,512,128]{2,1,0:T(8,128)(2,1)} %get-tuple-element.277.q_ref, bf16[8,1024,128]{2,1,0:T(8,128)(2,1)} %get-tuple-element.278.k_ref, bf16[8,1024,128]{2,1,0:T(8,128)(2,1)} %get-tuple-element.279.v_ref, ...), custom_call_target="tpu_custom_call" | custom-call | flops 1000 | bytes 1000 | tf_op jit(solution)/shard_map/pallas_call | solution.py:149
  123.5 5.8 %collective-permute-done.13 = bf16[256,512]{1,0:T(8,128)(2,1)S(1)} collective-permute-done((bf16[256,512]{1,0:T(8,128)(2,1)S(1)}, bf16[256,512]{1,0:T(8,128)(2,1)S(1)}, u32[]{:S(2)}, u32[]{:S(2)}) %collective-permute-start.13) | collective-permute-done | bytes 262176 | tf_op jit(solution)/shard_map/ppermute | solution.py:52
  136.9 6.9 %shard_map.256 = (f32[512,1024]{1,0:T(8,128)}, bf16[512,1024]{1,0:T(8,128)(2,1)}) custom-call(s32[4]{0:T(128)} %pad_add_fusion.pos_ref, bf16[512,1024]{1,0:T(8,128)(2,1)} %get-tuple-element.289.mixed_ref.refs_3_, bf16[512,1024]{1,0:T(8,128)(2,1)} %tok_ref.3, f32[1,1024]{1,0:T(1,128)} %bitcast.100, f32[1,1024]{1,0:T(1,128)} %bitcast.98, f32[1,1024]{1,0:T(1,128)} %bitcast.101, ...), custom_call_target="tpu_custom_call" | custom-call | flops 1000 | bytes 1000 | tf_op jit(solution)/shard_map/pallas_call | solution.py:149
  152.9 13.5 %shard_map.257 = (bf16[512,4096]{1,0:T(8,128)(2,1)}, bf16[512,4096]{1,0:T(8,128)(2,1)}) custom-call(s32[4]{0:T(128)} %pad_add_fusion.pos_ref, bf16[512,1024]{1,0:T(8,128)(2,1)} %get-tuple-element.293.second_ref.refs_0_, f32[1,4096]{1,0:T(1,128)} %bitcast.96, bf16[32,256,640]{2,1,0:T(8,128)(2,1)} %bitcast.66), custom_call_target="tpu_custom_call" | custom-call | flops 1000 | bytes 1000 | tf_op jit(solution)/shard_map/pallas_call | solution.py:149
  166.4 7.3 %shard_map.258 = bf16[4,2,2,256,512]{4,3,2,1,0:T(8,128)(2,1)} custom-call(s32[4]{0:T(128)} %pad_add_fusion.pos_ref, bf16[512,1024]{1,0:T(8,128)(2,1)} %grad_ref.3, bf16[512,4096]{1,0:T(8,128)(2,1)} %get-tuple-element.483.refs_1_.gelu_ref), custom_call_target="tpu_custom_call" | custom-call | flops 1000 | bytes 1000 | tf_op jit(solution)/shard_map/pallas_call | solution.py:149
  183.2 10.9 %shard_map.259 = (bf16[512,4096]{1,0:T(8,128)(2,1)}, f32[1,4096]{1,0:T(1,128)}) custom-call(s32[4]{0:T(128)} %pad_add_fusion.pos_ref, bf16[512,4096]{1,0:T(8,128)(2,1)} %get-tuple-element.309.slope_ref, bf16[512,1024]{1,0:T(8,128)(2,1)} %grad_ref.3, bf16[2,2,256,512]{3,2,1,0:T(8,128)(2,1)} %copy-done.4, ...), custom_call_target="tpu_custom_call" | custom-call | flops 1000 | bytes 1000 | tf_op jit(solution)/shard_map/pallas_call | solution.py:149
  194.1 8.3 %shard_map.260 = (bf16[2,2,256,512]{3,2,1,0:T(8,128)(2,1)}, bf16[2,2,256,512]{3,2,1,0:T(8,128)(2,1)}, bf16[2,2,256,512]{3,2,1,0:T(8,128)(2,1)}, bf16[2,2,256,512]{3,2,1,0:T(8,128)(2,1)}) custom-call(s32[4]{0:T(128)} %pad_add_fusion.pos_ref, bf16[512,1024]{1,0:T(8,128)(2,1)} %grad_ref.3, bf16[512,4096]{1,0:T(8,128)(2,1)} %get-tuple-element.483.refs_1_.gelu_ref, ...), custom_call_target="tpu_custom_call" | custom-call | flops 1000 | bytes 1000 | tf_op jit(solution)/shard_map/pallas_call | solution.py:149
  203.5 13.3 %shard_map.261 = (f32[512,1024]{1,0:T(8,128)}, bf16[512,1024]{1,0:T(8,128)(2,1)}, f32[4,1024]{1,0:T(4,128)}) custom-call(s32[4]{0:T(128)} %pad_add_fusion.pos_ref, bf16[512,4096]{1,0:T(8,128)(2,1)} %get-tuple-element.329.pre_ref.refs_1_, bf16[512,1024]{1,0:T(8,128)(2,1)} %grad_ref.3, f32[512,1024]{1,0:T(8,128)} %get-tuple-element.330.middle_ref, ...), custom_call_target="tpu_custom_call" | custom-call | flops 1000 | bytes 1000 | tf_op jit(solution)/shard_map/pallas_call | solution.py:149
  216.9 5.8 %shard_map.263.grad_ref = bf16[512,1024]{1,0:T(8,128)(2,1)} custom-call(s32[4]{0:T(128)} %pad_add_fusion.pos_ref, bf16[512,1024]{1,0:T(8,128)(2,1)} %get-tuple-element.331.refs_2_.low_ref, bf16[32,256,640]{2,1,0:T(8,128)(2,1)} %bitcast.68), custom_call_target="tpu_custom_call" | custom-call | flops 1000 | bytes 1000 | tf_op jit(solution)/shard_map/pallas_call | solution.py:149
  222.7 8.5 %shard_map.262 = bf16[4,2,2,256,640]{4,3,2,1,0:T(8,128)(2,1)} custom-call(s32[4]{0:T(128)} %pad_add_fusion.pos_ref, bf16[512,1024]{1,0:T(8,128)(2,1)} %get-tuple-element.293.second_ref.refs_0_, bf16[512,4096]{1,0:T(8,128)(2,1)} %get-tuple-element.329.pre_ref.refs_1_, bf16[512,1024]{1,0:T(8,128)(2,1)} %get-tuple-element.331.refs_2_.low_ref, ...), custom_call_target="tpu_custom_call" | custom-call | flops 1000 | bytes 1000 | tf_op jit(solution)/shard_map/pallas_call | solution.py:149
  231.2 4.0 shard_map.264
  238.2 13.2 %shard_map.265 = (bf16[8,512,128]{2,1,0:T(8,128)(2,1)}, bf16[8,1024,128]{2,1,0:T(8,128)(2,1)}, bf16[8,1024,128]{2,1,0:T(8,128)(2,1)}, f32[2,1024]{1,0:T(2,128)}) custom-call(s32[4]{0:T(128)} %pad_add_fusion.pos_ref, bf16[8,512,128]{2,1,0:T(8,128)(2,1)} %get-tuple-element.277.q_ref, bf16[8,1024,128]{2,1,0:T(8,128)(2,1)} %get-tuple-element.278.k_ref, ...), custom_call_target="tpu_custom_call" | custom-call | flops 1000 | bytes 1000 | tf_op jit(solution)/shard_map/pallas_call | solution.py:149
  251.4 10.3 %shard_map.266 = (bf16[2,2,256,640]{3,2,1,0:T(8,128)(2,1)}, bf16[2,2,256,640]{3,2,1,0:T(8,128)(2,1)}, bf16[2,2,256,640]{3,2,1,0:T(8,128)(2,1)}, bf16[2,2,256,640]{3,2,1,0:T(8,128)(2,1)}) custom-call(s32[4]{0:T(128)} %pad_add_fusion.pos_ref, bf16[512,1024]{1,0:T(8,128)(2,1)} %get-tuple-element.293.second_ref.refs_0_, ...), custom_call_target="tpu_custom_call" | custom-call | flops 1000 | bytes 1000 | tf_op jit(solution)/shard_map/pallas_call | solution.py:149
  270.9 13.2 %shard_map.268 = (bf16[8,512,128]{2,1,0:T(8,128)(2,1)}, bf16[8,1024,128]{2,1,0:T(8,128)(2,1)}, bf16[8,1024,128]{2,1,0:T(8,128)(2,1)}, f32[2,1024]{1,0:T(2,128)}) custom-call(s32[4]{0:T(128)} %pad_add_fusion.pos_ref, bf16[8,512,128]{2,1,0:T(8,128)(2,1)} %get-tuple-element.277.q_ref, ...), custom_call_target="tpu_custom_call", output_to_operand_aliasing={{0}: (9, {}), {1}: (10, {}), {2}: (11, {}), {3}: (12, {})} | custom-call | flops 1000 | bytes 1000 | tf_op jit(solution)/shard_map/pallas_call | solution.py:149
  284.1 8.4 %shard_map.269 = bf16[4,2,2,256,384]{4,3,2,1,0:T(8,128)(2,1)} custom-call(s32[4]{0:T(128)} %pad_add_fusion.pos_ref, bf16[1024,1024]{1,0:T(8,128)(2,1)} %fusion.5.first_ref.refs_0_, bf16[8,512,128]{2,1,0:T(8,128)(2,1)} %get-tuple-element.435.refs_1_.dq_ref, bf16[8,1024,128]{2,1,0:T(8,128)(2,1)} %get-tuple-element.455.refs_2_.dk_ref, ...), custom_call_target="tpu_custom_call" | custom-call | flops 1000 | bytes 1000 | tf_op jit(solution)/shard_map/pallas_call | solution.py:149
  296.1 4.4 %shard_map.270 = (bf16[2,256,640]{2,1,0:T(8,128)(2,1)}, bf16[2,256,640]{2,1,0:T(8,128)(2,1)}, bf16[2,256,640]{2,1,0:T(8,128)(2,1)}, bf16[2,256,640]{2,1,0:T(8,128)(2,1)}) custom-call(s32[4]{0:T(128)} %pad_add_fusion.pos_ref, bf16[2,2,256,640]{3,2,1,0:T(8,128)(2,1)} %get-tuple-element.385.refs_0_, bf16[2,2,256,640]{3,2,1,0:T(8,128)(2,1)} %collective-permute-done.29.refs_1_, ...), custom_call_target="tpu_custom_call" | custom-call | flops 1000 | bytes 1000 | tf_op jit(solution)/shard_map/pallas_call | solution.py:149
  306.5 9.1 %shard_map.272 = (bf16[2,2,256,384]{3,2,1,0:T(8,128)(2,1)}, bf16[2,2,256,384]{3,2,1,0:T(8,128)(2,1)}, bf16[2,2,256,384]{3,2,1,0:T(8,128)(2,1)}, bf16[2,2,256,384]{3,2,1,0:T(8,128)(2,1)}) custom-call(s32[4]{0:T(128)} %pad_add_fusion.pos_ref, bf16[1024,1024]{1,0:T(8,128)(2,1)} %fusion.5.first_ref.refs_0_, ...), custom_call_target="tpu_custom_call" | custom-call | flops 1000 | bytes 1000 | tf_op jit(solution)/shard_map/pallas_call | solution.py:149
  326.7 12.4 %shard_map.274 = (f32[512,1024]{1,0:T(8,128)}, f32[2,1024]{1,0:T(2,128)}) custom-call(s32[4]{0:T(128)} %pad_add_fusion.pos_ref, bf16[8,512,128]{2,1,0:T(8,128)(2,1)} %get-tuple-element.435.refs_1_.dq_ref, bf16[8,1024,128]{2,1,0:T(8,128)(2,1)} %get-tuple-element.455.refs_2_.dk_ref, bf16[8,1024,128]{2,1,0:T(8,128)(2,1)} %get-tuple-element.456.refs_3_.dv_ref, ...), custom_call_target="tpu_custom_call" | custom-call | flops 1000 | bytes 1000 | tf_op jit(solution)/shard_map/pallas_call | solution.py:149
  342.2 3.6 shard_map.275
  349.4 9.5 %shard_map.276 = (bf16[512,1024]{1,0:T(8,128)(2,1)}, f32[2,1024]{1,0:T(2,128)}) custom-call(s32[4]{0:T(128)} %pad_add_fusion.pos_ref, bf16[8,1024,128]{2,1,0:T(8,128)(2,1)} %get-tuple-element.455.refs_2_.dk_ref, bf16[8,1024,128]{2,1,0:T(8,128)(2,1)} %get-tuple-element.456.refs_3_.dv_ref, bf16[512,1024]{1,0:T(8,128)(2,1)} %copy-done.1, f32[1,1024]{1,0:T(1,128)} %bitcast.94, ...), custom_call_target="tpu_custom_call" | custom-call | flops 1000 | bytes 1000 | tf_op jit(solution)/shard_map/pallas_call | solution.py:149
  370.0 10.7 %shard_map.278 = bf16[512,1024]{1,0:T(8,128)(2,1)} custom-call(s32[4]{0:T(128)} %pad_add_fusion.pos_ref, bf16[512,4096]{1,0:T(8,128)(2,1)} %get-tuple-element.483.refs_1_.gelu_ref, f32[512,1024]{1,0:T(8,128)} %get-tuple-element.330.middle_ref, f32[1,1024]{1,0:T(1,128)} %bitcast.102, bf16[2,2,256,512]{3,2,1,0:T(8,128)(2,1)} %copy-done.4, ...), custom_call_target="tpu_custom_call" | custom-call | flops 1000 | bytes 1000 | tf_op jit(solution)/shard_map/pallas_call | solution.py:149
  383.7 3.6 collective-permute-start.50
  387.4 4.2 %collective-permute-done.50 = f32[96,128]{1,0:T(8,128)S(1)} collective-permute-done((f32[96,128]{1,0:T(8,128)S(1)}, f32[96,128]{1,0:T(8,128)S(1)}, u32[]{:S(2)}, u32[]{:S(2)}) %collective-permute-start.50) | collective-permute-done | bytes 49184 | tf_op jit(solution)/shard_map/ppermute | solution.py:52
  (204 shorter events, 110.0 us)
Async XLA Ops:
  7.2 125.6 %all-gather.3.cloned.1.call-start = ((), (), s32[]{:S(2)}) async-start(), calls=%async_computation | async-start | bytes 10813440 | tf_op jit(solution)/shard_map/all_gather | solution.py:886
  9.1 33.2 %collective-permute-start.3 = (bf16[512,1024]{1,0:T(8,128)(2,1)}, bf16[512,1024]{1,0:T(8,128)(2,1)S(1)}, u32[]{:S(2)}, u32[]{:S(2)}) collective-permute-start(bf16[512,1024]{1,0:T(8,128)(2,1)} %tok_ref.3), channel_id=1, source_target_pairs={{0,1},{2,3},{4,5},{6,7},{8,9},{10,11},{12,13},{14,15},{16,17},{18,... | collective-permute-start | bytes 3145736 | tf_op jit(solution)/shard_map/ppermute | solution.py:890
  18.9 23.4 %collective-permute-start.1 = (bf16[256,384]{1,0:T(8,128)(2,1)S(1)}, bf16[256,384]{1,0:T(8,128)(2,1)S(1)}, u32[]{:S(2)}, u32[]{:S(2)}) collective-permute-start(bf16[256,384]{1,0:T(8,128)(2,1)S(1)} %copy.35), channel_id=1, source_target_pairs={{0,4},{2,6},{4,0},{6,2},{1,5},{3,7},{5,1},{7,3},{8,12},{10,14},{12... | collective-permute-start | bytes 589832 | tf_op jit(solution)/shard_map/ppermute | solution.py:52
  18.9 23.4 %collective-permute-start = (bf16[256,384]{1,0:T(8,128)(2,1)S(1)}, bf16[256,384]{1,0:T(8,128)(2,1)S(1)}, u32[]{:S(2)}, u32[]{:S(2)}) collective-permute-start(bf16[256,384]{1,0:T(8,128)(2,1)S(1)} %copy.35), channel_id=1, source_target_pairs={{0,2},{2,0},{4,6},{6,4},{1,3},{3,1},{5,7},{7,5},{8,10},{10,8},{12,... | collective-permute-start | bytes 589832 | tf_op jit(solution)/shard_map/ppermute | solution.py:52
  44.2 20.1 %collective-permute-start.4 = (bf16[2,256,384]{2,1,0:T(8,128)(2,1)S(1)}, bf16[2,256,384]{2,1,0:T(8,128)(2,1)S(1)}, u32[]{:S(2)}, u32[]{:S(2)}) collective-permute-start(bf16[2,256,384]{2,1,0:T(8,128)(2,1)S(1)} %get-tuple-element.505), channel_id=1, source_target_pairs={{0,1},{1,0},{2,3},{3,2},{4,5},{5,4},{6,7},{7,6},{8,9},{9,8},{10,11... | collective-permute-start | bytes 1179656 | tf_op jit(solution)/shard_map/ppermute | solution.py:52
  57.6 25.1 %collective-permute-start.7 = (bf16[2,2,256,384]{3,2,1,0:T(8,128)(2,1)S(1)}, bf16[2,2,256,384]{3,2,1,0:T(8,128)(2,1)}, u32[]{:S(2)}, u32[]{:S(2)}) collective-permute-start(bf16[2,2,256,384]{3,2,1,0:T(8,128)(2,1)S(1)} %pad_maximum_fusion.4.rest_2_), channel_id=1, source_target_pairs={{0,1},{1,0},{2,3},{3,2},{4,5},{5,4},{6,7},{7,6},{8,9},{9,8},{10,11... | collective-permute-start | bytes 2359304 | tf_op jit(solution)/shard_map/ppermute | solution.py:52
  65.3 18.0 %collective-permute-start.5 = (bf16[2,2,256,384]{3,2,1,0:T(8,128)(2,1)}, bf16[2,2,256,384]{3,2,1,0:T(8,128)(2,1)}, u32[]{:S(2)}, u32[]{:S(2)}) collective-permute-start(bf16[2,2,256,384]{3,2,1,0:T(8,128)(2,1)} %pad_maximum_fusion.3.rest_0_), channel_id=1, source_target_pairs={{0,16},{16,0},{1,17},{17,1},{2,18},{18,2},{3,19},{19,3},{4,20},{20... | collective-permute-start | bytes 2359304 | tf_op jit(solution)/shard_map/ppermute | solution.py:52
  66.0 17.8 %collective-permute-start.10 = (bf16[2,2,256,384]{3,2,1,0:T(8,128)(2,1)S(1)}, bf16[2,2,256,384]{3,2,1,0:T(8,128)(2,1)}, u32[]{:S(2)}, u32[]{:S(2)}) collective-permute-start(bf16[2,2,256,384]{3,2,1,0:T(8,128)(2,1)S(1)} %pad_maximum_fusion.4.rest_2_), channel_id=1, source_target_pairs={{0,8},{8,0},{1,9},{9,1},{2,10},{10,2},{3,11},{11,3},{4,12},{12,4},... | collective-permute-start | bytes 2359304 | tf_op jit(solution)/shard_map/ppermute | solution.py:52
  66.1 17.8 %collective-permute-start.8 = (bf16[2,2,256,384]{3,2,1,0:T(8,128)(2,1)}, bf16[2,2,256,384]{3,2,1,0:T(8,128)(2,1)}, u32[]{:S(2)}, u32[]{:S(2)}) collective-permute-start(bf16[2,2,256,384]{3,2,1,0:T(8,128)(2,1)} %pad_maximum_fusion.3.rest_0_), channel_id=1, source_target_pairs={{0,8},{8,0},{1,9},{9,1},{2,10},{10,2},{3,11},{11,3},{4,12},{12,4},... | collective-permute-start | bytes 2359304 | tf_op jit(solution)/shard_map/ppermute | solution.py:52
  83.8 39.7 %collective-permute-start.14 = (bf16[256,512]{1,0:T(8,128)(2,1)S(1)}, bf16[256,512]{1,0:T(8,128)(2,1)S(1)}, u32[]{:S(2)}, u32[]{:S(2)}) collective-permute-start(bf16[256,512]{1,0:T(8,128)(2,1)S(1)} %copy-done.18), channel_id=1, source_target_pairs={{0,6},{2,4},{4,2},{6,0},{1,7},{3,5},{5,3},{7,1},{8,14},{10,12},{12... | collective-permute-start | bytes 786440 | tf_op jit(solution)/shard_map/ppermute | solution.py:52
  83.8 45.5 %collective-permute-start.13 = (bf16[256,512]{1,0:T(8,128)(2,1)S(1)}, bf16[256,512]{1,0:T(8,128)(2,1)S(1)}, u32[]{:S(2)}, u32[]{:S(2)}) collective-permute-start(bf16[256,512]{1,0:T(8,128)(2,1)S(1)} %copy-done.18), channel_id=1, source_target_pairs={{0,4},{2,6},{4,0},{6,2},{1,5},{3,7},{5,1},{7,3},{8,12},{10,14},{12... | collective-permute-start | bytes 786440 | tf_op jit(solution)/shard_map/ppermute | solution.py:52
  83.9 45.4 %collective-permute-start.12 = (bf16[256,512]{1,0:T(8,128)(2,1)S(1)}, bf16[256,512]{1,0:T(8,128)(2,1)}, u32[]{:S(2)}, u32[]{:S(2)}) collective-permute-start(bf16[256,512]{1,0:T(8,128)(2,1)S(1)} %copy-done.18), channel_id=1, source_target_pairs={{0,2},{2,0},{4,6},{6,4},{1,3},{3,1},{5,7},{7,5},{8,10},{10,8},{12,... | collective-permute-start | bytes 786440 | tf_op jit(solution)/shard_map/ppermute | solution.py:52
  149.3 24.4 %collective-permute-start.20 = (bf16[2,2,256,512]{3,2,1,0:T(8,128)(2,1)S(1)}, bf16[2,2,256,512]{3,2,1,0:T(8,128)(2,1)S(1)}, u32[]{:S(2)}, u32[]{:S(2)}) collective-permute-start(bf16[2,2,256,512]{3,2,1,0:T(8,128)(2,1)S(1)} %pad_maximum_fusion.2.rest_2_), channel_id=1, source_target_pairs={{0,8},{8,0},{1,9},{9,1},{2,10},{10,2},{3,11},{11,3},{4,12},{12,4},... | collective-permute-start | bytes 3145736 | tf_op jit(solution)/shard_map/ppermute | solution.py:52
  149.4 25.7 %collective-permute-start.18 = (bf16[2,2,256,512]{3,2,1,0:T(8,128)(2,1)S(1)}, bf16[2,2,256,512]{3,2,1,0:T(8,128)(2,1)}, u32[]{:S(2)}, u32[]{:S(2)}) collective-permute-start(bf16[2,2,256,512]{3,2,1,0:T(8,128)(2,1)S(1)} %pad_maximum_fusion.2.rest_2_), channel_id=1, source_target_pairs={{0,1},{1,0},{2,3},{3,2},{4,5},{5,4},{6,7},{7,6},{8,9},{9,8},{10,11... | collective-permute-start | bytes 3145736 | tf_op jit(solution)/shard_map/ppermute | solution.py:52
  152.1 23.0 %collective-permute-start.19 = (bf16[2,2,256,512]{3,2,1,0:T(8,128)(2,1)S(1)}, bf16[2,2,256,512]{3,2,1,0:T(8,128)(2,1)}, u32[]{:S(2)}, u32[]{:S(2)}) collective-permute-start(bf16[2,2,256,512]{3,2,1,0:T(8,128)(2,1)S(1)} %pad_maximum_fusion.1.rest_0_), channel_id=1, source_target_pairs={{0,8},{8,0},{1,9},{9,1},{2,10},{10,2},{3,11},{11,3},{4,12},{12,4},... | collective-permute-start | bytes 3145736 | tf_op jit(solution)/shard_map/ppermute | solution.py:52
  152.3 25.5 %collective-permute-start.17 = (bf16[2,2,256,512]{3,2,1,0:T(8,128)(2,1)S(1)}, bf16[2,2,256,512]{3,2,1,0:T(8,128)(2,1)}, u32[]{:S(2)}, u32[]{:S(2)}) collective-permute-start(bf16[2,2,256,512]{3,2,1,0:T(8,128)(2,1)S(1)} %pad_maximum_fusion.1.rest_0_), channel_id=1, source_target_pairs={{0,16},{16,0},{1,17},{17,1},{2,18},{18,2},{3,19},{19,3},{4,20},{20... | collective-permute-start | bytes 3145736 | tf_op jit(solution)/shard_map/ppermute | solution.py:52
  202.4 28.7 %collective-permute-start.24 = (bf16[2,2,256,512]{3,2,1,0:T(8,128)(2,1)}, bf16[2,2,256,512]{3,2,1,0:T(8,128)(2,1)}, u32[]{:S(2)}, u32[]{:S(2)}) collective-permute-start(bf16[2,2,256,512]{3,2,1,0:T(8,128)(2,1)} %get-tuple-element.326), channel_id=1, source_target_pairs={{0,16},{16,0},{1,17},{17,1},{2,18},{18,2},{3,19},{19,3},{4,20},{20... | collective-permute-start | bytes 3145736 | tf_op jit(solution)/shard_map/ppermute | solution.py:52
  203.0 28.2 %collective-permute-start.25 = (bf16[2,2,256,512]{3,2,1,0:T(8,128)(2,1)}, bf16[2,2,256,512]{3,2,1,0:T(8,128)(2,1)}, u32[]{:S(2)}, u32[]{:S(2)}) collective-permute-start(bf16[2,2,256,512]{3,2,1,0:T(8,128)(2,1)} %get-tuple-element.328), channel_id=1, source_target_pairs={{0,1},{1,0},{2,3},{3,2},{4,5},{5,4},{6,7},{7,6},{8,9},{9,8},{10,11... | collective-permute-start | bytes 3145736 | tf_op jit(solution)/shard_map/ppermute | solution.py:52
  264.9 30.9 %collective-permute-start.29 = (bf16[2,2,256,640]{3,2,1,0:T(8,128)(2,1)}, bf16[2,2,256,640]{3,2,1,0:T(8,128)(2,1)}, u32[]{:S(2)}, u32[]{:S(2)}) collective-permute-start(bf16[2,2,256,640]{3,2,1,0:T(8,128)(2,1)} %get-tuple-element.378), channel_id=1, source_target_pairs={{0,16},{16,0},{1,17},{17,1},{2,18},{18,2},{3,19},{19,3},{4,20},{20... | collective-permute-start | bytes 3932168 | tf_op jit(solution)/shard_map/ppermute | solution.py:52
  266.0 30.1 %collective-permute-start.30 = (bf16[2,2,256,640]{3,2,1,0:T(8,128)(2,1)}, bf16[2,2,256,640]{3,2,1,0:T(8,128)(2,1)}, u32[]{:S(2)}, u32[]{:S(2)}) collective-permute-start(bf16[2,2,256,640]{3,2,1,0:T(8,128)(2,1)} %get-tuple-element.380), channel_id=1, source_target_pairs={{0,1},{1,0},{2,3},{3,2},{4,5},{5,4},{6,7},{7,6},{8,9},{9,8},{10,11... | collective-permute-start | bytes 3932168 | tf_op jit(solution)/shard_map/ppermute | solution.py:52
  266.5 25.9 %collective-permute-start.31 = (bf16[256,512]{1,0:T(8,128)(2,1)}, bf16[256,512]{1,0:T(8,128)(2,1)S(1)}, u32[]{:S(2)}, u32[]{:S(2)}) collective-permute-start(bf16[256,512]{1,0:T(8,128)(2,1)} %get-tuple-element.382), channel_id=1, source_target_pairs={{0,2},{2,0},{4,6},{6,4},{1,3},{3,1},{5,7},{7,5},{8,10},{10,8},{12,... | collective-permute-start | bytes 786440 | tf_op jit(solution)/shard_map/ppermute | solution.py:52
  266.5 25.9 %collective-permute-start.32 = (bf16[256,512]{1,0:T(8,128)(2,1)}, bf16[256,512]{1,0:T(8,128)(2,1)}, u32[]{:S(2)}, u32[]{:S(2)}) collective-permute-start(bf16[256,512]{1,0:T(8,128)(2,1)} %get-tuple-element.383), channel_id=1, source_target_pairs={{0,4},{2,6},{4,0},{6,2},{1,5},{3,7},{5,1},{7,3},{8,12},{10,14},{12... | collective-permute-start | bytes 786440 | tf_op jit(solution)/shard_map/ppermute | solution.py:52
  268.6 23.9 %collective-permute-start.33 = (bf16[256,512]{1,0:T(8,128)(2,1)}, bf16[256,512]{1,0:T(8,128)(2,1)}, u32[]{:S(2)}, u32[]{:S(2)}) collective-permute-start(bf16[256,512]{1,0:T(8,128)(2,1)} %get-tuple-element.384), channel_id=1, source_target_pairs={{0,6},{2,4},{4,2},{6,0},{1,7},{3,5},{5,3},{7,1},{8,14},{10,12},{12... | collective-permute-start | bytes 786440 | tf_op jit(solution)/shard_map/ppermute | solution.py:52
  300.5 17.4 %collective-permute-start.35 = (bf16[2,256,640]{2,1,0:T(8,128)(2,1)}, bf16[2,256,640]{2,1,0:T(8,128)(2,1)S(1)}, u32[]{:S(2)}, u32[]{:S(2)}) collective-permute-start(bf16[2,256,640]{2,1,0:T(8,128)(2,1)} %get-tuple-element.411), channel_id=1, source_target_pairs={{0,1},{1,0},{2,3},{3,2},{4,5},{5,4},{6,7},{7,6},{8,9},{9,8},{10,11... | collective-permute-start | bytes 1966088 | tf_op jit(solution)/shard_map/ppermute | solution.py:52
  301.2 17.1 %collective-permute-start.36 = (bf16[2,256,640]{2,1,0:T(8,128)(2,1)}, bf16[2,256,640]{2,1,0:T(8,128)(2,1)}, u32[]{:S(2)}, u32[]{:S(2)}) collective-permute-start(bf16[2,256,640]{2,1,0:T(8,128)(2,1)} %get-tuple-element.413), channel_id=1, source_target_pairs={{0,16},{16,0},{1,17},{17,1},{2,18},{18,2},{3,19},{19,3},{4,20},{20... | collective-permute-start | bytes 1966088 | tf_op jit(solution)/shard_map/ppermute | solution.py:52
  318.7 22.5 %collective-permute-start.37 = (bf16[2,2,256,384]{3,2,1,0:T(8,128)(2,1)}, bf16[2,2,256,384]{3,2,1,0:T(8,128)(2,1)S(1)}, u32[]{:S(2)}, u32[]{:S(2)}) collective-permute-start(bf16[2,2,256,384]{3,2,1,0:T(8,128)(2,1)} %get-tuple-element.418), channel_id=1, source_target_pairs={{0,16},{16,0},{1,17},{17,1},{2,18},{18,2},{3,19},{19,3},{4,20},{20... | collective-permute-start | bytes 2359304 | tf_op jit(solution)/shard_map/ppermute | solution.py:52
  320.2 21.1 %collective-permute-start.38 = (bf16[2,2,256,384]{3,2,1,0:T(8,128)(2,1)}, bf16[2,2,256,384]{3,2,1,0:T(8,128)(2,1)}, u32[]{:S(2)}, u32[]{:S(2)}) collective-permute-start(bf16[2,2,256,384]{3,2,1,0:T(8,128)(2,1)} %get-tuple-element.420), channel_id=1, source_target_pairs={{0,1},{1,0},{2,3},{3,2},{4,5},{5,4},{6,7},{7,6},{8,9},{9,8},{10,11... | collective-permute-start | bytes 2359304 | tf_op jit(solution)/shard_map/ppermute | solution.py:52
  324.7 16.6 %collective-permute-start.40 = (bf16[256,640]{1,0:T(8,128)(2,1)}, bf16[256,640]{1,0:T(8,128)(2,1)S(1)}, u32[]{:S(2)}, u32[]{:S(2)}) collective-permute-start(bf16[256,640]{1,0:T(8,128)(2,1)} %get-tuple-element.434), channel_id=1, source_target_pairs={{0,4},{2,6},{4,0},{6,2},{1,5},{3,7},{5,1},{7,3},{8,12},{10,14},{12... | collective-permute-start | bytes 983048 | tf_op jit(solution)/shard_map/ppermute | solution.py:52
  362.8 38.0 %collective-permute-start.49 = (bf16[512,1024]{1,0:T(8,128)(2,1)}, bf16[512,1024]{1,0:T(8,128)(2,1)}, u32[]{:S(2)}, u32[]{:S(2)}) collective-permute-start(bf16[512,1024]{1,0:T(8,128)(2,1)} %get-tuple-element.492), channel_id=1, source_target_pairs={{1,0},{3,2},{5,4},{7,6},{9,8},{11,10},{13,12},{15,14},{17,16},{19,... | collective-permute-start | bytes 3145736 | tf_op jit(solution)/shard_map/ppermute | solution.py:1030
  364.1 19.6 %collective-permute-start.45 = (bf16[256,384]{1,0:T(8,128)(2,1)}, bf16[256,384]{1,0:T(8,128)(2,1)S(1)}, u32[]{:S(2)}, u32[]{:S(2)}) collective-permute-start(bf16[256,384]{1,0:T(8,128)(2,1)} %get-tuple-element.479), channel_id=1, source_target_pairs={{0,2},{2,0},{4,6},{6,4},{1,3},{3,1},{5,7},{7,5},{8,10},{10,8},{12,... | collective-permute-start | bytes 589832 | tf_op jit(solution)/shard_map/ppermute | solution.py:52
  364.2 19.5 %collective-permute-start.46 = (bf16[256,384]{1,0:T(8,128)(2,1)}, bf16[256,384]{1,0:T(8,128)(2,1)S(1)}, u32[]{:S(2)}, u32[]{:S(2)}) collective-permute-start(bf16[256,384]{1,0:T(8,128)(2,1)} %get-tuple-element.480), channel_id=1, source_target_pairs={{0,4},{2,6},{4,0},{6,2},{1,5},{3,7},{5,1},{7,3},{8,12},{10,14},{12... | collective-permute-start | bytes 589832 | tf_op jit(solution)/shard_map/ppermute | solution.py:52
  367.1 16.6 %collective-permute-start.47 = (bf16[256,384]{1,0:T(8,128)(2,1)}, bf16[256,384]{1,0:T(8,128)(2,1)S(1)}, u32[]{:S(2)}, u32[]{:S(2)}) collective-permute-start(bf16[256,384]{1,0:T(8,128)(2,1)} %get-tuple-element.481), channel_id=1, source_target_pairs={{0,6},{2,4},{4,2},{6,0},{1,7},{3,5},{5,3},{7,1},{8,14},{10,12},{12... | collective-permute-start | bytes 589832 | tf_op jit(solution)/shard_map/ppermute | solution.py:52
  (54 other events, 654.3 us)
Sparse Core Ops, SparseCore 0:
  11.5 121.1 all-gather.2

commit v5 on v4

--- a/solution.py
+++ b/solution.py
@@ -267,7 +267,7 @@
     heads = width // HEAD_DIM
     step = min(rows, 128)
 
-    def body(pos_ref, q_ref, k_ref, v_ref, sk_ref, sq_ref, mixed_ref, exact_ref, lse_ref, bias):
+    def body(pos_ref, q_ref, k_ref, v_ref, sk_ref, sq_ref, mixed_ref, exact_ref, probs_ref, bias):
         @pl.when(pl.program_id(0) == 0)
         def _():
             bias[...] = mask_bias(sk_ref[...], sq_ref[...], rows)
@@ -281,9 +281,12 @@
                 top = jnp.max(scores, axis=0, keepdims=True)
                 expo = jnp.exp(scores - top)
                 total = jnp.sum(expo, axis=0, keepdims=True)
-                share = jnp.broadcast_to(1.0 / total, (8, step)).T[:, :1]
-                outs.append(dot_tn(expo.astype(BF), v_ref[0, :keys]) * share)
-                lse_ref[0, head : head + 1, here] = top + jnp.log(total)
+                probs = (expo * (1.0 / total)).astype(BF)
+                outs.append(dot_tn(probs, v_ref[0, :keys]))
+                probs_ref[0, head, :keys, here] = probs
+                end = both - rows + min(rows, (tile // 2 + 1) * 2 * step)
+                if end > keys:
+                    probs_ref[0, head, keys:end, here] = jnp.zeros((end - keys, step), BF)
             lane = lax.broadcasted_iota(jnp.int32, outs[0].shape, 1)
             out = outs[0]
             for head in range(1, heads):
@@ -300,9 +303,9 @@
         [
             shape((rows, blocks * width), BF),
             shape((rows, blocks * width), F32),
-            shape((blocks, heads, rows), F32),
+            shape((blocks, heads, both, rows), BF),
         ],
-        [at_cols(rows, width), at_cols(rows, width), at_lead(1, heads, rows)],
+        [at_cols(rows, width), at_cols(rows, width), at_lead(1, heads, both, rows)],
         [pltpu.VMEM((both, rows), F32)],
     )
 
@@ -507,7 +510,7 @@
     )[0]
 
 
-def attend_back_call(pos, span, query, key, value, seg_k, seg_q, lse, mixed_grad, exact, earlier=()):
+def attend_back_call(pos, span, query, key, value, probs, mixed_grad, exact, earlier=()):
     blocks, both, width = key.shape
     rows = query.shape[1]
     heads = width // HEAD_DIM
@@ -515,12 +518,8 @@
     begin = span[0]
     n = len(earlier)
 
-    def body(pos_ref, q_ref, k_ref, v_ref, sk_ref, sq_ref, lse_ref, grad_ref, exact_ref, *rest):
-        dq_ref, dk_ref, dv_ref, sums_ref, bias, dq_t, dk, dv = rest[n:]
-
-        @pl.when(pl.program_id(0) == 0)
-        def _():
-            bias[...] = mask_bias(sk_ref[...], sq_ref[...], rows)
+    def body(pos_ref, q_ref, k_ref, v_ref, p_ref, grad_ref, exact_ref, *rest):
+        dq_ref, dk_ref, dv_ref, sums_ref, dq_t, dk, dv = rest[n:]
 
         key_t = k_ref[0].T
         inner_t = (grad_ref[...].astype(F32) * exact_ref[...]).T
@@ -533,12 +532,11 @@
                 lanes = slice(head * HEAD_DIM, (head + 1) * HEAD_DIM)
                 q_head = head_only(q_ref[0, here], head)
                 g_head = head_only(grad_ref[here], head)
-                scores = dot_nt(k_ref[0, :keys], q_head) + bias[:keys, here]
-                probs = jnp.exp(scores - lse_ref[0, head : head + 1, here])
+                low = p_ref[0, head, :keys, here]
                 prob_grad = dot_nt(v_ref[0, :keys], g_head)
                 inner = jnp.sum(inner_t[lanes, here], axis=0, keepdims=True)
-                score_grad = (probs * (prob_grad - inner)).astype(BF)
-                dv[:keys] += dot(probs.astype(BF), g_head)
+                score_grad = (low.astype(F32) * (prob_grad - inner)).astype(BF)
+                dv[:keys] += dot(low, g_head)
                 dk[:keys] += dot(score_grad, q_head)
                 dq_t[lanes, here] = dot(key_t[lanes, :keys], score_grad)
         dq = (dq_t[...].T * HEAD_DIM**-0.5).astype(BF)
@@ -554,14 +552,12 @@
         body,
         pos,
         (span[1] - span[0],),
-        (query, key, value, seg_k, seg_q, lse, mixed_grad, exact, *earlier),
+        (query, key, value, probs, mixed_grad, exact, *earlier),
         [
             at_lead(1, rows, width, place=at),
             at_lead(1, both, width, place=at),
             at_lead(1, both, width, place=at),
-            full((both, 1)),
-            full((1, rows)),
-            at_lead(1, heads, rows, place=at),
+            at_lead(1, heads, both, rows, place=at),
             at_cols(rows, width, at),
             at_cols(rows, width, at),
         ]
@@ -579,12 +575,11 @@
             at_cols(2, width, at),
         ],
         [
-            pltpu.VMEM((both, rows), F32),
             pltpu.VMEM((width, rows), F32),
             pltpu.VMEM((both, width), F32),
             pltpu.VMEM((both, width), F32),
         ],
-        {9: 0, 10: 1, 11: 2, 12: 3} if n else {},
+        {7: 0, 8: 1, 9: 2, 10: 3} if n else {},
     )
 
 
@@ -906,7 +901,7 @@
     down.one()
     qkv.parts, first = stage(qkv.parts, first)
     query, key, value = qkv_call(lay, pos, first, b_qv[0:1], b_qv[1:2], qkv.parts, width)
-    mixed, exact, lse = attend_call(pos, query, key, value, seg_k, seg_q)
+    mixed, exact, probs = attend_call(pos, query, key, value, seg_k, seg_q)
     mixed, up_parts = stage(down, mixed, up_parts)
     down.two()
     middle, second = branch_call(
@@ -961,7 +956,7 @@
     grad_up.sent, mixed_grad = stage(grad_down, grad_up.sent, mixed_grad)
     grad_down.send_two()
     grad_up.swap()
-    partial = attend_back_call(pos, (0, half), query, key, value, seg_k, seg_q, lse, mixed_grad, exact)
+    partial = attend_back_call(pos, (0, half), query, key, value, probs, mixed_grad, exact)
     partial, grad_up.received = stage(grad_down, partial, grad_up.received)
     grad_down.sum_two()
     grad_up.own()
@@ -969,7 +964,7 @@
     grad_up.send_one()
     grad_down.send_three()
     dq, dk, dv, sums_qv = attend_back_call(
-        pos, (half, blocks), query, key, value, seg_k, seg_q, lse, mixed_grad, exact, partial
+        pos, (half, blocks), query, key, value, probs, mixed_grad, exact, partial
     )
 
     def qkv_tile(left, ins, xs):
@@ -1030,11 +1025,12 @@
     back = lax.ppermute(back, "tx", [(1, 0)])
     grad_up.sum_three((hidden, width))
     result = result_call(lay, pos, gelu, middle, row(b_down), down.parts, hidden)
-    pieces, result, grad_up.out = stage(grad_qkv, pieces, result, grad_up.out)
+    pieces, result, back, grad_up.out = stage(grad_qkv, pieces, result, back, grad_up.out)
     small = sum(pieces)
+    token_grad = (first_grad + back.astype(F32)).astype(BF)
     small = small + trade(small, "tx", 2, 1)
+    small, token_grad = stage(small, token_grad)
     small = sum(around(small, "tz", nz)).reshape(-1)
-    token_grad = (first_grad + back.astype(F32)).astype(BF)
     grad_qkv.sum_three(((3, width),))
     at = 4 * dim
     late = small[at + gelu.shape[1] :]

time: 415 us -> 415 us (level)
  waiting for transfers between devices: 91.6 us -> 98.6 us
  starting transfers between devices: 58.3 us -> 53.3 us
    ppermute x1, waiting for transfers between devices: 0.01 us -> 7.75 us  [per_device(): back = lax.ppermute(back, 'tx', [(1, 0)])]
    ppermute x52, starting transfers between devices: 52 us -> 47.1 us  [trade(): return lax.ppermute(value, axis, [(s, s ^ distance) for s in range(size)])]
  transfers between devices with their start and end apart: 55 -> 55, of which waited for: 23 -> 25; matrix products, arithmetic and copies ran while one was open for 3% -> 4% of each run, Pallas kernels for 46% -> 46%
where the time goes in v5:
time: 415 us; the launch traced here: 411 us
  Pallas kernels  221 us (53%)
  waiting for transfers between devices  98.6 us (24%)
  starting transfers between devices  53.3 us (13%)
  between operations  14.9 us (4%)
  other arithmetic  14.7 us (4%)
  local copies, waits for them, and re-layouts  8.33 us (2%)
    pallas_call x27, Pallas kernels, kernel_call(): pl.pallas_call(body, out_shape=outs, grid_spec=pltpu.PrefetchScalarGridSp...  221 us
    ppermute x52, waiting for transfers between devices, trade(): return lax.ppermute(value, axis, [(s, s ^ distance) for s in range(size)])  87.4 us
    ppermute x52, starting transfers between devices, trade(): return lax.ppermute(value, axis, [(s, s ^ distance) for s in range(size)])  47.1 us
  transfers between devices with their start and end apart: 55, of which 25 were waited for; matrix products, arithmetic and copies ran while one was open for 4% of the time, Pallas kernels for 46%

profile of v5, /device:TPU:0, one launch (start us, length us, event | category | flops | bytes accessed | tf_op | source)
XLA Modules:
  0.0 411.0 jit_solution(203298244666900051)
XLA Ops:
  9.1 4.9 %collective-permute-start.3 = (bf16[512,1024]{1,0:T(8,128)(2,1)}, bf16[512,1024]{1,0:T(8,128)(2,1)S(1)}, u32[]{:S(2)}, u32[]{:S(2)}) collective-permute-start(bf16[512,1024]{1,0:T(8,128)(2,1)} %tok_ref.3), channel_id=1, source_target_pairs={{0,1},{2,3},{4,5},{6,7},{8,9},{10,11},{12,13},{14,15},{16,17},{18,... | collective-permute-start | bytes 3145736 | tf_op jit(solution)/shard_map/ppermute | solution.py:885
  15.2 3.7 collective-permute-start.2
  20.5 4.5 %collective-permute-done.2 = bf16[256,384]{1,0:T(8,128)(2,1)S(1)} collective-permute-done((bf16[256,384]{1,0:T(8,128)(2,1)S(1)}, bf16[256,384]{1,0:T(8,128)(2,1)S(1)}, u32[]{:S(2)}, u32[]{:S(2)}) %collective-permute-start.2) | collective-permute-done | bytes 196640 | tf_op jit(solution)/shard_map/ppermute | solution.py:52
  25.0 17.3 %collective-permute-done.1 = bf16[256,384]{1,0:T(8,128)(2,1)S(1)} collective-permute-done((bf16[256,384]{1,0:T(8,128)(2,1)S(1)}, bf16[256,384]{1,0:T(8,128)(2,1)S(1)}, u32[]{:S(2)}, u32[]{:S(2)}) %collective-permute-start.1) | collective-permute-done | bytes 196640 | tf_op jit(solution)/shard_map/ppermute | solution.py:52
  44.7 12.8 %collective-permute-done.6 = bf16[2,256,384]{2,1,0:T(8,128)(2,1)S(1)} collective-permute-done((bf16[2,256,384]{2,1,0:T(8,128)(2,1)S(1)}, bf16[2,256,384]{2,1,0:T(8,128)(2,1)S(1)}, u32[]{:S(2)}, u32[]{:S(2)}) %collective-permute-start.6) | collective-permute-done | bytes 393248 | tf_op jit(solution)/shard_map/ppermute | solution.py:52
  57.6 6.7 %collective-permute-done.4 = bf16[2,256,384]{2,1,0:T(8,128)(2,1)S(1)} collective-permute-done((bf16[2,256,384]{2,1,0:T(8,128)(2,1)S(1)}, bf16[2,256,384]{2,1,0:T(8,128)(2,1)S(1)}, u32[]{:S(2)}, u32[]{:S(2)}) %collective-permute-start.4) | collective-permute-done | bytes 393248 | tf_op jit(solution)/shard_map/ppermute | solution.py:52
  69.6 13.1 %collective-permute-done.7.rest_3_ = bf16[2,2,256,384]{3,2,1,0:T(8,128)(2,1)} collective-permute-done((bf16[2,2,256,384]{3,2,1,0:T(8,128)(2,1)S(1)}, bf16[2,2,256,384]{3,2,1,0:T(8,128)(2,1)}, u32[]{:S(2)}, u32[]{:S(2)}) %collective-permute-start.7) | collective-permute-done | bytes 786464 | tf_op jit(solution)/shard_map/ppermute | solution.py:52
  84.0 4.3 %collective-permute-start.12 = (bf16[256,512]{1,0:T(8,128)(2,1)S(1)}, bf16[256,512]{1,0:T(8,128)(2,1)}, u32[]{:S(2)}, u32[]{:S(2)}) collective-permute-start(bf16[256,512]{1,0:T(8,128)(2,1)S(1)} %copy-done.18), channel_id=1, source_target_pairs={{0,2},{2,0},{4,6},{6,4},{1,3},{3,1},{5,7},{7,5},{8,10},{10,8},{12,... | collective-permute-start | bytes 786440 | tf_op jit(solution)/shard_map/ppermute | solution.py:52
  91.7 11.4 %shard_map.254 = (bf16[8,512,128]{2,1,0:T(8,128)(2,1)}, bf16[8,1024,128]{2,1,0:T(8,128)(2,1)}, bf16[8,1024,128]{2,1,0:T(8,128)(2,1)}) custom-call(s32[4]{0:T(128)} %pad_add_fusion.pos_ref, bf16[1024,1024]{1,0:T(8,128)(2,1)} %fusion.5.first_ref.refs_0_, f32[1,1024]{1,0:T(1,128)} %get-tuple-element.521.bq_ref, f32[1,1024]{1,0:T(1,128)} %get-tuple-element.520.bv_ref, ...), custom_call_target="tpu_custom_call" | custom-call | flops 1000 | bytes 1000 | tf_op jit(solution)/shard_map/pallas_call | solution.py:149
  103.0 22.2 %shard_map.255 = (bf16[512,1024]{1,0:T(8,128)(2,1)}, f32[512,1024]{1,0:T(8,128)}, bf16[8,2,1024,512]{3,2,1,0:T(8,128)(2,1)}) custom-call(s32[4]{0:T(128)} %pad_add_fusion.pos_ref, bf16[8,512,128]{2,1,0:T(8,128)(2,1)} %get-tuple-element.280.q_ref, bf16[8,1024,128]{2,1,0:T(8,128)(2,1)} %get-tuple-element.281.k_ref, ...), custom_call_target="tpu_custom_call" | custom-call | flops 1000 | bytes 1000 | tf_op jit(solution)/shard_map/pallas_call | solution.py:149
  125.2 4.1 %collective-permute-done.13 = bf16[256,512]{1,0:T(8,128)(2,1)S(1)} collective-permute-done((bf16[256,512]{1,0:T(8,128)(2,1)S(1)}, bf16[256,512]{1,0:T(8,128)(2,1)S(1)}, u32[]{:S(2)}, u32[]{:S(2)}) %collective-permute-start.13) | collective-permute-done | bytes 262176 | tf_op jit(solution)/shard_map/ppermute | solution.py:52
  136.9 6.9 %shard_map.256 = (f32[512,1024]{1,0:T(8,128)}, bf16[512,1024]{1,0:T(8,128)(2,1)}) custom-call(s32[4]{0:T(128)} %pad_add_fusion.pos_ref, bf16[512,1024]{1,0:T(8,128)(2,1)} %get-tuple-element.292.mixed_ref.refs_3_, bf16[512,1024]{1,0:T(8,128)(2,1)} %tok_ref.3, f32[1,1024]{1,0:T(1,128)} %bitcast.100, f32[1,1024]{1,0:T(1,128)} %bitcast.98, f32[1,1024]{1,0:T(1,128)} %bitcast.101, ...), custom_call_target="tpu_custom_call" | custom-call | flops 1000 | bytes 1000 | tf_op jit(solution)/shard_map/pallas_call | solution.py:149
  152.9 13.5 %shard_map.257 = (bf16[512,4096]{1,0:T(8,128)(2,1)}, bf16[512,4096]{1,0:T(8,128)(2,1)}) custom-call(s32[4]{0:T(128)} %pad_add_fusion.pos_ref, bf16[512,1024]{1,0:T(8,128)(2,1)} %get-tuple-element.296.second_ref.refs_0_, f32[1,4096]{1,0:T(1,128)} %bitcast.96, bf16[32,256,640]{2,1,0:T(8,128)(2,1)} %bitcast.66), custom_call_target="tpu_custom_call" | custom-call | flops 1000 | bytes 1000 | tf_op jit(solution)/shard_map/pallas_call | solution.py:149
  166.4 7.3 %shard_map.258 = bf16[4,2,2,256,512]{4,3,2,1,0:T(8,128)(2,1)} custom-call(s32[4]{0:T(128)} %pad_add_fusion.pos_ref, bf16[512,1024]{1,0:T(8,128)(2,1)} %grad_ref.3, bf16[512,4096]{1,0:T(8,128)(2,1)} %get-tuple-element.486.refs_1_.gelu_ref), custom_call_target="tpu_custom_call" | custom-call | flops 1000 | bytes 1000 | tf_op jit(solution)/shard_map/pallas_call | solution.py:149
  183.2 11.0 %shard_map.259 = (bf16[512,4096]{1,0:T(8,128)(2,1)}, f32[1,4096]{1,0:T(1,128)}) custom-call(s32[4]{0:T(128)} %pad_add_fusion.pos_ref, bf16[512,4096]{1,0:T(8,128)(2,1)} %get-tuple-element.312.slope_ref, bf16[512,1024]{1,0:T(8,128)(2,1)} %grad_ref.3, bf16[2,2,256,512]{3,2,1,0:T(8,128)(2,1)} %copy-done.4, ...), custom_call_target="tpu_custom_call" | custom-call | flops 1000 | bytes 1000 | tf_op jit(solution)/shard_map/pallas_call | solution.py:149
  194.2 8.3 %shard_map.260 = (bf16[2,2,256,512]{3,2,1,0:T(8,128)(2,1)}, bf16[2,2,256,512]{3,2,1,0:T(8,128)(2,1)}, bf16[2,2,256,512]{3,2,1,0:T(8,128)(2,1)}, bf16[2,2,256,512]{3,2,1,0:T(8,128)(2,1)}) custom-call(s32[4]{0:T(128)} %pad_add_fusion.pos_ref, bf16[512,1024]{1,0:T(8,128)(2,1)} %grad_ref.3, bf16[512,4096]{1,0:T(8,128)(2,1)} %get-tuple-element.486.refs_1_.gelu_ref, ...), custom_call_target="tpu_custom_call" | custom-call | flops 1000 | bytes 1000 | tf_op jit(solution)/shard_map/pallas_call | solution.py:149
  203.6 13.3 %shard_map.261 = (f32[512,1024]{1,0:T(8,128)}, bf16[512,1024]{1,0:T(8,128)(2,1)}, f32[4,1024]{1,0:T(4,128)}) custom-call(s32[4]{0:T(128)} %pad_add_fusion.pos_ref, bf16[512,4096]{1,0:T(8,128)(2,1)} %get-tuple-element.332.pre_ref.refs_1_, bf16[512,1024]{1,0:T(8,128)(2,1)} %grad_ref.3, f32[512,1024]{1,0:T(8,128)} %get-tuple-element.333.middle_ref, ...), custom_call_target="tpu_custom_call" | custom-call | flops 1000 | bytes 1000 | tf_op jit(solution)/shard_map/pallas_call | solution.py:149
  216.9 5.8 %shard_map.263.grad_ref = bf16[512,1024]{1,0:T(8,128)(2,1)} custom-call(s32[4]{0:T(128)} %pad_add_fusion.pos_ref, bf16[512,1024]{1,0:T(8,128)(2,1)} %get-tuple-element.334.refs_2_.low_ref, bf16[32,256,640]{2,1,0:T(8,128)(2,1)} %bitcast.68), custom_call_target="tpu_custom_call" | custom-call | flops 1000 | bytes 1000 | tf_op jit(solution)/shard_map/pallas_call | solution.py:149
  222.7 8.5 %shard_map.262 = bf16[4,2,2,256,640]{4,3,2,1,0:T(8,128)(2,1)} custom-call(s32[4]{0:T(128)} %pad_add_fusion.pos_ref, bf16[512,1024]{1,0:T(8,128)(2,1)} %get-tuple-element.296.second_ref.refs_0_, bf16[512,4096]{1,0:T(8,128)(2,1)} %get-tuple-element.332.pre_ref.refs_1_, bf16[512,1024]{1,0:T(8,128)(2,1)} %get-tuple-element.334.refs_2_.low_ref, ...), custom_call_target="tpu_custom_call" | custom-call | flops 1000 | bytes 1000 | tf_op jit(solution)/shard_map/pallas_call | solution.py:149
  231.2 4.0 shard_map.264
  238.2 11.5 %shard_map.265 = (bf16[8,512,128]{2,1,0:T(8,128)(2,1)}, bf16[8,1024,128]{2,1,0:T(8,128)(2,1)}, bf16[8,1024,128]{2,1,0:T(8,128)(2,1)}, f32[2,1024]{1,0:T(2,128)}) custom-call(s32[4]{0:T(128)} %pad_add_fusion.pos_ref, bf16[8,512,128]{2,1,0:T(8,128)(2,1)} %get-tuple-element.280.q_ref, bf16[8,1024,128]{2,1,0:T(8,128)(2,1)} %get-tuple-element.281.k_ref, ...), custom_call_target="tpu_custom_call" | custom-call | flops 1000 | bytes 1000 | tf_op jit(solution)/shard_map/pallas_call | solution.py:149
  251.0 10.2 %shard_map.266 = (bf16[2,2,256,640]{3,2,1,0:T(8,128)(2,1)}, bf16[2,2,256,640]{3,2,1,0:T(8,128)(2,1)}, bf16[2,2,256,640]{3,2,1,0:T(8,128)(2,1)}, bf16[2,2,256,640]{3,2,1,0:T(8,128)(2,1)}) custom-call(s32[4]{0:T(128)} %pad_add_fusion.pos_ref, bf16[512,1024]{1,0:T(8,128)(2,1)} %get-tuple-element.296.second_ref.refs_0_, ...), custom_call_target="tpu_custom_call" | custom-call | flops 1000 | bytes 1000 | tf_op jit(solution)/shard_map/pallas_call | solution.py:149
  270.8 11.5 %shard_map.268 = (bf16[8,512,128]{2,1,0:T(8,128)(2,1)}, bf16[8,1024,128]{2,1,0:T(8,128)(2,1)}, bf16[8,1024,128]{2,1,0:T(8,128)(2,1)}, f32[2,1024]{1,0:T(2,128)}) custom-call(s32[4]{0:T(128)} %pad_add_fusion.pos_ref, bf16[8,512,128]{2,1,0:T(8,128)(2,1)} %get-tuple-element.280.q_ref, ...), custom_call_target="tpu_custom_call", output_to_operand_aliasing={{0}: (7, {}), {1}: (8, {}), {2}: (9, {}), {3}: (10, {})} | custom-call | flops 1000 | bytes 1000 | tf_op jit(solution)/shard_map/pallas_call | solution.py:149
  282.3 8.3 %shard_map.269 = bf16[4,2,2,256,384]{4,3,2,1,0:T(8,128)(2,1)} custom-call(s32[4]{0:T(128)} %pad_add_fusion.pos_ref, bf16[1024,1024]{1,0:T(8,128)(2,1)} %fusion.5.first_ref.refs_0_, bf16[8,512,128]{2,1,0:T(8,128)(2,1)} %get-tuple-element.438.refs_1_.dq_ref, bf16[8,1024,128]{2,1,0:T(8,128)(2,1)} %get-tuple-element.458.refs_2_.dk_ref, ...), custom_call_target="tpu_custom_call" | custom-call | flops 1000 | bytes 1000 | tf_op jit(solution)/shard_map/pallas_call | solution.py:149
  290.7 4.1 collective-permute-done.29.refs_1_
  296.0 4.5 %shard_map.270 = (bf16[2,256,640]{2,1,0:T(8,128)(2,1)}, bf16[2,256,640]{2,1,0:T(8,128)(2,1)}, bf16[2,256,640]{2,1,0:T(8,128)(2,1)}, bf16[2,256,640]{2,1,0:T(8,128)(2,1)}) custom-call(s32[4]{0:T(128)} %pad_add_fusion.pos_ref, bf16[2,2,256,640]{3,2,1,0:T(8,128)(2,1)} %get-tuple-element.388.refs_0_, bf16[2,2,256,640]{3,2,1,0:T(8,128)(2,1)} %collective-permute-done.29.refs_1_, ...), custom_call_target="tpu_custom_call" | custom-call | flops 1000 | bytes 1000 | tf_op jit(solution)/shard_map/pallas_call | solution.py:149
  306.4 9.1 %shard_map.272 = (bf16[2,2,256,384]{3,2,1,0:T(8,128)(2,1)}, bf16[2,2,256,384]{3,2,1,0:T(8,128)(2,1)}, bf16[2,2,256,384]{3,2,1,0:T(8,128)(2,1)}, bf16[2,2,256,384]{3,2,1,0:T(8,128)(2,1)}) custom-call(s32[4]{0:T(128)} %pad_add_fusion.pos_ref, bf16[1024,1024]{1,0:T(8,128)(2,1)} %fusion.5.first_ref.refs_0_, ...), custom_call_target="tpu_custom_call" | custom-call | flops 1000 | bytes 1000 | tf_op jit(solution)/shard_map/pallas_call | solution.py:149
  320.2 3.5 shard_map.273
  325.7 12.4 %shard_map.274 = (f32[512,1024]{1,0:T(8,128)}, f32[2,1024]{1,0:T(2,128)}) custom-call(s32[4]{0:T(128)} %pad_add_fusion.pos_ref, bf16[8,512,128]{2,1,0:T(8,128)(2,1)} %get-tuple-element.438.refs_1_.dq_ref, bf16[8,1024,128]{2,1,0:T(8,128)(2,1)} %get-tuple-element.458.refs_2_.dk_ref, bf16[8,1024,128]{2,1,0:T(8,128)(2,1)} %get-tuple-element.459.refs_3_.dv_ref, ...), custom_call_target="tpu_custom_call" | custom-call | flops 1000 | bytes 1000 | tf_op jit(solution)/shard_map/pallas_call | solution.py:149
  349.1 9.6 %shard_map.276 = (bf16[512,1024]{1,0:T(8,128)(2,1)}, f32[2,1024]{1,0:T(2,128)}) custom-call(s32[4]{0:T(128)} %pad_add_fusion.pos_ref, bf16[8,1024,128]{2,1,0:T(8,128)(2,1)} %get-tuple-element.458.refs_2_.dk_ref, bf16[8,1024,128]{2,1,0:T(8,128)(2,1)} %get-tuple-element.459.refs_3_.dv_ref, bf16[512,1024]{1,0:T(8,128)(2,1)} %copy-done.1, f32[1,1024]{1,0:T(1,128)} %bitcast.94, ...), custom_call_target="tpu_custom_call" | custom-call | flops 1000 | bytes 1000 | tf_op jit(solution)/shard_map/pallas_call | solution.py:149
  369.0 10.7 %shard_map.278 = bf16[512,1024]{1,0:T(8,128)(2,1)} custom-call(s32[4]{0:T(128)} %pad_add_fusion.pos_ref, bf16[512,4096]{1,0:T(8,128)(2,1)} %get-tuple-element.486.refs_1_.gelu_ref, f32[512,1024]{1,0:T(8,128)} %get-tuple-element.333.middle_ref, f32[1,1024]{1,0:T(1,128)} %bitcast.102, bf16[2,2,256,512]{3,2,1,0:T(8,128)(2,1)} %copy-done.4, ...), custom_call_target="tpu_custom_call" | custom-call | flops 1000 | bytes 1000 | tf_op jit(solution)/shard_map/pallas_call | solution.py:149
  382.7 7.7 %collective-permute-done.49 = bf16[512,1024]{1,0:T(8,128)(2,1)} collective-permute-done((bf16[512,1024]{1,0:T(8,128)(2,1)}, bf16[512,1024]{1,0:T(8,128)(2,1)}, u32[]{:S(2)}, u32[]{:S(2)}) %collective-permute-start.49) | collective-permute-done | bytes 1048608 | tf_op jit(solution)/shard_map/ppermute | solution.py:1025
  (204 shorter events, 109.7 us)
Async XLA Ops:
  7.2 125.6 %all-gather.3.cloned.1.call-start = ((), (), s32[]{:S(2)}) async-start(), calls=%async_computation | async-start | bytes 10813440 | tf_op jit(solution)/shard_map/all_gather | solution.py:881
  9.1 33.2 %collective-permute-start.3 = (bf16[512,1024]{1,0:T(8,128)(2,1)}, bf16[512,1024]{1,0:T(8,128)(2,1)S(1)}, u32[]{:S(2)}, u32[]{:S(2)}) collective-permute-start(bf16[512,1024]{1,0:T(8,128)(2,1)} %tok_ref.3), channel_id=1, source_target_pairs={{0,1},{2,3},{4,5},{6,7},{8,9},{10,11},{12,13},{14,15},{16,17},{18,... | collective-permute-start | bytes 3145736 | tf_op jit(solution)/shard_map/ppermute | solution.py:885
  18.9 23.4 %collective-permute-start.1 = (bf16[256,384]{1,0:T(8,128)(2,1)S(1)}, bf16[256,384]{1,0:T(8,128)(2,1)S(1)}, u32[]{:S(2)}, u32[]{:S(2)}) collective-permute-start(bf16[256,384]{1,0:T(8,128)(2,1)S(1)} %copy.35), channel_id=1, source_target_pairs={{0,4},{2,6},{4,0},{6,2},{1,5},{3,7},{5,1},{7,3},{8,12},{10,14},{12... | collective-permute-start | bytes 589832 | tf_op jit(solution)/shard_map/ppermute | solution.py:52
  18.9 23.4 %collective-permute-start = (bf16[256,384]{1,0:T(8,128)(2,1)S(1)}, bf16[256,384]{1,0:T(8,128)(2,1)S(1)}, u32[]{:S(2)}, u32[]{:S(2)}) collective-permute-start(bf16[256,384]{1,0:T(8,128)(2,1)S(1)} %copy.35), channel_id=1, source_target_pairs={{0,2},{2,0},{4,6},{6,4},{1,3},{3,1},{5,7},{7,5},{8,10},{10,8},{12,... | collective-permute-start | bytes 589832 | tf_op jit(solution)/shard_map/ppermute | solution.py:52
  44.2 20.1 %collective-permute-start.4 = (bf16[2,256,384]{2,1,0:T(8,128)(2,1)S(1)}, bf16[2,256,384]{2,1,0:T(8,128)(2,1)S(1)}, u32[]{:S(2)}, u32[]{:S(2)}) collective-permute-start(bf16[2,256,384]{2,1,0:T(8,128)(2,1)S(1)} %get-tuple-element.511), channel_id=1, source_target_pairs={{0,1},{1,0},{2,3},{3,2},{4,5},{5,4},{6,7},{7,6},{8,9},{9,8},{10,11... | collective-permute-start | bytes 1179656 | tf_op jit(solution)/shard_map/ppermute | solution.py:52
  57.6 25.1 %collective-permute-start.7 = (bf16[2,2,256,384]{3,2,1,0:T(8,128)(2,1)S(1)}, bf16[2,2,256,384]{3,2,1,0:T(8,128)(2,1)}, u32[]{:S(2)}, u32[]{:S(2)}) collective-permute-start(bf16[2,2,256,384]{3,2,1,0:T(8,128)(2,1)S(1)} %pad_maximum_fusion.4.rest_2_), channel_id=1, source_target_pairs={{0,1},{1,0},{2,3},{3,2},{4,5},{5,4},{6,7},{7,6},{8,9},{9,8},{10,11... | collective-permute-start | bytes 2359304 | tf_op jit(solution)/shard_map/ppermute | solution.py:52
  65.3 18.1 %collective-permute-start.5 = (bf16[2,2,256,384]{3,2,1,0:T(8,128)(2,1)}, bf16[2,2,256,384]{3,2,1,0:T(8,128)(2,1)}, u32[]{:S(2)}, u32[]{:S(2)}) collective-permute-start(bf16[2,2,256,384]{3,2,1,0:T(8,128)(2,1)} %pad_maximum_fusion.3.rest_0_), channel_id=1, source_target_pairs={{0,16},{16,0},{1,17},{17,1},{2,18},{18,2},{3,19},{19,3},{4,20},{20... | collective-permute-start | bytes 2359304 | tf_op jit(solution)/shard_map/ppermute | solution.py:52
  66.0 17.9 %collective-permute-start.10 = (bf16[2,2,256,384]{3,2,1,0:T(8,128)(2,1)S(1)}, bf16[2,2,256,384]{3,2,1,0:T(8,128)(2,1)}, u32[]{:S(2)}, u32[]{:S(2)}) collective-permute-start(bf16[2,2,256,384]{3,2,1,0:T(8,128)(2,1)S(1)} %pad_maximum_fusion.4.rest_2_), channel_id=1, source_target_pairs={{0,8},{8,0},{1,9},{9,1},{2,10},{10,2},{3,11},{11,3},{4,12},{12,4},... | collective-permute-start | bytes 2359304 | tf_op jit(solution)/shard_map/ppermute | solution.py:52
  66.1 17.9 %collective-permute-start.8 = (bf16[2,2,256,384]{3,2,1,0:T(8,128)(2,1)}, bf16[2,2,256,384]{3,2,1,0:T(8,128)(2,1)}, u32[]{:S(2)}, u32[]{:S(2)}) collective-permute-start(bf16[2,2,256,384]{3,2,1,0:T(8,128)(2,1)} %pad_maximum_fusion.3.rest_0_), channel_id=1, source_target_pairs={{0,8},{8,0},{1,9},{9,1},{2,10},{10,2},{3,11},{11,3},{4,12},{12,4},... | collective-permute-start | bytes 2359304 | tf_op jit(solution)/shard_map/ppermute | solution.py:52
  83.9 41.3 %collective-permute-start.14 = (bf16[256,512]{1,0:T(8,128)(2,1)S(1)}, bf16[256,512]{1,0:T(8,128)(2,1)S(1)}, u32[]{:S(2)}, u32[]{:S(2)}) collective-permute-start(bf16[256,512]{1,0:T(8,128)(2,1)S(1)} %copy-done.18), channel_id=1, source_target_pairs={{0,6},{2,4},{4,2},{6,0},{1,7},{3,5},{5,3},{7,1},{8,14},{10,12},{12... | collective-permute-start | bytes 786440 | tf_op jit(solution)/shard_map/ppermute | solution.py:52
  83.9 45.4 %collective-permute-start.13 = (bf16[256,512]{1,0:T(8,128)(2,1)S(1)}, bf16[256,512]{1,0:T(8,128)(2,1)S(1)}, u32[]{:S(2)}, u32[]{:S(2)}) collective-permute-start(bf16[256,512]{1,0:T(8,128)(2,1)S(1)} %copy-done.18), channel_id=1, source_target_pairs={{0,4},{2,6},{4,0},{6,2},{1,5},{3,7},{5,1},{7,3},{8,12},{10,14},{12... | collective-permute-start | bytes 786440 | tf_op jit(solution)/shard_map/ppermute | solution.py:52
  84.0 45.3 %collective-permute-start.12 = (bf16[256,512]{1,0:T(8,128)(2,1)S(1)}, bf16[256,512]{1,0:T(8,128)(2,1)}, u32[]{:S(2)}, u32[]{:S(2)}) collective-permute-start(bf16[256,512]{1,0:T(8,128)(2,1)S(1)} %copy-done.18), channel_id=1, source_target_pairs={{0,2},{2,0},{4,6},{6,4},{1,3},{3,1},{5,7},{7,5},{8,10},{10,8},{12,... | collective-permute-start | bytes 786440 | tf_op jit(solution)/shard_map/ppermute | solution.py:52
  149.3 24.4 %collective-permute-start.20 = (bf16[2,2,256,512]{3,2,1,0:T(8,128)(2,1)S(1)}, bf16[2,2,256,512]{3,2,1,0:T(8,128)(2,1)S(1)}, u32[]{:S(2)}, u32[]{:S(2)}) collective-permute-start(bf16[2,2,256,512]{3,2,1,0:T(8,128)(2,1)S(1)} %pad_maximum_fusion.2.rest_2_), channel_id=1, source_target_pairs={{0,8},{8,0},{1,9},{9,1},{2,10},{10,2},{3,11},{11,3},{4,12},{12,4},... | collective-permute-start | bytes 3145736 | tf_op jit(solution)/shard_map/ppermute | solution.py:52
  149.4 25.7 %collective-permute-start.18 = (bf16[2,2,256,512]{3,2,1,0:T(8,128)(2,1)S(1)}, bf16[2,2,256,512]{3,2,1,0:T(8,128)(2,1)}, u32[]{:S(2)}, u32[]{:S(2)}) collective-permute-start(bf16[2,2,256,512]{3,2,1,0:T(8,128)(2,1)S(1)} %pad_maximum_fusion.2.rest_2_), channel_id=1, source_target_pairs={{0,1},{1,0},{2,3},{3,2},{4,5},{5,4},{6,7},{7,6},{8,9},{9,8},{10,11... | collective-permute-start | bytes 3145736 | tf_op jit(solution)/shard_map/ppermute | solution.py:52
  152.1 23.0 %collective-permute-start.19 = (bf16[2,2,256,512]{3,2,1,0:T(8,128)(2,1)S(1)}, bf16[2,2,256,512]{3,2,1,0:T(8,128)(2,1)}, u32[]{:S(2)}, u32[]{:S(2)}) collective-permute-start(bf16[2,2,256,512]{3,2,1,0:T(8,128)(2,1)S(1)} %pad_maximum_fusion.1.rest_0_), channel_id=1, source_target_pairs={{0,8},{8,0},{1,9},{9,1},{2,10},{10,2},{3,11},{11,3},{4,12},{12,4},... | collective-permute-start | bytes 3145736 | tf_op jit(solution)/shard_map/ppermute | solution.py:52
  152.3 25.5 %collective-permute-start.17 = (bf16[2,2,256,512]{3,2,1,0:T(8,128)(2,1)S(1)}, bf16[2,2,256,512]{3,2,1,0:T(8,128)(2,1)}, u32[]{:S(2)}, u32[]{:S(2)}) collective-permute-start(bf16[2,2,256,512]{3,2,1,0:T(8,128)(2,1)S(1)} %pad_maximum_fusion.1.rest_0_), channel_id=1, source_target_pairs={{0,16},{16,0},{1,17},{17,1},{2,18},{18,2},{3,19},{19,3},{4,20},{20... | collective-permute-start | bytes 3145736 | tf_op jit(solution)/shard_map/ppermute | solution.py:52
  202.5 28.7 %collective-permute-start.24 = (bf16[2,2,256,512]{3,2,1,0:T(8,128)(2,1)}, bf16[2,2,256,512]{3,2,1,0:T(8,128)(2,1)}, u32[]{:S(2)}, u32[]{:S(2)}) collective-permute-start(bf16[2,2,256,512]{3,2,1,0:T(8,128)(2,1)} %get-tuple-element.329), channel_id=1, source_target_pairs={{0,16},{16,0},{1,17},{17,1},{2,18},{18,2},{3,19},{19,3},{4,20},{20... | collective-permute-start | bytes 3145736 | tf_op jit(solution)/shard_map/ppermute | solution.py:52
  203.0 28.2 %collective-permute-start.25 = (bf16[2,2,256,512]{3,2,1,0:T(8,128)(2,1)}, bf16[2,2,256,512]{3,2,1,0:T(8,128)(2,1)}, u32[]{:S(2)}, u32[]{:S(2)}) collective-permute-start(bf16[2,2,256,512]{3,2,1,0:T(8,128)(2,1)} %get-tuple-element.331), channel_id=1, source_target_pairs={{0,1},{1,0},{2,3},{3,2},{4,5},{5,4},{6,7},{7,6},{8,9},{9,8},{10,11... | collective-permute-start | bytes 3145736 | tf_op jit(solution)/shard_map/ppermute | solution.py:52
  235.1 15.9 %collective-permute-start.28 = (bf16[4,2,2,256,640]{4,3,2,1,0:T(8,128)(2,1)}, bf16[4,2,2,256,640]{4,3,2,1,0:T(8,128)(2,1)}, u32[]{:S(2)}, u32[]{:S(2)}) collective-permute-start(bf16[4,2,2,256,640]{4,3,2,1,0:T(8,128)(2,1)} %shard_map.262), channel_id=1, source_target_pairs={{0,8},{8,0},{1,9},{9,1},{2,10},{10,2},{3,11},{11,3},{4,12},{12,4},... | collective-permute-start | bytes 15728648 | tf_op jit(solution)/shard_map/ppermute | solution.py:52
  264.4 30.3 %collective-permute-start.29 = (bf16[2,2,256,640]{3,2,1,0:T(8,128)(2,1)}, bf16[2,2,256,640]{3,2,1,0:T(8,128)(2,1)}, u32[]{:S(2)}, u32[]{:S(2)}) collective-permute-start(bf16[2,2,256,640]{3,2,1,0:T(8,128)(2,1)} %get-tuple-element.381), channel_id=1, source_target_pairs={{0,16},{16,0},{1,17},{17,1},{2,18},{18,2},{3,19},{19,3},{4,20},{20... | collective-permute-start | bytes 3932168 | tf_op jit(solution)/shard_map/ppermute | solution.py:52
  265.9 30.0 %collective-permute-start.30 = (bf16[2,2,256,640]{3,2,1,0:T(8,128)(2,1)}, bf16[2,2,256,640]{3,2,1,0:T(8,128)(2,1)}, u32[]{:S(2)}, u32[]{:S(2)}) collective-permute-start(bf16[2,2,256,640]{3,2,1,0:T(8,128)(2,1)} %get-tuple-element.383), channel_id=1, source_target_pairs={{0,1},{1,0},{2,3},{3,2},{4,5},{5,4},{6,7},{7,6},{8,9},{9,8},{10,11... | collective-permute-start | bytes 3932168 | tf_op jit(solution)/shard_map/ppermute | solution.py:52
  266.5 24.2 %collective-permute-start.31 = (bf16[256,512]{1,0:T(8,128)(2,1)}, bf16[256,512]{1,0:T(8,128)(2,1)S(1)}, u32[]{:S(2)}, u32[]{:S(2)}) collective-permute-start(bf16[256,512]{1,0:T(8,128)(2,1)} %get-tuple-element.385), channel_id=1, source_target_pairs={{0,2},{2,0},{4,6},{6,4},{1,3},{3,1},{5,7},{7,5},{8,10},{10,8},{12,... | collective-permute-start | bytes 786440 | tf_op jit(solution)/shard_map/ppermute | solution.py:52
  266.5 24.2 %collective-permute-start.32 = (bf16[256,512]{1,0:T(8,128)(2,1)}, bf16[256,512]{1,0:T(8,128)(2,1)}, u32[]{:S(2)}, u32[]{:S(2)}) collective-permute-start(bf16[256,512]{1,0:T(8,128)(2,1)} %get-tuple-element.386), channel_id=1, source_target_pairs={{0,4},{2,6},{4,0},{6,2},{1,5},{3,7},{5,1},{7,3},{8,12},{10,14},{12... | collective-permute-start | bytes 786440 | tf_op jit(solution)/shard_map/ppermute | solution.py:52
  268.5 22.2 %collective-permute-start.33 = (bf16[256,512]{1,0:T(8,128)(2,1)}, bf16[256,512]{1,0:T(8,128)(2,1)}, u32[]{:S(2)}, u32[]{:S(2)}) collective-permute-start(bf16[256,512]{1,0:T(8,128)(2,1)} %get-tuple-element.387), channel_id=1, source_target_pairs={{0,6},{2,4},{4,2},{6,0},{1,7},{3,5},{5,3},{7,1},{8,14},{10,12},{12... | collective-permute-start | bytes 786440 | tf_op jit(solution)/shard_map/ppermute | solution.py:52
  300.4 17.4 %collective-permute-start.35 = (bf16[2,256,640]{2,1,0:T(8,128)(2,1)}, bf16[2,256,640]{2,1,0:T(8,128)(2,1)S(1)}, u32[]{:S(2)}, u32[]{:S(2)}) collective-permute-start(bf16[2,256,640]{2,1,0:T(8,128)(2,1)} %get-tuple-element.414), channel_id=1, source_target_pairs={{0,1},{1,0},{2,3},{3,2},{4,5},{5,4},{6,7},{7,6},{8,9},{9,8},{10,11... | collective-permute-start | bytes 1966088 | tf_op jit(solution)/shard_map/ppermute | solution.py:52
  301.1 17.1 %collective-permute-start.36 = (bf16[2,256,640]{2,1,0:T(8,128)(2,1)}, bf16[2,256,640]{2,1,0:T(8,128)(2,1)}, u32[]{:S(2)}, u32[]{:S(2)}) collective-permute-start(bf16[2,256,640]{2,1,0:T(8,128)(2,1)} %get-tuple-element.416), channel_id=1, source_target_pairs={{0,16},{16,0},{1,17},{17,1},{2,18},{18,2},{3,19},{19,3},{4,20},{20... | collective-permute-start | bytes 1966088 | tf_op jit(solution)/shard_map/ppermute | solution.py:52
  318.6 21.6 %collective-permute-start.37 = (bf16[2,2,256,384]{3,2,1,0:T(8,128)(2,1)}, bf16[2,2,256,384]{3,2,1,0:T(8,128)(2,1)S(1)}, u32[]{:S(2)}, u32[]{:S(2)}) collective-permute-start(bf16[2,2,256,384]{3,2,1,0:T(8,128)(2,1)} %get-tuple-element.421), channel_id=1, source_target_pairs={{0,16},{16,0},{1,17},{17,1},{2,18},{18,2},{3,19},{19,3},{4,20},{20... | collective-permute-start | bytes 2359304 | tf_op jit(solution)/shard_map/ppermute | solution.py:52
  319.2 21.1 %collective-permute-start.38 = (bf16[2,2,256,384]{3,2,1,0:T(8,128)(2,1)}, bf16[2,2,256,384]{3,2,1,0:T(8,128)(2,1)}, u32[]{:S(2)}, u32[]{:S(2)}) collective-permute-start(bf16[2,2,256,384]{3,2,1,0:T(8,128)(2,1)} %get-tuple-element.423), channel_id=1, source_target_pairs={{0,1},{1,0},{2,3},{3,2},{4,5},{5,4},{6,7},{7,6},{8,9},{9,8},{10,11... | collective-permute-start | bytes 2359304 | tf_op jit(solution)/shard_map/ppermute | solution.py:52
  323.7 16.6 %collective-permute-start.40 = (bf16[256,640]{1,0:T(8,128)(2,1)}, bf16[256,640]{1,0:T(8,128)(2,1)S(1)}, u32[]{:S(2)}, u32[]{:S(2)}) collective-permute-start(bf16[256,640]{1,0:T(8,128)(2,1)} %get-tuple-element.437), channel_id=1, source_target_pairs={{0,4},{2,6},{4,0},{6,2},{1,5},{3,7},{5,1},{7,3},{8,12},{10,14},{12... | collective-permute-start | bytes 983048 | tf_op jit(solution)/shard_map/ppermute | solution.py:52
  362.7 27.8 %collective-permute-start.49 = (bf16[512,1024]{1,0:T(8,128)(2,1)}, bf16[512,1024]{1,0:T(8,128)(2,1)}, u32[]{:S(2)}, u32[]{:S(2)}) collective-permute-start(bf16[512,1024]{1,0:T(8,128)(2,1)} %get-tuple-element.487), channel_id=1, source_target_pairs={{1,0},{3,2},{5,4},{7,6},{9,8},{11,10},{13,12},{15,14},{17,16},{19,... | collective-permute-start | bytes 3145736 | tf_op jit(solution)/shard_map/ppermute | solution.py:1025
  364.0 18.7 %collective-permute-start.45 = (bf16[256,384]{1,0:T(8,128)(2,1)}, bf16[256,384]{1,0:T(8,128)(2,1)S(1)}, u32[]{:S(2)}, u32[]{:S(2)}) collective-permute-start(bf16[256,384]{1,0:T(8,128)(2,1)} %get-tuple-element.482), channel_id=1, source_target_pairs={{0,2},{2,0},{4,6},{6,4},{1,3},{3,1},{5,7},{7,5},{8,10},{10,8},{12,... | collective-permute-start | bytes 589832 | tf_op jit(solution)/shard_map/ppermute | solution.py:52
  364.0 18.6 %collective-permute-start.46 = (bf16[256,384]{1,0:T(8,128)(2,1)}, bf16[256,384]{1,0:T(8,128)(2,1)S(1)}, u32[]{:S(2)}, u32[]{:S(2)}) collective-permute-start(bf16[256,384]{1,0:T(8,128)(2,1)} %get-tuple-element.483), channel_id=1, source_target_pairs={{0,4},{2,6},{4,0},{6,2},{1,5},{3,7},{5,1},{7,3},{8,12},{10,14},{12... | collective-permute-start | bytes 589832 | tf_op jit(solution)/shard_map/ppermute | solution.py:52
  (54 other events, 666.1 us)
Sparse Core Ops, SparseCore 0:
  11.5 121.1 all-gather.2

commit v6 on v4

--- a/solution.py
+++ b/solution.py
@@ -1030,11 +1030,12 @@
     back = lax.ppermute(back, "tx", [(1, 0)])
     grad_up.sum_three((hidden, width))
     result = result_call(lay, pos, gelu, middle, row(b_down), down.parts, hidden)
-    pieces, result, grad_up.out = stage(grad_qkv, pieces, result, grad_up.out)
+    pieces, result, back, grad_up.out = stage(grad_qkv, pieces, result, back, grad_up.out)
     small = sum(pieces)
+    token_grad = (first_grad + back.astype(F32)).astype(BF)
     small = small + trade(small, "tx", 2, 1)
+    small, token_grad = stage(small, token_grad)
     small = sum(around(small, "tz", nz)).reshape(-1)
-    token_grad = (first_grad + back.astype(F32)).astype(BF)
     grad_qkv.sum_three(((3, width),))
     at = 4 * dim
     late = small[at + gelu.shape[1] :]

time: 415 us -> 416 us (level)
    ppermute x1, waiting for transfers between devices: 0.01 us -> 6.84 us  [per_device(): back = lax.ppermute(back, 'tx', [(1, 0)])]
  transfers between devices with their start and end apart: 55 -> 55, of which waited for: 23 -> 24; matrix products, arithmetic and copies ran while one was open for 3% -> 4% of each run, Pallas kernels for 46% -> 46%
where the time goes in v6:
time: 416 us; the launch traced here: 411 us
  Pallas kernels  223 us (54%)
  waiting for transfers between devices  95.3 us (23%)
  starting transfers between devices  54.7 us (13%)
  between operations  14.9 us (4%)
  other arithmetic  14.6 us (4%)
  local copies, waits for them, and re-layouts  8.37 us (2%)
    pallas_call x27, Pallas kernels, kernel_call(): pl.pallas_call(body, out_shape=outs, grid_spec=pltpu.PrefetchScalarGridSp...  223 us
    ppermute x52, waiting for transfers between devices, trade(): return lax.ppermute(value, axis, [(s, s ^ distance) for s in range(size)])  85 us
    ppermute x52, starting transfers between devices, trade(): return lax.ppermute(value, axis, [(s, s ^ distance) for s in range(size)])  48.5 us
  transfers between devices with their start and end apart: 55, of which 24 were waited for; matrix products, arithmetic and copies ran while one was open for 4% of the time, Pallas kernels for 46%

profile of v6, /device:TPU:0, one launch (start us, length us, event | category | flops | bytes accessed | tf_op | source)
XLA Modules:
  0.0 411.2 jit_solution(7276652456980599359)
XLA Ops:
  9.1 4.9 %collective-permute-start.3 = (bf16[512,1024]{1,0:T(8,128)(2,1)}, bf16[512,1024]{1,0:T(8,128)(2,1)S(1)}, u32[]{:S(2)}, u32[]{:S(2)}) collective-permute-start(bf16[512,1024]{1,0:T(8,128)(2,1)} %tok_ref.3), channel_id=1, source_target_pairs={{0,1},{2,3},{4,5},{6,7},{8,9},{10,11},{12,13},{14,15},{16,17},{18,... | collective-permute-start | bytes 3145736 | tf_op jit(solution)/shard_map/ppermute | solution.py:890
  15.2 3.7 collective-permute-start.2
  20.5 4.5 %collective-permute-done.2 = bf16[256,384]{1,0:T(8,128)(2,1)S(1)} collective-permute-done((bf16[256,384]{1,0:T(8,128)(2,1)S(1)}, bf16[256,384]{1,0:T(8,128)(2,1)S(1)}, u32[]{:S(2)}, u32[]{:S(2)}) %collective-permute-start.2) | collective-permute-done | bytes 196640 | tf_op jit(solution)/shard_map/ppermute | solution.py:52
  25.0 17.3 %collective-permute-done.1 = bf16[256,384]{1,0:T(8,128)(2,1)S(1)} collective-permute-done((bf16[256,384]{1,0:T(8,128)(2,1)S(1)}, bf16[256,384]{1,0:T(8,128)(2,1)S(1)}, u32[]{:S(2)}, u32[]{:S(2)}) %collective-permute-start.1) | collective-permute-done | bytes 196640 | tf_op jit(solution)/shard_map/ppermute | solution.py:52
  44.7 12.8 %collective-permute-done.6 = bf16[2,256,384]{2,1,0:T(8,128)(2,1)S(1)} collective-permute-done((bf16[2,256,384]{2,1,0:T(8,128)(2,1)S(1)}, bf16[2,256,384]{2,1,0:T(8,128)(2,1)S(1)}, u32[]{:S(2)}, u32[]{:S(2)}) %collective-permute-start.6) | collective-permute-done | bytes 393248 | tf_op jit(solution)/shard_map/ppermute | solution.py:52
  57.6 6.7 %collective-permute-done.4 = bf16[2,256,384]{2,1,0:T(8,128)(2,1)S(1)} collective-permute-done((bf16[2,256,384]{2,1,0:T(8,128)(2,1)S(1)}, bf16[2,256,384]{2,1,0:T(8,128)(2,1)S(1)}, u32[]{:S(2)}, u32[]{:S(2)}) %collective-permute-start.4) | collective-permute-done | bytes 393248 | tf_op jit(solution)/shard_map/ppermute | solution.py:52
  69.6 13.2 %collective-permute-done.7.rest_3_ = bf16[2,2,256,384]{3,2,1,0:T(8,128)(2,1)} collective-permute-done((bf16[2,2,256,384]{3,2,1,0:T(8,128)(2,1)S(1)}, bf16[2,2,256,384]{3,2,1,0:T(8,128)(2,1)}, u32[]{:S(2)}, u32[]{:S(2)}) %collective-permute-start.7) | collective-permute-done | bytes 786464 | tf_op jit(solution)/shard_map/ppermute | solution.py:52
  83.9 4.3 %collective-permute-start.12 = (bf16[256,512]{1,0:T(8,128)(2,1)S(1)}, bf16[256,512]{1,0:T(8,128)(2,1)}, u32[]{:S(2)}, u32[]{:S(2)}) collective-permute-start(bf16[256,512]{1,0:T(8,128)(2,1)S(1)} %copy-done.18), channel_id=1, source_target_pairs={{0,2},{2,0},{4,6},{6,4},{1,3},{3,1},{5,7},{7,5},{8,10},{10,8},{12,... | collective-permute-start | bytes 786440 | tf_op jit(solution)/shard_map/ppermute | solution.py:52
  91.6 11.4 %shard_map.254 = (bf16[8,512,128]{2,1,0:T(8,128)(2,1)}, bf16[8,1024,128]{2,1,0:T(8,128)(2,1)}, bf16[8,1024,128]{2,1,0:T(8,128)(2,1)}) custom-call(s32[4]{0:T(128)} %pad_add_fusion.pos_ref, bf16[1024,1024]{1,0:T(8,128)(2,1)} %fusion.5.first_ref.refs_0_, f32[1,1024]{1,0:T(1,128)} %get-tuple-element.521.bq_ref, f32[1,1024]{1,0:T(1,128)} %get-tuple-element.520.bv_ref, ...), custom_call_target="tpu_custom_call" | custom-call | flops 1000 | bytes 1000 | tf_op jit(solution)/shard_map/pallas_call | solution.py:149
  102.9 20.6 %shard_map.255 = (bf16[512,1024]{1,0:T(8,128)(2,1)}, f32[512,1024]{1,0:T(8,128)}, f32[8,2,512]{2,1,0:T(2,128)}) custom-call(s32[4]{0:T(128)} %pad_add_fusion.pos_ref, bf16[8,512,128]{2,1,0:T(8,128)(2,1)} %get-tuple-element.280.q_ref, bf16[8,1024,128]{2,1,0:T(8,128)(2,1)} %get-tuple-element.281.k_ref, bf16[8,1024,128]{2,1,0:T(8,128)(2,1)} %get-tuple-element.282.v_ref, ...), custom_call_target="tpu_custom_call" | custom-call | flops 1000 | bytes 1000 | tf_op jit(solution)/shard_map/pallas_call | solution.py:149
  123.5 5.8 %collective-permute-done.13 = bf16[256,512]{1,0:T(8,128)(2,1)S(1)} collective-permute-done((bf16[256,512]{1,0:T(8,128)(2,1)S(1)}, bf16[256,512]{1,0:T(8,128)(2,1)S(1)}, u32[]{:S(2)}, u32[]{:S(2)}) %collective-permute-start.13) | collective-permute-done | bytes 262176 | tf_op jit(solution)/shard_map/ppermute | solution.py:52
  136.9 6.9 %shard_map.256 = (f32[512,1024]{1,0:T(8,128)}, bf16[512,1024]{1,0:T(8,128)(2,1)}) custom-call(s32[4]{0:T(128)} %pad_add_fusion.pos_ref, bf16[512,1024]{1,0:T(8,128)(2,1)} %get-tuple-element.292.mixed_ref.refs_3_, bf16[512,1024]{1,0:T(8,128)(2,1)} %tok_ref.3, f32[1,1024]{1,0:T(1,128)} %bitcast.100, f32[1,1024]{1,0:T(1,128)} %bitcast.98, f32[1,1024]{1,0:T(1,128)} %bitcast.101, ...), custom_call_target="tpu_custom_call" | custom-call | flops 1000 | bytes 1000 | tf_op jit(solution)/shard_map/pallas_call | solution.py:149
  152.9 13.5 %shard_map.257 = (bf16[512,4096]{1,0:T(8,128)(2,1)}, bf16[512,4096]{1,0:T(8,128)(2,1)}) custom-call(s32[4]{0:T(128)} %pad_add_fusion.pos_ref, bf16[512,1024]{1,0:T(8,128)(2,1)} %get-tuple-element.296.second_ref.refs_0_, f32[1,4096]{1,0:T(1,128)} %bitcast.96, bf16[32,256,640]{2,1,0:T(8,128)(2,1)} %bitcast.66), custom_call_target="tpu_custom_call" | custom-call | flops 1000 | bytes 1000 | tf_op jit(solution)/shard_map/pallas_call | solution.py:149
  166.4 7.3 %shard_map.258 = bf16[4,2,2,256,512]{4,3,2,1,0:T(8,128)(2,1)} custom-call(s32[4]{0:T(128)} %pad_add_fusion.pos_ref, bf16[512,1024]{1,0:T(8,128)(2,1)} %grad_ref.3, bf16[512,4096]{1,0:T(8,128)(2,1)} %get-tuple-element.486.refs_1_.gelu_ref), custom_call_target="tpu_custom_call" | custom-call | flops 1000 | bytes 1000 | tf_op jit(solution)/shard_map/pallas_call | solution.py:149
  183.2 10.9 %shard_map.259 = (bf16[512,4096]{1,0:T(8,128)(2,1)}, f32[1,4096]{1,0:T(1,128)}) custom-call(s32[4]{0:T(128)} %pad_add_fusion.pos_ref, bf16[512,4096]{1,0:T(8,128)(2,1)} %get-tuple-element.312.slope_ref, bf16[512,1024]{1,0:T(8,128)(2,1)} %grad_ref.3, bf16[2,2,256,512]{3,2,1,0:T(8,128)(2,1)} %copy-done.4, ...), custom_call_target="tpu_custom_call" | custom-call | flops 1000 | bytes 1000 | tf_op jit(solution)/shard_map/pallas_call | solution.py:149
  194.1 8.3 %shard_map.260 = (bf16[2,2,256,512]{3,2,1,0:T(8,128)(2,1)}, bf16[2,2,256,512]{3,2,1,0:T(8,128)(2,1)}, bf16[2,2,256,512]{3,2,1,0:T(8,128)(2,1)}, bf16[2,2,256,512]{3,2,1,0:T(8,128)(2,1)}) custom-call(s32[4]{0:T(128)} %pad_add_fusion.pos_ref, bf16[512,1024]{1,0:T(8,128)(2,1)} %grad_ref.3, bf16[512,4096]{1,0:T(8,128)(2,1)} %get-tuple-element.486.refs_1_.gelu_ref, ...), custom_call_target="tpu_custom_call" | custom-call | flops 1000 | bytes 1000 | tf_op jit(solution)/shard_map/pallas_call | solution.py:149
  203.5 13.3 %shard_map.261 = (f32[512,1024]{1,0:T(8,128)}, bf16[512,1024]{1,0:T(8,128)(2,1)}, f32[4,1024]{1,0:T(4,128)}) custom-call(s32[4]{0:T(128)} %pad_add_fusion.pos_ref, bf16[512,4096]{1,0:T(8,128)(2,1)} %get-tuple-element.332.pre_ref.refs_1_, bf16[512,1024]{1,0:T(8,128)(2,1)} %grad_ref.3, f32[512,1024]{1,0:T(8,128)} %get-tuple-element.333.middle_ref, ...), custom_call_target="tpu_custom_call" | custom-call | flops 1000 | bytes 1000 | tf_op jit(solution)/shard_map/pallas_call | solution.py:149
  216.9 5.8 %shard_map.263.grad_ref = bf16[512,1024]{1,0:T(8,128)(2,1)} custom-call(s32[4]{0:T(128)} %pad_add_fusion.pos_ref, bf16[512,1024]{1,0:T(8,128)(2,1)} %get-tuple-element.334.refs_2_.low_ref, bf16[32,256,640]{2,1,0:T(8,128)(2,1)} %bitcast.68), custom_call_target="tpu_custom_call" | custom-call | flops 1000 | bytes 1000 | tf_op jit(solution)/shard_map/pallas_call | solution.py:149
  222.7 8.5 %shard_map.262 = bf16[4,2,2,256,640]{4,3,2,1,0:T(8,128)(2,1)} custom-call(s32[4]{0:T(128)} %pad_add_fusion.pos_ref, bf16[512,1024]{1,0:T(8,128)(2,1)} %get-tuple-element.296.second_ref.refs_0_, bf16[512,4096]{1,0:T(8,128)(2,1)} %get-tuple-element.332.pre_ref.refs_1_, bf16[512,1024]{1,0:T(8,128)(2,1)} %get-tuple-element.334.refs_2_.low_ref, ...), custom_call_target="tpu_custom_call" | custom-call | flops 1000 | bytes 1000 | tf_op jit(solution)/shard_map/pallas_call | solution.py:149
  231.2 4.0 shard_map.264
  238.2 13.2 %shard_map.265 = (bf16[8,512,128]{2,1,0:T(8,128)(2,1)}, bf16[8,1024,128]{2,1,0:T(8,128)(2,1)}, bf16[8,1024,128]{2,1,0:T(8,128)(2,1)}, f32[2,1024]{1,0:T(2,128)}) custom-call(s32[4]{0:T(128)} %pad_add_fusion.pos_ref, bf16[8,512,128]{2,1,0:T(8,128)(2,1)} %get-tuple-element.280.q_ref, bf16[8,1024,128]{2,1,0:T(8,128)(2,1)} %get-tuple-element.281.k_ref, ...), custom_call_target="tpu_custom_call" | custom-call | flops 1000 | bytes 1000 | tf_op jit(solution)/shard_map/pallas_call | solution.py:149
  251.4 10.3 %shard_map.266 = (bf16[2,2,256,640]{3,2,1,0:T(8,128)(2,1)}, bf16[2,2,256,640]{3,2,1,0:T(8,128)(2,1)}, bf16[2,2,256,640]{3,2,1,0:T(8,128)(2,1)}, bf16[2,2,256,640]{3,2,1,0:T(8,128)(2,1)}) custom-call(s32[4]{0:T(128)} %pad_add_fusion.pos_ref, bf16[512,1024]{1,0:T(8,128)(2,1)} %get-tuple-element.296.second_ref.refs_0_, ...), custom_call_target="tpu_custom_call" | custom-call | flops 1000 | bytes 1000 | tf_op jit(solution)/shard_map/pallas_call | solution.py:149
  270.9 13.2 %shard_map.268 = (bf16[8,512,128]{2,1,0:T(8,128)(2,1)}, bf16[8,1024,128]{2,1,0:T(8,128)(2,1)}, bf16[8,1024,128]{2,1,0:T(8,128)(2,1)}, f32[2,1024]{1,0:T(2,128)}) custom-call(s32[4]{0:T(128)} %pad_add_fusion.pos_ref, bf16[8,512,128]{2,1,0:T(8,128)(2,1)} %get-tuple-element.280.q_ref, ...), custom_call_target="tpu_custom_call", output_to_operand_aliasing={{0}: (9, {}), {1}: (10, {}), {2}: (11, {}), {3}: (12, {})} | custom-call | flops 1000 | bytes 1000 | tf_op jit(solution)/shard_map/pallas_call | solution.py:149
  284.1 8.4 %shard_map.269 = bf16[4,2,2,256,384]{4,3,2,1,0:T(8,128)(2,1)} custom-call(s32[4]{0:T(128)} %pad_add_fusion.pos_ref, bf16[1024,1024]{1,0:T(8,128)(2,1)} %fusion.5.first_ref.refs_0_, bf16[8,512,128]{2,1,0:T(8,128)(2,1)} %get-tuple-element.438.refs_1_.dq_ref, bf16[8,1024,128]{2,1,0:T(8,128)(2,1)} %get-tuple-element.458.refs_2_.dk_ref, ...), custom_call_target="tpu_custom_call" | custom-call | flops 1000 | bytes 1000 | tf_op jit(solution)/shard_map/pallas_call | solution.py:149
  296.1 4.4 %shard_map.270 = (bf16[2,256,640]{2,1,0:T(8,128)(2,1)}, bf16[2,256,640]{2,1,0:T(8,128)(2,1)}, bf16[2,256,640]{2,1,0:T(8,128)(2,1)}, bf16[2,256,640]{2,1,0:T(8,128)(2,1)}) custom-call(s32[4]{0:T(128)} %pad_add_fusion.pos_ref, bf16[2,2,256,640]{3,2,1,0:T(8,128)(2,1)} %get-tuple-element.388.refs_0_, bf16[2,2,256,640]{3,2,1,0:T(8,128)(2,1)} %collective-permute-done.29.refs_1_, ...), custom_call_target="tpu_custom_call" | custom-call | flops 1000 | bytes 1000 | tf_op jit(solution)/shard_map/pallas_call | solution.py:149
  306.5 9.1 %shard_map.272 = (bf16[2,2,256,384]{3,2,1,0:T(8,128)(2,1)}, bf16[2,2,256,384]{3,2,1,0:T(8,128)(2,1)}, bf16[2,2,256,384]{3,2,1,0:T(8,128)(2,1)}, bf16[2,2,256,384]{3,2,1,0:T(8,128)(2,1)}) custom-call(s32[4]{0:T(128)} %pad_add_fusion.pos_ref, bf16[1024,1024]{1,0:T(8,128)(2,1)} %fusion.5.first_ref.refs_0_, ...), custom_call_target="tpu_custom_call" | custom-call | flops 1000 | bytes 1000 | tf_op jit(solution)/shard_map/pallas_call | solution.py:149
  321.2 3.5 shard_map.273
  326.7 12.4 %shard_map.274 = (f32[512,1024]{1,0:T(8,128)}, f32[2,1024]{1,0:T(2,128)}) custom-call(s32[4]{0:T(128)} %pad_add_fusion.pos_ref, bf16[8,512,128]{2,1,0:T(8,128)(2,1)} %get-tuple-element.438.refs_1_.dq_ref, bf16[8,1024,128]{2,1,0:T(8,128)(2,1)} %get-tuple-element.458.refs_2_.dk_ref, bf16[8,1024,128]{2,1,0:T(8,128)(2,1)} %get-tuple-element.459.refs_3_.dv_ref, ...), custom_call_target="tpu_custom_call" | custom-call | flops 1000 | bytes 1000 | tf_op jit(solution)/shard_map/pallas_call | solution.py:149
  342.2 3.6 shard_map.275
  349.4 9.5 %shard_map.276 = (bf16[512,1024]{1,0:T(8,128)(2,1)}, f32[2,1024]{1,0:T(2,128)}) custom-call(s32[4]{0:T(128)} %pad_add_fusion.pos_ref, bf16[8,1024,128]{2,1,0:T(8,128)(2,1)} %get-tuple-element.458.refs_2_.dk_ref, bf16[8,1024,128]{2,1,0:T(8,128)(2,1)} %get-tuple-element.459.refs_3_.dv_ref, bf16[512,1024]{1,0:T(8,128)(2,1)} %copy-done.1, f32[1,1024]{1,0:T(1,128)} %bitcast.94, ...), custom_call_target="tpu_custom_call" | custom-call | flops 1000 | bytes 1000 | tf_op jit(solution)/shard_map/pallas_call | solution.py:149
  370.0 10.7 %shard_map.278 = bf16[512,1024]{1,0:T(8,128)(2,1)} custom-call(s32[4]{0:T(128)} %pad_add_fusion.pos_ref, bf16[512,4096]{1,0:T(8,128)(2,1)} %get-tuple-element.486.refs_1_.gelu_ref, f32[512,1024]{1,0:T(8,128)} %get-tuple-element.333.middle_ref, f32[1,1024]{1,0:T(1,128)} %bitcast.102, bf16[2,2,256,512]{3,2,1,0:T(8,128)(2,1)} %copy-done.4, ...), custom_call_target="tpu_custom_call" | custom-call | flops 1000 | bytes 1000 | tf_op jit(solution)/shard_map/pallas_call | solution.py:149
  383.7 6.8 %collective-permute-done.49 = bf16[512,1024]{1,0:T(8,128)(2,1)} collective-permute-done((bf16[512,1024]{1,0:T(8,128)(2,1)}, bf16[512,1024]{1,0:T(8,128)(2,1)}, u32[]{:S(2)}, u32[]{:S(2)}) %collective-permute-start.49) | collective-permute-done | bytes 1048608 | tf_op jit(solution)/shard_map/ppermute | solution.py:1030
  (204 shorter events, 107.6 us)
Async XLA Ops:
  7.2 125.6 %all-gather.3.cloned.1.call-start = ((), (), s32[]{:S(2)}) async-start(), calls=%async_computation | async-start | bytes 10813440 | tf_op jit(solution)/shard_map/all_gather | solution.py:886
  9.1 33.2 %collective-permute-start.3 = (bf16[512,1024]{1,0:T(8,128)(2,1)}, bf16[512,1024]{1,0:T(8,128)(2,1)S(1)}, u32[]{:S(2)}, u32[]{:S(2)}) collective-permute-start(bf16[512,1024]{1,0:T(8,128)(2,1)} %tok_ref.3), channel_id=1, source_target_pairs={{0,1},{2,3},{4,5},{6,7},{8,9},{10,11},{12,13},{14,15},{16,17},{18,... | collective-permute-start | bytes 3145736 | tf_op jit(solution)/shard_map/ppermute | solution.py:890
  18.9 23.4 %collective-permute-start.1 = (bf16[256,384]{1,0:T(8,128)(2,1)S(1)}, bf16[256,384]{1,0:T(8,128)(2,1)S(1)}, u32[]{:S(2)}, u32[]{:S(2)}) collective-permute-start(bf16[256,384]{1,0:T(8,128)(2,1)S(1)} %copy.35), channel_id=1, source_target_pairs={{0,4},{2,6},{4,0},{6,2},{1,5},{3,7},{5,1},{7,3},{8,12},{10,14},{12... | collective-permute-start | bytes 589832 | tf_op jit(solution)/shard_map/ppermute | solution.py:52
  18.9 23.4 %collective-permute-start = (bf16[256,384]{1,0:T(8,128)(2,1)S(1)}, bf16[256,384]{1,0:T(8,128)(2,1)S(1)}, u32[]{:S(2)}, u32[]{:S(2)}) collective-permute-start(bf16[256,384]{1,0:T(8,128)(2,1)S(1)} %copy.35), channel_id=1, source_target_pairs={{0,2},{2,0},{4,6},{6,4},{1,3},{3,1},{5,7},{7,5},{8,10},{10,8},{12,... | collective-permute-start | bytes 589832 | tf_op jit(solution)/shard_map/ppermute | solution.py:52
  44.2 20.1 %collective-permute-start.4 = (bf16[2,256,384]{2,1,0:T(8,128)(2,1)S(1)}, bf16[2,256,384]{2,1,0:T(8,128)(2,1)S(1)}, u32[]{:S(2)}, u32[]{:S(2)}) collective-permute-start(bf16[2,256,384]{2,1,0:T(8,128)(2,1)S(1)} %get-tuple-element.511), channel_id=1, source_target_pairs={{0,1},{1,0},{2,3},{3,2},{4,5},{5,4},{6,7},{7,6},{8,9},{9,8},{10,11... | collective-permute-start | bytes 1179656 | tf_op jit(solution)/shard_map/ppermute | solution.py:52
  57.6 25.1 %collective-permute-start.7 = (bf16[2,2,256,384]{3,2,1,0:T(8,128)(2,1)S(1)}, bf16[2,2,256,384]{3,2,1,0:T(8,128)(2,1)}, u32[]{:S(2)}, u32[]{:S(2)}) collective-permute-start(bf16[2,2,256,384]{3,2,1,0:T(8,128)(2,1)S(1)} %pad_maximum_fusion.4.rest_2_), channel_id=1, source_target_pairs={{0,1},{1,0},{2,3},{3,2},{4,5},{5,4},{6,7},{7,6},{8,9},{9,8},{10,11... | collective-permute-start | bytes 2359304 | tf_op jit(solution)/shard_map/ppermute | solution.py:52
  65.3 18.0 %collective-permute-start.5 = (bf16[2,2,256,384]{3,2,1,0:T(8,128)(2,1)}, bf16[2,2,256,384]{3,2,1,0:T(8,128)(2,1)}, u32[]{:S(2)}, u32[]{:S(2)}) collective-permute-start(bf16[2,2,256,384]{3,2,1,0:T(8,128)(2,1)} %pad_maximum_fusion.3.rest_0_), channel_id=1, source_target_pairs={{0,16},{16,0},{1,17},{17,1},{2,18},{18,2},{3,19},{19,3},{4,20},{20... | collective-permute-start | bytes 2359304 | tf_op jit(solution)/shard_map/ppermute | solution.py:52
  66.0 17.8 %collective-permute-start.10 = (bf16[2,2,256,384]{3,2,1,0:T(8,128)(2,1)S(1)}, bf16[2,2,256,384]{3,2,1,0:T(8,128)(2,1)}, u32[]{:S(2)}, u32[]{:S(2)}) collective-permute-start(bf16[2,2,256,384]{3,2,1,0:T(8,128)(2,1)S(1)} %pad_maximum_fusion.4.rest_2_), channel_id=1, source_target_pairs={{0,8},{8,0},{1,9},{9,1},{2,10},{10,2},{3,11},{11,3},{4,12},{12,4},... | collective-permute-start | bytes 2359304 | tf_op jit(solution)/shard_map/ppermute | solution.py:52
  66.1 17.8 %collective-permute-start.8 = (bf16[2,2,256,384]{3,2,1,0:T(8,128)(2,1)}, bf16[2,2,256,384]{3,2,1,0:T(8,128)(2,1)}, u32[]{:S(2)}, u32[]{:S(2)}) collective-permute-start(bf16[2,2,256,384]{3,2,1,0:T(8,128)(2,1)} %pad_maximum_fusion.3.rest_0_), channel_id=1, source_target_pairs={{0,8},{8,0},{1,9},{9,1},{2,10},{10,2},{3,11},{11,3},{4,12},{12,4},... | collective-permute-start | bytes 2359304 | tf_op jit(solution)/shard_map/ppermute | solution.py:52
  83.8 39.7 %collective-permute-start.14 = (bf16[256,512]{1,0:T(8,128)(2,1)S(1)}, bf16[256,512]{1,0:T(8,128)(2,1)S(1)}, u32[]{:S(2)}, u32[]{:S(2)}) collective-permute-start(bf16[256,512]{1,0:T(8,128)(2,1)S(1)} %copy-done.18), channel_id=1, source_target_pairs={{0,6},{2,4},{4,2},{6,0},{1,7},{3,5},{5,3},{7,1},{8,14},{10,12},{12... | collective-permute-start | bytes 786440 | tf_op jit(solution)/shard_map/ppermute | solution.py:52
  83.8 45.5 %collective-permute-start.13 = (bf16[256,512]{1,0:T(8,128)(2,1)S(1)}, bf16[256,512]{1,0:T(8,128)(2,1)S(1)}, u32[]{:S(2)}, u32[]{:S(2)}) collective-permute-start(bf16[256,512]{1,0:T(8,128)(2,1)S(1)} %copy-done.18), channel_id=1, source_target_pairs={{0,4},{2,6},{4,0},{6,2},{1,5},{3,7},{5,1},{7,3},{8,12},{10,14},{12... | collective-permute-start | bytes 786440 | tf_op jit(solution)/shard_map/ppermute | solution.py:52
  83.9 45.4 %collective-permute-start.12 = (bf16[256,512]{1,0:T(8,128)(2,1)S(1)}, bf16[256,512]{1,0:T(8,128)(2,1)}, u32[]{:S(2)}, u32[]{:S(2)}) collective-permute-start(bf16[256,512]{1,0:T(8,128)(2,1)S(1)} %copy-done.18), channel_id=1, source_target_pairs={{0,2},{2,0},{4,6},{6,4},{1,3},{3,1},{5,7},{7,5},{8,10},{10,8},{12,... | collective-permute-start | bytes 786440 | tf_op jit(solution)/shard_map/ppermute | solution.py:52
  149.3 24.4 %collective-permute-start.20 = (bf16[2,2,256,512]{3,2,1,0:T(8,128)(2,1)S(1)}, bf16[2,2,256,512]{3,2,1,0:T(8,128)(2,1)S(1)}, u32[]{:S(2)}, u32[]{:S(2)}) collective-permute-start(bf16[2,2,256,512]{3,2,1,0:T(8,128)(2,1)S(1)} %pad_maximum_fusion.2.rest_2_), channel_id=1, source_target_pairs={{0,8},{8,0},{1,9},{9,1},{2,10},{10,2},{3,11},{11,3},{4,12},{12,4},... | collective-permute-start | bytes 3145736 | tf_op jit(solution)/shard_map/ppermute | solution.py:52
  149.4 25.7 %collective-permute-start.18 = (bf16[2,2,256,512]{3,2,1,0:T(8,128)(2,1)S(1)}, bf16[2,2,256,512]{3,2,1,0:T(8,128)(2,1)}, u32[]{:S(2)}, u32[]{:S(2)}) collective-permute-start(bf16[2,2,256,512]{3,2,1,0:T(8,128)(2,1)S(1)} %pad_maximum_fusion.2.rest_2_), channel_id=1, source_target_pairs={{0,1},{1,0},{2,3},{3,2},{4,5},{5,4},{6,7},{7,6},{8,9},{9,8},{10,11... | collective-permute-start | bytes 3145736 | tf_op jit(solution)/shard_map/ppermute | solution.py:52
  152.1 23.0 %collective-permute-start.19 = (bf16[2,2,256,512]{3,2,1,0:T(8,128)(2,1)S(1)}, bf16[2,2,256,512]{3,2,1,0:T(8,128)(2,1)}, u32[]{:S(2)}, u32[]{:S(2)}) collective-permute-start(bf16[2,2,256,512]{3,2,1,0:T(8,128)(2,1)S(1)} %pad_maximum_fusion.1.rest_0_), channel_id=1, source_target_pairs={{0,8},{8,0},{1,9},{9,1},{2,10},{10,2},{3,11},{11,3},{4,12},{12,4},... | collective-permute-start | bytes 3145736 | tf_op jit(solution)/shard_map/ppermute | solution.py:52
  152.3 25.5 %collective-permute-start.17 = (bf16[2,2,256,512]{3,2,1,0:T(8,128)(2,1)S(1)}, bf16[2,2,256,512]{3,2,1,0:T(8,128)(2,1)}, u32[]{:S(2)}, u32[]{:S(2)}) collective-permute-start(bf16[2,2,256,512]{3,2,1,0:T(8,128)(2,1)S(1)} %pad_maximum_fusion.1.rest_0_), channel_id=1, source_target_pairs={{0,16},{16,0},{1,17},{17,1},{2,18},{18,2},{3,19},{19,3},{4,20},{20... | collective-permute-start | bytes 3145736 | tf_op jit(solution)/shard_map/ppermute | solution.py:52
  202.4 28.7 %collective-permute-start.24 = (bf16[2,2,256,512]{3,2,1,0:T(8,128)(2,1)}, bf16[2,2,256,512]{3,2,1,0:T(8,128)(2,1)}, u32[]{:S(2)}, u32[]{:S(2)}) collective-permute-start(bf16[2,2,256,512]{3,2,1,0:T(8,128)(2,1)} %get-tuple-element.329), channel_id=1, source_target_pairs={{0,16},{16,0},{1,17},{17,1},{2,18},{18,2},{3,19},{19,3},{4,20},{20... | collective-permute-start | bytes 3145736 | tf_op jit(solution)/shard_map/ppermute | solution.py:52
  203.0 28.2 %collective-permute-start.25 = (bf16[2,2,256,512]{3,2,1,0:T(8,128)(2,1)}, bf16[2,2,256,512]{3,2,1,0:T(8,128)(2,1)}, u32[]{:S(2)}, u32[]{:S(2)}) collective-permute-start(bf16[2,2,256,512]{3,2,1,0:T(8,128)(2,1)} %get-tuple-element.331), channel_id=1, source_target_pairs={{0,1},{1,0},{2,3},{3,2},{4,5},{5,4},{6,7},{7,6},{8,9},{9,8},{10,11... | collective-permute-start | bytes 3145736 | tf_op jit(solution)/shard_map/ppermute | solution.py:52
  264.9 30.9 %collective-permute-start.29 = (bf16[2,2,256,640]{3,2,1,0:T(8,128)(2,1)}, bf16[2,2,256,640]{3,2,1,0:T(8,128)(2,1)}, u32[]{:S(2)}, u32[]{:S(2)}) collective-permute-start(bf16[2,2,256,640]{3,2,1,0:T(8,128)(2,1)} %get-tuple-element.381), channel_id=1, source_target_pairs={{0,16},{16,0},{1,17},{17,1},{2,18},{18,2},{3,19},{19,3},{4,20},{20... | collective-permute-start | bytes 3932168 | tf_op jit(solution)/shard_map/ppermute | solution.py:52
  266.0 30.1 %collective-permute-start.30 = (bf16[2,2,256,640]{3,2,1,0:T(8,128)(2,1)}, bf16[2,2,256,640]{3,2,1,0:T(8,128)(2,1)}, u32[]{:S(2)}, u32[]{:S(2)}) collective-permute-start(bf16[2,2,256,640]{3,2,1,0:T(8,128)(2,1)} %get-tuple-element.383), channel_id=1, source_target_pairs={{0,1},{1,0},{2,3},{3,2},{4,5},{5,4},{6,7},{7,6},{8,9},{9,8},{10,11... | collective-permute-start | bytes 3932168 | tf_op jit(solution)/shard_map/ppermute | solution.py:52
  266.5 25.9 %collective-permute-start.31 = (bf16[256,512]{1,0:T(8,128)(2,1)}, bf16[256,512]{1,0:T(8,128)(2,1)S(1)}, u32[]{:S(2)}, u32[]{:S(2)}) collective-permute-start(bf16[256,512]{1,0:T(8,128)(2,1)} %get-tuple-element.385), channel_id=1, source_target_pairs={{0,2},{2,0},{4,6},{6,4},{1,3},{3,1},{5,7},{7,5},{8,10},{10,8},{12,... | collective-permute-start | bytes 786440 | tf_op jit(solution)/shard_map/ppermute | solution.py:52
  266.5 25.9 %collective-permute-start.32 = (bf16[256,512]{1,0:T(8,128)(2,1)}, bf16[256,512]{1,0:T(8,128)(2,1)}, u32[]{:S(2)}, u32[]{:S(2)}) collective-permute-start(bf16[256,512]{1,0:T(8,128)(2,1)} %get-tuple-element.386), channel_id=1, source_target_pairs={{0,4},{2,6},{4,0},{6,2},{1,5},{3,7},{5,1},{7,3},{8,12},{10,14},{12... | collective-permute-start | bytes 786440 | tf_op jit(solution)/shard_map/ppermute | solution.py:52
  268.6 23.9 %collective-permute-start.33 = (bf16[256,512]{1,0:T(8,128)(2,1)}, bf16[256,512]{1,0:T(8,128)(2,1)}, u32[]{:S(2)}, u32[]{:S(2)}) collective-permute-start(bf16[256,512]{1,0:T(8,128)(2,1)} %get-tuple-element.387), channel_id=1, source_target_pairs={{0,6},{2,4},{4,2},{6,0},{1,7},{3,5},{5,3},{7,1},{8,14},{10,12},{12... | collective-permute-start | bytes 786440 | tf_op jit(solution)/shard_map/ppermute | solution.py:52
  300.5 17.4 %collective-permute-start.35 = (bf16[2,256,640]{2,1,0:T(8,128)(2,1)}, bf16[2,256,640]{2,1,0:T(8,128)(2,1)S(1)}, u32[]{:S(2)}, u32[]{:S(2)}) collective-permute-start(bf16[2,256,640]{2,1,0:T(8,128)(2,1)} %get-tuple-element.414), channel_id=1, source_target_pairs={{0,1},{1,0},{2,3},{3,2},{4,5},{5,4},{6,7},{7,6},{8,9},{9,8},{10,11... | collective-permute-start | bytes 1966088 | tf_op jit(solution)/shard_map/ppermute | solution.py:52
  301.2 17.1 %collective-permute-start.36 = (bf16[2,256,640]{2,1,0:T(8,128)(2,1)}, bf16[2,256,640]{2,1,0:T(8,128)(2,1)}, u32[]{:S(2)}, u32[]{:S(2)}) collective-permute-start(bf16[2,256,640]{2,1,0:T(8,128)(2,1)} %get-tuple-element.416), channel_id=1, source_target_pairs={{0,16},{16,0},{1,17},{17,1},{2,18},{18,2},{3,19},{19,3},{4,20},{20... | collective-permute-start | bytes 1966088 | tf_op jit(solution)/shard_map/ppermute | solution.py:52
  318.7 22.5 %collective-permute-start.37 = (bf16[2,2,256,384]{3,2,1,0:T(8,128)(2,1)}, bf16[2,2,256,384]{3,2,1,0:T(8,128)(2,1)S(1)}, u32[]{:S(2)}, u32[]{:S(2)}) collective-permute-start(bf16[2,2,256,384]{3,2,1,0:T(8,128)(2,1)} %get-tuple-element.421), channel_id=1, source_target_pairs={{0,16},{16,0},{1,17},{17,1},{2,18},{18,2},{3,19},{19,3},{4,20},{20... | collective-permute-start | bytes 2359304 | tf_op jit(solution)/shard_map/ppermute | solution.py:52
  320.2 21.1 %collective-permute-start.38 = (bf16[2,2,256,384]{3,2,1,0:T(8,128)(2,1)}, bf16[2,2,256,384]{3,2,1,0:T(8,128)(2,1)}, u32[]{:S(2)}, u32[]{:S(2)}) collective-permute-start(bf16[2,2,256,384]{3,2,1,0:T(8,128)(2,1)} %get-tuple-element.423), channel_id=1, source_target_pairs={{0,1},{1,0},{2,3},{3,2},{4,5},{5,4},{6,7},{7,6},{8,9},{9,8},{10,11... | collective-permute-start | bytes 2359304 | tf_op jit(solution)/shard_map/ppermute | solution.py:52
  324.7 16.6 %collective-permute-start.40 = (bf16[256,640]{1,0:T(8,128)(2,1)}, bf16[256,640]{1,0:T(8,128)(2,1)S(1)}, u32[]{:S(2)}, u32[]{:S(2)}) collective-permute-start(bf16[256,640]{1,0:T(8,128)(2,1)} %get-tuple-element.437), channel_id=1, source_target_pairs={{0,4},{2,6},{4,0},{6,2},{1,5},{3,7},{5,1},{7,3},{8,12},{10,14},{12... | collective-permute-start | bytes 983048 | tf_op jit(solution)/shard_map/ppermute | solution.py:52
  362.8 27.8 %collective-permute-start.49 = (bf16[512,1024]{1,0:T(8,128)(2,1)}, bf16[512,1024]{1,0:T(8,128)(2,1)}, u32[]{:S(2)}, u32[]{:S(2)}) collective-permute-start(bf16[512,1024]{1,0:T(8,128)(2,1)} %get-tuple-element.487), channel_id=1, source_target_pairs={{1,0},{3,2},{5,4},{7,6},{9,8},{11,10},{13,12},{15,14},{17,16},{19,... | collective-permute-start | bytes 3145736 | tf_op jit(solution)/shard_map/ppermute | solution.py:1030
  364.1 19.6 %collective-permute-start.45 = (bf16[256,384]{1,0:T(8,128)(2,1)}, bf16[256,384]{1,0:T(8,128)(2,1)S(1)}, u32[]{:S(2)}, u32[]{:S(2)}) collective-permute-start(bf16[256,384]{1,0:T(8,128)(2,1)} %get-tuple-element.482), channel_id=1, source_target_pairs={{0,2},{2,0},{4,6},{6,4},{1,3},{3,1},{5,7},{7,5},{8,10},{10,8},{12,... | collective-permute-start | bytes 589832 | tf_op jit(solution)/shard_map/ppermute | solution.py:52
  364.2 19.5 %collective-permute-start.46 = (bf16[256,384]{1,0:T(8,128)(2,1)}, bf16[256,384]{1,0:T(8,128)(2,1)S(1)}, u32[]{:S(2)}, u32[]{:S(2)}) collective-permute-start(bf16[256,384]{1,0:T(8,128)(2,1)} %get-tuple-element.483), channel_id=1, source_target_pairs={{0,4},{2,6},{4,0},{6,2},{1,5},{3,7},{5,1},{7,3},{8,12},{10,14},{12... | collective-permute-start | bytes 589832 | tf_op jit(solution)/shard_map/ppermute | solution.py:52
  367.1 16.6 %collective-permute-start.47 = (bf16[256,384]{1,0:T(8,128)(2,1)}, bf16[256,384]{1,0:T(8,128)(2,1)S(1)}, u32[]{:S(2)}, u32[]{:S(2)}) collective-permute-start(bf16[256,384]{1,0:T(8,128)(2,1)} %get-tuple-element.484), channel_id=1, source_target_pairs={{0,6},{2,4},{4,2},{6,0},{1,7},{3,5},{5,3},{7,1},{8,14},{10,12},{12... | collective-permute-start | bytes 589832 | tf_op jit(solution)/shard_map/ppermute | solution.py:52
  (54 other events, 660.5 us)
Sparse Core Ops, SparseCore 0:
  11.5 121.1 all-gather.2
